TPU v7x, 32 devices: a whole 2x2x4 slice. The times are simulated.
32 devices in a mesh: expert: 8 (over z, y), tensor: 4 (over x, core).
Axes of the slice: x: 2, y: 2, z: 4, core: 2. Of those that a mesh axis runs over, the one named last changes fastest.
Arguments:
- tokens: bfloat16 [4096, 2048], P('expert'), may hold values from -6 to 6
- lengths: int32 [8], P('expert'), may hold values from 256 to 512, as said below
- routes: int32 [4096, 6], P('expert'), may hold values from 0 to 15, all different within a row; in each aligned block of 512 rows (0 to 511, 512 to 1023, ...) at most 288 rows name the same one
- gain_attn: float32 [2048], replicated, may hold values from 0.1 to 1.9
- w_query: bfloat16 [2048, 3072], P('expert', 'tensor'), may hold values from -0.125 to 0.125
- w_latent: bfloat16 [2048, 576], replicated, may hold values from -0.125 to 0.125
- gain_latent: float32 [512], replicated, may hold values from 0.1 to 1.9
- w_kv: bfloat16 [512, 4096], P('expert', 'tensor'), may hold values from -0.25 to 0.25
- w_out: bfloat16 [2048, 2048], P('tensor', 'expert'), may hold values from -0.5 to 0.5
- gain_ffn: float32 [2048], replicated, may hold values from 0.1 to 1.9
- w_router: bfloat16 [2048, 16], replicated, may hold values from -0.0625 to 0.0625
- w_shared_gate: bfloat16 [2048, 2816], P('expert', 'tensor'), may hold values from -0.125 to 0.125
- w_shared_up: bfloat16 [2048, 2816], P('expert', 'tensor'), may hold values from -0.125 to 0.125
- w_shared_down: bfloat16 [2816, 2048], P('tensor', 'expert'), may hold values from -0.109375 to 0.109375
- w_gate: bfloat16 [16, 2048, 1408], P('expert', None, 'tensor'), may hold values from -0.125 to 0.125
- w_up: bfloat16 [16, 2048, 1408], P('expert', None, 'tensor'), may hold values from -0.125 to 0.125
- w_down: bfloat16 [16, 1408, 2048], P('expert', 'tensor'), may hold values from -6 to 6
- cotangent: bfloat16 [4096, 2048], P('expert'), may hold values from -6 to 6
Outputs:
- output: bfloat16 [4096, 2048], P('expert')
- grad_tokens: bfloat16 [4096, 2048], P('expert')
- grad_gain_attn: float32 [2048], replicated
- grad_query: float32 [2048, 3072], P('expert', 'tensor')
- grad_latent: float32 [2048, 576], replicated
- grad_gain_latent: float32 [512], replicated
- grad_kv: float32 [512, 4096], P('expert', 'tensor')
- grad_out: float32 [2048, 2048], P('tensor', 'expert')
- grad_gain_ffn: float32 [2048], replicated
- grad_router: float32 [2048, 16], replicated
- grad_shared_gate: float32 [2048, 2816], P('expert', 'tensor')
- grad_shared_up: float32 [2048, 2816], P('expert', 'tensor')
- grad_shared_down: float32 [2816, 2048], P('tensor', 'expert')
- grad_gate: float32 [16, 2048, 1408], P('expert', None, 'tensor')
- grad_up: float32 [16, 2048, 1408], P('expert', None, 'tensor')
- grad_down: float32 [16, 1408, 2048], P('expert', 'tensor')
Inputs may be any that keep to these rules, and one draw needn't show every extreme that they name: Group g of the expert axis holds one causal sequence in its first lengths[g] rows; the rest of its 512 rows is padding; some group's sequence fills all 512 rows. `routes`: each row names 6 different experts; within the rows of one group no expert is named more than 288 times, a bound that some block reaches.
All inputs are finite; a program needn't handle non-finite values.
Results may differ from a plain program's by a relative error of at most 0.028.
Values may be sent and summed in bfloat16 or wider, within the bound.
A program may use at most 384 MiB of HBM per device.

v0:
```python
import jax
import jax.numpy as jnp
from jax import lax
from jax.sharding import PartitionSpec as P

NOPE = 128
ROPE = 64
VD = 128
KVR = 512


EPS = 1e-06
ROPE_BASE = 10000.0
HIGH = lax.Precision.HIGHEST


def inv_rms(v):
    return lax.rsqrt(jnp.mean(v * v, axis=-1, keepdims=True) + EPS)


def rope_tables(count, width):
    half = width // 2
    freq = ROPE_BASE ** (-(jnp.arange(half, dtype=jnp.float32) * 2.0 / width))
    angle = jnp.arange(count, dtype=jnp.float32)[:, None] * freq[None, :]
    return (jnp.cos(angle), jnp.sin(angle))


def rotate(v, cosine, sine):
    half = v.shape[-1] // 2
    first = v[..., :half]
    second = v[..., half:]
    return jnp.concatenate(
        [first * cosine - second * sine, second * cosine + first * sine], axis=-1
    )


def rotate_back(grad, cosine, sine):
    half = grad.shape[-1] // 2
    first = grad[..., :half]
    second = grad[..., half:]
    return jnp.concatenate(
        [first * cosine + second * sine, second * cosine - first * sine], axis=-1
    )


def norm_back(grad, normed, scale_row, gain):
    weighted = grad * gain
    return scale_row * (weighted - normed * jnp.mean(weighted * normed, axis=-1, keepdims=True))


def silu_parts(gate):
    sig = jax.nn.sigmoid(gate)
    return (gate * sig, sig * (1.0 + gate * (1.0 - sig)))


def mat(left, right):
    return jnp.dot(left, right, preferred_element_type=jnp.float32)


def mat_tn(left, right):
    return lax.dot_general(
        left, right, (((0,), (0,)), ((), ())), preferred_element_type=jnp.float32
    )


def mat_nt(left, right):
    return lax.dot_general(
        left, right, (((1,), (1,)), ((), ())), preferred_element_type=jnp.float32
    )


def exact_tn(left, right):
    return lax.dot_general(
        left, right, (((0,), (0,)), ((), ())), precision=HIGH, preferred_element_type=jnp.float32
    )


def exact_nt(left, right):
    return lax.dot_general(
        left, right, (((1,), (1,)), ((), ())), precision=HIGH, preferred_element_type=jnp.float32
    )


def shards(
    tokens,
    lengths,
    routes,
    gain_attn,
    w_query,
    w_latent,
    gain_latent,
    w_kv,
    w_out,
    gain_ffn,
    w_router,
    w_shared_gate,
    w_shared_up,
    w_shared_down,
    w_gate,
    w_up,
    w_down,
    cotangent,
):
    groups = lax.axis_size("expert")
    tensors = lax.axis_size("tensor")
    tindex = lax.axis_index("tensor")
    rows, width = tokens.shape
    quarter = rows // tensors
    experts_local = w_gate.shape[0]
    total_experts = experts_local * groups
    top = routes.shape[1]
    cap = 3 * rows * top // (2 * total_experts * tensors) * tensors
    slice_cap = cap // tensors
    entries = rows * top
    capacity_all = total_experts * cap
    query_w, kv_up, out_proj, shared_gate, shared_up, shared_down = (
        lax.all_gather(w_query, "expert", axis=0, tiled=True),
        lax.all_gather(w_kv, "expert", axis=0, tiled=True),
        lax.all_gather(w_out, "expert", axis=1, tiled=True),
        lax.all_gather(w_shared_gate, "expert", axis=0, tiled=True),
        lax.all_gather(w_shared_up, "expert", axis=0, tiled=True),
        lax.all_gather(w_shared_down, "expert", axis=1, tiled=True),
    )
    heads = out_proj.shape[0] // VD
    xf = tokens.astype(jnp.float32)
    scale_one = inv_rms(xf)
    normed_one = xf * scale_one
    xn1 = (normed_one * gain_attn).astype(jnp.bfloat16)
    cosine, sine = rope_tables(rows, ROPE)
    qfull = mat(xn1, query_w).reshape(rows, heads, NOPE + ROPE)
    qcat = jnp.concatenate(
        [qfull[..., :NOPE], rotate(qfull[..., NOPE:], cosine[:, None, :], sine[:, None, :])],
        axis=-1,
    ).astype(jnp.bfloat16)
    latent = mat(xn1, w_latent)
    comp = latent[:, :KVR]
    scale_lat = inv_rms(comp)
    normed_lat = comp * scale_lat
    compressed = (normed_lat * gain_latent).astype(jnp.bfloat16)
    key_rope = rotate(latent[:, KVR:], cosine, sine).astype(jnp.bfloat16)
    key_value = mat(compressed, kv_up).astype(jnp.bfloat16).reshape(rows, heads, NOPE + VD)
    keys = jnp.concatenate(
        [key_value[..., :NOPE], jnp.broadcast_to(key_rope[:, None, :], (rows, heads, ROPE))],
        axis=-1,
    )
    values = key_value[..., NOPE:]
    causal = jnp.arange(rows)[:, None] >= jnp.arange(rows)[None, :]
    score_scale = (NOPE + ROPE) ** (-0.5)

    def scores():
        raw = (
            jnp.einsum("qhd,khd->hqk", qcat, keys, preferred_element_type=jnp.float32) * score_scale
        )
        return jnp.where(causal[None], raw, -jnp.inf)

    score_now = scores()
    peak = jnp.max(score_now, axis=-1, keepdims=True)
    expo = jnp.exp(score_now - peak)
    total = jnp.sum(expo, axis=-1, keepdims=True)
    log_total = peak + jnp.log(total)
    probs = (expo / total).astype(jnp.bfloat16)
    attended = (
        jnp.einsum("hqk,khd->qhd", probs, values, preferred_element_type=jnp.float32)
        .astype(jnp.bfloat16)
        .reshape(rows, heads * VD)
    )
    attn = lax.psum(mat(attended, out_proj).astype(jnp.bfloat16), "tensor").astype(jnp.float32)
    live_int = (jnp.arange(rows) < lengths[0]).astype(jnp.int32)
    live = live_int.astype(jnp.float32)[:, None]
    resid = xf + live * attn
    scale_two = inv_rms(resid)
    normed_two = resid * scale_two
    xn2 = (normed_two * gain_ffn).astype(jnp.bfloat16)
    router = jax.nn.softmax(mat(xn2, w_router), axis=-1)
    choose = (routes[..., None] == jnp.arange(total_experts)[None, None, :]).astype(jnp.float32)
    gates = jnp.sum(choose * router[:, None, :], axis=-1) * live
    marks = (
        (routes[..., None] == jnp.arange(total_experts)[None, None, :]).astype(jnp.int32)
        * live_int[:, None, None]
    ).reshape(entries, total_experts)
    rank = jnp.sum((jnp.cumsum(marks, axis=0) - marks) * marks, axis=-1)
    flat_ids = routes.reshape(entries)
    valid = jnp.repeat(live_int, top) > 0
    slot = jnp.where(valid, flat_ids * cap + rank, capacity_all)
    owner = (
        jnp.full((capacity_all + 1,), entries, jnp.int32)
        .at[slot]
        .set(jnp.arange(entries, dtype=jnp.int32))[:capacity_all]
    )
    source_row = jnp.where(owner < entries, owner // top, rows)
    lower = tindex * slice_cap
    mine = valid & (rank >= lower) & (rank < lower + slice_cap)
    local_slot = jnp.where(mine, flat_ids * slice_cap + rank - lower, total_experts * slice_cap)
    padded = jnp.concatenate([xn2, jnp.zeros((1, width), jnp.bfloat16)], axis=0)
    outgoing = padded[source_row].reshape(groups, experts_local, cap, width)
    arrived = lax.all_to_all(outgoing, "expert", split_axis=0, concat_axis=0, tiled=True)
    hgate = jnp.einsum("sjcd,jdf->sjcf", arrived, w_gate, preferred_element_type=jnp.float32)
    hup = jnp.einsum("sjcd,jdf->sjcf", arrived, w_up, preferred_element_type=jnp.float32)
    act, dact = silu_parts(hgate)
    hidden = (act * hup).astype(jnp.bfloat16)
    partial_value = jnp.einsum(
        "sjcf,jfd->sjcd", hidden, w_down, preferred_element_type=jnp.float32
    ).astype(jnp.bfloat16)
    returned = lax.all_to_all(
        partial_value, "expert", split_axis=0, concat_axis=0, tiled=True
    ).reshape(capacity_all, width)
    picked = jnp.concatenate([returned, jnp.zeros((1, width), jnp.bfloat16)], axis=0)[slot].reshape(
        rows, top, width
    )
    picked_full = picked.astype(jnp.float32)
    routed = jnp.sum(picked_full * gates[..., None], axis=1)
    sgate = mat(xn2, shared_gate)
    sup = mat(xn2, shared_up)
    sact, sdact = silu_parts(sgate)
    shid = (sact * sup).astype(jnp.bfloat16)
    ffn = lax.psum((routed + mat(shid, shared_down)).astype(jnp.bfloat16), "tensor").astype(
        jnp.float32
    )
    output = (resid + live * ffn).astype(jnp.bfloat16)
    dout = cotangent.astype(jnp.float32)
    dffn = (dout * live).astype(jnp.bfloat16)
    dshid = mat_nt(dffn, shared_down)
    grad_sdown = mat_tn(shid, dffn)
    dsgate = (dshid * sup * sdact).astype(jnp.bfloat16)
    dsup = (dshid * sact).astype(jnp.bfloat16)
    grad_sgate = mat_tn(xn2, dsgate)
    grad_sup = mat_tn(xn2, dsup)
    dnorm_two = mat_nt(dsgate, shared_gate) + mat_nt(dsup, shared_up)
    dgates = jnp.einsum(
        "rd,rkd->rk",
        dffn.astype(jnp.float32),
        picked_full,
        precision=HIGH,
        preferred_element_type=jnp.float32,
    )
    drouter = jnp.sum(choose * dgates[..., None], axis=1)
    dlogit = router * (drouter - jnp.sum(router * drouter, axis=-1, keepdims=True))
    grad_router = exact_tn(xn2.astype(jnp.float32), dlogit)
    dnorm_two = dnorm_two + exact_nt(dlogit, w_router.astype(jnp.float32))
    dweighted = (
        (dffn.astype(jnp.float32)[:, None, :] * gates[..., None])
        .reshape(entries, width)
        .astype(jnp.bfloat16)
    )
    dslots = jnp.concatenate([dweighted, jnp.zeros((1, width), jnp.bfloat16)], axis=0)[
        owner
    ].reshape(groups, experts_local, cap, width)
    dreturn = lax.all_to_all(dslots, "expert", split_axis=0, concat_axis=0, tiled=True)
    dhidden = jnp.einsum("sjcd,jfd->sjcf", dreturn, w_down, preferred_element_type=jnp.float32)
    grad_down = jnp.einsum("sjcf,sjcd->jfd", hidden, dreturn, preferred_element_type=jnp.float32)
    dgate_h = (dhidden * hup * dact).astype(jnp.bfloat16)
    dup_h = (dhidden * act).astype(jnp.bfloat16)
    grad_gate = jnp.einsum("sjcd,sjcf->jdf", arrived, dgate_h, preferred_element_type=jnp.float32)
    grad_up = jnp.einsum("sjcd,sjcf->jdf", arrived, dup_h, preferred_element_type=jnp.float32)
    drows = jnp.einsum("sjcf,jdf->sjcd", dgate_h, w_gate, preferred_element_type=jnp.float32)
    drows = drows + jnp.einsum("sjcf,jdf->sjcd", dup_h, w_up, preferred_element_type=jnp.float32)
    dsummed = lax.psum_scatter(
        drows.astype(jnp.bfloat16), "tensor", scatter_dimension=2, tiled=True
    )
    dback = lax.all_to_all(dsummed, "expert", split_axis=0, concat_axis=0, tiled=True).reshape(
        total_experts * slice_cap, width
    )
    dpicked = jnp.concatenate([dback, jnp.zeros((1, width), jnp.bfloat16)], axis=0)[
        local_slot
    ].reshape(rows, top, width)
    dnorm_two = dnorm_two + jnp.sum(dpicked.astype(jnp.float32), axis=1)
    dnorm_two = lax.psum(dnorm_two.astype(jnp.bfloat16), "tensor").astype(jnp.float32)
    grad_gain_ffn = jnp.sum(
        lax.dynamic_slice_in_dim(dnorm_two * normed_two, tindex * quarter, quarter, 0), axis=0
    )
    dresid = dout + norm_back(dnorm_two, normed_two, scale_two, gain_ffn)
    dattn = (dresid * live).astype(jnp.bfloat16)
    grad_out = mat_tn(attended, dattn)
    dattended = mat_nt(dattn, out_proj).astype(jnp.bfloat16).reshape(rows, heads, VD)
    pfull = jnp.exp(scores() - log_total)
    dvalues = jnp.einsum("hqk,qhd->khd", probs, dattended, preferred_element_type=jnp.float32)
    dprobs = jnp.einsum("qhd,khd->hqk", dattended, values, preferred_element_type=jnp.float32)
    dscore = (
        pfull * (dprobs - jnp.sum(pfull * dprobs, axis=-1, keepdims=True)) * score_scale
    ).astype(jnp.bfloat16)
    dquery = jnp.einsum("hqk,khd->qhd", dscore, keys, preferred_element_type=jnp.float32)
    dkeys = jnp.einsum("hqk,qhd->khd", dscore, qcat, preferred_element_type=jnp.float32)
    dkv = (
        jnp.concatenate([dkeys[..., :NOPE], dvalues], axis=-1)
        .astype(jnp.bfloat16)
        .reshape(rows, heads * (NOPE + VD))
    )
    grad_kv = mat_tn(compressed, dkv)
    dcomp = mat_nt(dkv, kv_up)
    grad_gain_latent = jnp.sum(dcomp * normed_lat, axis=0)
    dlatent = jnp.concatenate(
        [
            norm_back(dcomp, normed_lat, scale_lat, gain_latent),
            rotate_back(jnp.sum(dkeys[..., NOPE:], axis=1), cosine, sine),
        ],
        axis=-1,
    )
    dqfull = jnp.concatenate(
        [dquery[..., :NOPE], rotate_back(dquery[..., NOPE:], cosine[:, None, :], sine[:, None, :])],
        axis=-1,
    )
    dqfull = dqfull.astype(jnp.bfloat16).reshape(rows, heads * (NOPE + ROPE))
    grad_query = mat_tn(xn1, dqfull)
    grad_latent = exact_tn(xn1.astype(jnp.float32), dlatent)
    dnorm_one = mat_nt(dqfull, query_w) + exact_nt(dlatent, w_latent.astype(jnp.float32))
    dnorm_one = lax.psum(dnorm_one.astype(jnp.bfloat16), "tensor").astype(jnp.float32)
    grad_gain_attn = jnp.sum(
        lax.dynamic_slice_in_dim(dnorm_one * normed_one, tindex * quarter, quarter, 0), axis=0
    )
    grad_tokens = (dresid + norm_back(dnorm_one, normed_one, scale_one, gain_attn)).astype(
        jnp.bfloat16
    )
    grad_latent, grad_gain_attn, grad_gain_latent, grad_gain_ffn, grad_router = lax.psum(
        (grad_latent, grad_gain_attn, grad_gain_latent, grad_gain_ffn, grad_router),
        ("expert", "tensor"),
    )
    grad_query, grad_kv, grad_out, grad_sgate, grad_sup, grad_sdown = (
        lax.psum_scatter(
            grad_query.astype(jnp.bfloat16), "expert", scatter_dimension=0, tiled=True
        ).astype(jnp.float32),
        lax.psum_scatter(
            grad_kv.astype(jnp.bfloat16), "expert", scatter_dimension=0, tiled=True
        ).astype(jnp.float32),
        lax.psum_scatter(
            grad_out.astype(jnp.bfloat16), "expert", scatter_dimension=1, tiled=True
        ).astype(jnp.float32),
        lax.psum_scatter(
            grad_sgate.astype(jnp.bfloat16), "expert", scatter_dimension=0, tiled=True
        ).astype(jnp.float32),
        lax.psum_scatter(
            grad_sup.astype(jnp.bfloat16), "expert", scatter_dimension=0, tiled=True
        ).astype(jnp.float32),
        lax.psum_scatter(
            grad_sdown.astype(jnp.bfloat16), "expert", scatter_dimension=1, tiled=True
        ).astype(jnp.float32),
    )
    return (
        output,
        grad_tokens,
        grad_gain_attn,
        grad_query,
        grad_latent,
        grad_gain_latent,
        grad_kv,
        grad_out,
        grad_gain_ffn,
        grad_router,
        grad_sgate,
        grad_sup,
        grad_sdown,
        grad_gate,
        grad_up,
        grad_down,
    )


def solution(mesh):
    in_specs = (
        P("expert", None),
        P("expert"),
        P("expert", None),
        P(),
        P("expert", "tensor"),
        P(),
        P(),
        P("expert", "tensor"),
        P("tensor", "expert"),
        P(),
        P(),
        P("expert", "tensor"),
        P("expert", "tensor"),
        P("tensor", "expert"),
        P("expert", None, "tensor"),
        P("expert", None, "tensor"),
        P("expert", "tensor", None),
        P("expert", None),
    )
    out_specs = (
        P("expert", None),
        P("expert", None),
        P(),
        P("expert", "tensor"),
        P(),
        P(),
        P("expert", "tensor"),
        P("tensor", "expert"),
        P(),
        P(),
        P("expert", "tensor"),
        P("expert", "tensor"),
        P("tensor", "expert"),
        P("expert", None, "tensor"),
        P("expert", None, "tensor"),
        P("expert", "tensor", None),
    )
    return jax.shard_map(shards, mesh=mesh, in_specs=in_specs, out_specs=out_specs, check_vma=False)
```

profile of v0, /device:TPU:0, one launch (start us, length us, event | category | flops | bytes accessed | tf_op | source)
XLA Modules:
  0.0 3204.9 jit_solution(2762995197374463652)
XLA Ops:
  16.7 9.5 reduce-window.6
  45.9 7.2 all-gather.7.cloned.1.call-done
  59.8 54.7 %all-gather.9.cloned.1.call-done = bf16[2048,768]{1,0:T(8,128)(2,1)} async-done(((bf16[256,768]{1,0:T(8,128)(2,1)}), bf16[2048,768]{1,0:T(8,128)(2,1)}) %all-gather.9.cloned.1.call-update) | async-done | bytes 3145744 | tf_op jit(solution)/shard_map/all_gather | solution.py:117
  124.6 41.8 %all-gather.11.cloned.1.call-done = bf16[512,2048]{1,0:T(8,128)(2,1)} async-done(((bf16[512,256]{1,0:T(8,128)(2,1)}), bf16[512,2048]{1,0:T(8,128)(2,1)}) %all-gather.11.cloned.1.call-update) | async-done | bytes 2097168 | tf_op jit(solution)/shard_map/all_gather | solution.py:119
  171.2 12.3 scatter_custom_fusion
  184.2 36.1 %all-reduce.14.cloned.1.call-done = bf16[512,2048]{1,0:T(8,128)(2,1)} async-done(((bf16[512,2048]{1,0:T(8,128)(2,1)}), bf16[512,2048]{1,0:T(8,128)(2,1)}) %all-reduce.14.cloned.1.call-update) | async-done | bytes 2097168 | tf_op jit(solution)/shard_map/psum | solution.py:167
  223.7 6.2 fusion.90
  232.8 37.0 %gather_fusion = bf16[4608,2048]{1,0:T(8,128)(2,1)} fusion(bf16[513,2048]{1,0:T(8,128)(2,1)} %concatenate.41, s32[5120]{0:T(1024)S(1)} %pad_clamp_fusion.1), kind=kCustom, calls=%fused_computation | custom fusion | bytes 37767168 | tf_op jit(solution)/shard_map/gather | solution.py:195
  269.7 416.2 %all_to_all.20 = bf16[8,2,288,2048]{3,2,1,0:T(8,128)(2,1)} all-to-all(bf16[8,2,288,2048]{3,2,1,0:T(8,128)(2,1)} %bitcast.162), channel_id=1, replica_groups=mesh['expert'=8,'tensor'=4] {'expert'}, dimensions={0} | all-to-all | bytes 37748736 | tf_op jit(solution)/shard_map/all_to_all | solution.py:196
  685.9 15.6 fusion.8
  701.6 18.6 fusion.13
  720.2 14.8 convert_bitcast_fusion
  734.9 16.9 copy.98
  751.9 6.2 all-to-all-start.1
  758.4 13.0 mul.599
  771.3 29.6 mul.600
  803.8 361.1 %all-to-all-done.1 = bf16[8,2,288,2048]{3,2,1,0:T(8,128)(2,1)} async-done(((bf16[8,2,288,2048]{3,2,1,0:T(8,128)(2,1)}), bf16[8,2,288,2048]{3,2,1,0:T(8,128)(2,1)}, u32[]{:S(2)}, u32[]{:S(2)}) %all-to-all-start.1) | async-done | bytes 18874400 | tf_op jit(solution)/shard_map/all_to_all | solution.py:204
  1164.9 16.9 concatenate.42
  1181.8 32.7 %gather_fusion.1 = bf16[3072,2048]{1,0:T(8,128)(2,1)} fusion(bf16[4609,2048]{1,0:T(8,128)(2,1)} %concatenate.42, s32[3072]{0:T(1024)S(1)} %broadcast_clamp_fusion.1), kind=kCustom, calls=%fused_computation.1 | custom fusion | bytes 25178112 | tf_op jit(solution)/shard_map/gather | solution.py:207
  1214.5 20.3 reshape.352
  1234.8 14.5 fusion.21
  1250.4 9.6 multiply_convert_fusion
  1260.1 5.8 concatenate.43
  1265.8 41.5 %gather_fusion.2 = bf16[4608,2048]{1,0:T(8,128)(2,1)} fusion(bf16[3073,2048]{1,0:T(8,128)(2,1)} %concatenate.43, s32[5120]{0:T(1024)S(1)} %pad_clamp_fusion), kind=kCustom, calls=%fused_computation.2 | custom fusion | bytes 37767168 | tf_op jit(solution)/shard_map/gather | solution.py:245
  1307.4 414.2 %all_to_all.21 = bf16[8,2,288,2048]{3,2,1,0:T(8,128)(2,1)} all-to-all(bf16[8,2,288,2048]{3,2,1,0:T(8,128)(2,1)} %bitcast.163), channel_id=1, replica_groups=mesh['expert'=8,'tensor'=4] {'expert'}, dimensions={0} | all-to-all | bytes 37748736 | tf_op jit(solution)/shard_map/all_to_all | solution.py:248
  1721.6 19.9 fusion.12
  1741.5 19.7 fusion.35
  1761.2 22.5 fusion.1
  1786.2 319.1 %all-reduce.18.cloned.1.call-done = bf16[8,2,288,2048]{3,2,0,1:T(8,128)(2,1)} async-done(((bf16[8,2,288,2048]{3,2,0,1:T(8,128)(2,1)}), bf16[8,2,288,2048]{3,2,0,1:T(8,128)(2,1)}) %all-reduce.18.cloned.1.call-update) | async-done | bytes 18874384
  2110.6 5.6 all-to-all-start.3
  2117.1 125.9 %all-gather.15.cloned.1.call-done = bf16[2048,704]{0,1:T(8,128)(2,1)} async-done(((bf16[256,704]{0,1:T(8,128)(2,1)}), bf16[2048,704]{0,1:T(8,128)(2,1)}) %all-gather.15.cloned.1.call-update) | async-done | bytes 2883600 | tf_op jit(solution)/shard_map/all_gather | solution.py:121
  2242.9 4.6 fusion.100
  2247.6 55.8 %all-gather.13.cloned.1.call-done = bf16[2048,704]{0,1:T(8,128)(2,1)} async-done(((bf16[256,704]{0,1:T(8,128)(2,1)}), bf16[2048,704]{0,1:T(8,128)(2,1)}) %all-gather.13.cloned.1.call-update) | async-done | bytes 2883600 | tf_op jit(solution)/shard_map/all_gather | solution.py:120
  2303.4 4.6 fusion.99
  2308.0 55.7 %all-gather.17.cloned.1.call-done = bf16[704,2048]{1,0:T(8,128)(2,1)} async-done(((bf16[704,256]{1,0:T(8,128)(2,1)}), bf16[704,2048]{1,0:T(8,128)(2,1)}) %all-gather.17.cloned.1.call-update) | async-done | bytes 2883600 | tf_op jit(solution)/shard_map/all_gather | solution.py:122
  2363.7 6.6 multiply_convert_fusion.5
  2378.1 5.3 concatenate.44
  2383.4 27.0 gather_fusion.3
  2410.3 22.1 reshape.356
  2432.4 17.9 reduce_sum.184
  2450.3 8.2 add_convert_fusion.3
  2466.4 5.2 convolution_convert_fusion.3
  2471.8 15.2 multiply_reduce_fusion
  2490.2 18.1 all-reduce.16.cloned.1.call-done
  2520.7 8.7 fusion.55
  2530.7 9.6 fusion.52
  2549.4 6.5 add_convert_fusion.2
  2559.1 5.0 convolution_convert_fusion.4
  2568.0 17.4 reduce-scatter.14.cloned.1.call-done
  2587.3 74.1 %reduce-scatter.16.cloned.1.call-done = bf16[256,704]{0,1:T(8,128)(2,1)} async-done(((bf16[2048,704]{0,1:T(8,128)(2,1)}), bf16[256,704]{0,1:T(8,128)(2,1)}) %reduce-scatter.16.cloned.1.call-update) | async-done | bytes 360464 | tf_op jit(solution)/shard_map/reduce_scatter | solution.py:330
  2663.3 73.9 %reduce-scatter.18.cloned.1.call-done = bf16[704,256]{1,0:T(8,128)(2,1)} async-done(((bf16[704,2048]{1,0:T(8,128)(2,1)}), bf16[704,256]{1,0:T(8,128)(2,1)}) %reduce-scatter.18.cloned.1.call-update) | async-done | bytes 360464 | tf_op jit(solution)/shard_map/reduce_scatter | solution.py:333
  2742.3 14.3 convolution_bitcast_fusion
  2756.6 13.7 fusion.25
  2770.3 5.7 fusion.62
  2776.0 13.7 convolution_bitcast_fusion.1
  2793.4 31.8 all-reduce.22.cloned.1.call-done
  2829.4 62.6 %reduce-scatter.10.cloned.1.call-done = bf16[64,1024]{1,0:T(8,128)(2,1)} async-done(((bf16[512,1024]{1,0:T(8,128)(2,1)}), bf16[64,1024]{1,0:T(8,128)(2,1)}) %reduce-scatter.10.cloned.1.call-update) | async-done | bytes 131088 | tf_op jit(solution)/shard_map/reduce_scatter | solution.py:321
  2893.6 6.2 convert_multiply_fusion
  2901.2 40.8 %all-reduce.5 = (f32[2048]{0:T(1024)}, f32[512]{0:T(512)}, f32[2048]{0:T(1024)}) all-reduce(f32[2048]{0:T(1024)S(1)} %fusion.61, f32[512]{0:T(512)S(1)} %copy-done.95, f32[2048]{0:T(1024)S(1)} %fusion.60), channel_id=1, replica_groups=mesh['expert'=8,'tensor'=4] {'expert','tensor'}, use_global_device_ids=true, to_apply=%region_27.28 | all-reduce | flops 4608 | bytes 36864 | tf_op jit(solution)/shard_map/psum | solution.py:313
  2942.0 5.4 add_convert_fusion.1
  2947.5 15.5 reduce-scatter.12.cloned.1.call-done
  2964.8 75.3 %reduce-scatter.8.cloned.1.call-done = bf16[256,768]{1,0:T(8,128)(2,1)} async-done(((bf16[2048,768]{1,0:T(8,128)(2,1)}), bf16[256,768]{1,0:T(8,128)(2,1)}) %reduce-scatter.8.cloned.1.call-update) | async-done | bytes 393232 | tf_op jit(solution)/shard_map/reduce_scatter | solution.py:318
  3042.0 150.2 %all-reduce.20.cloned.1.call-done = (f32[2048,576]{0,1:T(8,128)}, f32[2048,16]{0,1:T(8,128)}) async-done(((f32[2048,576]{0,1:T(8,128)}, f32[2048,16]{0,1:T(8,128)}), (f32[2048,576]{0,1:T(8,128)}, f32[2048,16]{0,1:T(8,128)})) %all-reduce.20.cloned.1.call-update) | async-done | bytes 4849680 | tf_op jit(solution)/shard_map/psum | solution.py:313
  3192.2 5.2 copy.158
  (342 shorter events, 141.3 us)
Async XLA Ops:
  7.2 713.0 %copy-start = (bf16[2,352,2048]{2,1,0:T(8,128)(2,1)S(1)}, bf16[2,352,2048]{2,1,0:T(8,128)(2,1)}, u32[]{:S(2)}) copy-start(bf16[2,352,2048]{2,1,0:T(8,128)(2,1)} %param.34) | copy-start | bytes 8650756
  7.2 19.0 copy-start.54
  7.2 45.9 %all-gather.7.cloned.1.call-start = ((), (), s32[]{:S(2)}) async-start(), calls=%async_computation.10 | async-start | bytes 1179648 | tf_op jit(solution)/shard_map/all_gather | solution.py:118
  7.9 106.6 %all-gather.9.cloned.1.call-start = ((), (), s32[]{:S(2)}) async-start(), calls=%async_computation.11 | async-start | bytes 3538944 | tf_op jit(solution)/shard_map/all_gather | solution.py:117
  8.7 157.6 %all-gather.11.cloned.1.call-start = ((), (), s32[]{:S(2)}) async-start(), calls=%async_computation.12 | async-start | bytes 2359296 | tf_op jit(solution)/shard_map/all_gather | solution.py:119
  9.4 210.8 %all-reduce.14.cloned.1.call-start = ((), (), s32[]{:S(2)}) async-start(), calls=%async_computation.13 | async-start | bytes 4194304 | tf_op jit(solution)/shard_map/psum | solution.py:167
  15.0 99.5 %copy-start.72 = (f32[512]{0:T(512)}, f32[512]{0:T(512)S(1)}, u32[]{:S(2)}) copy-start(f32[512]{0:T(512)S(1)} %add_rsqrt_fusion.2) | copy-start | bytes 6148
  31.2 22.0 copy-start.91
  32.1 87.0 %copy-start.32 = (f32[512,32]{0,1:T(8,128)}, f32[512,32]{0,1:T(8,128)S(1)}, u32[]{:S(2)}) copy-start(f32[512,32]{0,1:T(8,128)S(1)} %get-tuple-element.55) | copy-start | bytes 196612
  32.1 87.0 %copy-start.34 = (f32[512,32]{0,1:T(8,128)}, f32[512,32]{0,1:T(8,128)S(1)}, u32[]{:S(2)}) copy-start(f32[512,32]{0,1:T(8,128)S(1)} %get-tuple-element.56) | copy-start | bytes 196612
  45.9 12.9 copy-start.87
  59.8 59.5 %copy-start.41 = (bf16[512,4,128]{0,2,1:T(8,128)(2,1)}, bf16[512,4,128]{0,2,1:T(8,128)(2,1)S(1)}, u32[]{:S(2)}) copy-start(bf16[512,4,128]{0,2,1:T(8,128)(2,1)S(1)} %slice.97) | copy-start | bytes 1572868
  124.5 99.1 %copy-start.45 = (bf16[4,128,512]{2,1,0:T(8,128)(2,1)}, bf16[4,128,512]{2,1,0:T(8,128)(2,1)S(1)}, u32[]{:S(2)}) copy-start(bf16[4,128,512]{2,1,0:T(8,128)(2,1)S(1)} %convolution_convert_fusion.10) | copy-start | bytes 1572868
  124.5 46.0 %copy-start.74 = (s32[3072,1]{0,1:T(1,128)S(1)}, s32[3072,1]{0,1:T(1,128)}, u32[]{:S(2)}) copy-start(s32[3072,1]{0,1:T(1,128)} %mul.612) | copy-start | bytes 36868
  124.5 46.0 %copy-start.75 = (s32[3072,1]{0,1:T(1,128)S(1)}, s32[3072,1]{0,1:T(1,128)}, u32[]{:S(2)}) copy-start(s32[3072,1]{0,1:T(1,128)} %mul.570) | copy-start | bytes 36868
  124.5 46.0 %copy-start.76 = (s32[3072]{0:T(1024)S(1)}, s32[3072]{0:T(1024)}, u32[]{:S(2)}) copy-start(s32[3072]{0:T(1024)} %fusion.66) | copy-start | bytes 36868
  124.5 46.0 %copy-start.77 = (pred[3072,1]{0,1:T(4,128)(4,1)S(1)}, pred[3072,1]{0,1:T(4,128)(4,1)}, u32[]{:S(2)}) copy-start(pred[3072,1]{0,1:T(4,128)(4,1)} %gt.19) | copy-start | bytes 9220
  170.5 53.1 %copy-start.63 = (f32[2048]{0:T(1024)S(1)}, f32[2048]{0:T(1024)}, u32[]{:S(2)}) copy-start(f32[2048]{0:T(1024)} %param.27) | copy-start | bytes 24580
  171.2 58.7 %copy-start.79 = (s32[3072,1]{0,1:T(1,128)}, s32[3072,1]{0,1:T(1,128)S(1)}, u32[]{:S(2)}) copy-start(s32[3072,1]{0,1:T(1,128)S(1)} %get-tuple-element.48) | copy-start | bytes 36868
  183.5 46.4 %copy-start.69 = (f32[512]{0:T(512)}, f32[512]{0:T(512)S(1)}, u32[]{:S(2)}) copy-start(f32[512]{0:T(512)S(1)} %fusion.79) | copy-start | bytes 6148
  269.7 416.2 %copy-start.21 = (bf16[2,2048,352]{1,2,0:T(8,128)(2,1)S(1)}, bf16[2,2048,352]{1,2,0:T(8,128)(2,1)}, u32[]{:S(2)}) copy-start(bf16[2,2048,352]{1,2,0:T(8,128)(2,1)} %param.32) | copy-start | bytes 8650756
  751.9 6.5 copy-start.80
  751.9 413.0 %all-to-all-start.1 = ((bf16[8,2,288,2048]{3,2,1,0:T(8,128)(2,1)}), bf16[8,2,288,2048]{3,2,1,0:T(8,128)(2,1)}, u32[]{:S(2)}, u32[]{:S(2)}) async-start(bf16[8,2,288,2048]{3,2,1,0:T(8,128)(2,1)} %copy.98), calls=%async_computation.1 | async-start | bytes 37748736 | tf_op jit(solution)/shard_map/all_to_all | solution.py:204
  758.1 1347.2 %all-reduce.18.cloned.1.call-start = ((), (), s32[]{:S(2)}) async-start(), calls=%async_computation.24 | async-start | bytes 37748736
  771.3 29.6 copy-start.47
  803.2 378.6 %copy-start.81 = (f32[512]{0:T(512)}, f32[512]{0:T(512)S(1)}, u32[]{:S(2)}) copy-start(f32[512]{0:T(512)S(1)} %get-tuple-element.63) | copy-start | bytes 6148
  803.8 378.0 %copy-start.85 = (f32[512]{0:T(512)}, f32[512]{0:T(512)S(1)}, u32[]{:S(2)}) copy-start(f32[512]{0:T(512)S(1)} %fusion.71) | copy-start | bytes 6148
  803.8 445.6 %copy-start.38 = (f32[512,16]{0,1:T(8,128)}, f32[512,16]{0,1:T(8,128)S(1)}, u32[]{:S(2)}) copy-start(f32[512,16]{0,1:T(8,128)S(1)} %fusion.70) | copy-start | bytes 98308
  1234.8 14.6 copy-start.56
  1234.8 15.2 copy-start.70
  1250.2 9.8 copy-start.24
  1741.5 19.7 copy-start.20
  1783.6 459.3 %all-gather.15.cloned.1.call-start = ((), (), s32[]{:S(2)}) async-start(), calls=%async_computation.15 | async-start | bytes 3244032 | tf_op jit(solution)/shard_map/all_gather | solution.py:121
  1784.2 519.2 %all-gather.13.cloned.1.call-start = ((), (), s32[]{:S(2)}) async-start(), calls=%async_computation.14 | async-start | bytes 3244032 | tf_op jit(solution)/shard_map/all_gather | solution.py:120
  2110.6 6.4 copy-start.78
  2110.6 132.3 %copy-start.6 = (bf16[512,2048]{1,0:T(8,128)(2,1)S(1)}, bf16[512,2048]{1,0:T(8,128)(2,1)}, u32[]{:S(2)}) copy-start(bf16[512,2048]{1,0:T(8,128)(2,1)} %copy-done.5) | copy-start | bytes 6291460
  2110.6 267.5 %all-to-all-start.3 = ((bf16[8,2,72,2048]{3,2,1,0:T(8,128)(2,1)}), bf16[8,2,72,2048]{3,2,1,0:T(8,128)(2,1)}, u32[]{:S(2)}, u32[]{:S(2)}) async-start(bf16[8,2,72,2048]{3,2,1,0:T(8,128)(2,1)} %copy.102), calls=%async_computation.3 | async-start | bytes 9437184 | tf_op jit(solution)/shard_map/all_to_all | solution.py:260
  2116.3 247.4 %all-gather.17.cloned.1.call-start = ((), (), s32[]{:S(2)}) async-start(), calls=%async_computation.16 | async-start | bytes 3244032 | tf_op jit(solution)/shard_map/all_gather | solution.py:122
  2117.0 391.3 %all-reduce.16.cloned.1.call-start = ((), (), s32[]{:S(2)}) async-start(), calls=%async_computation.17 | async-start | bytes 4194304 | tf_op jit(solution)/shard_map/psum | solution.py:267
  2247.6 116.1 %copy-start.71 = (f32[512]{0:T(512)S(1)}, f32[512]{0:T(512)}, u32[]{:S(2)}) copy-start(f32[512]{0:T(512)} %copy-done.69) | copy-start | bytes 6148
  2363.7 6.6 copy-start.22
  2370.2 7.8 copy-start.30
  2378.1 72.2 %copy-start.89 = (f32[512]{0:T(512)}, f32[512]{0:T(512)S(1)}, u32[]{:S(2)}) copy-start(f32[512]{0:T(512)S(1)} %multiply_reduce_fusion.8) | copy-start | bytes 6148
  2432.4 17.9 copy-start.39
  2432.4 17.9 copy-start.48
  2458.6 126.8 %reduce-scatter.14.cloned.1.call-start = ((), (), s32[]{:S(2)}) async-start(), calls=%async_computation.21 | async-start | bytes 3244032 | tf_op jit(solution)/shard_map/reduce_scatter | solution.py:327
  2463.0 198.4 %reduce-scatter.16.cloned.1.call-start = ((), (), s32[]{:S(2)}) async-start(), calls=%async_computation.22 | async-start | bytes 3244032 | tf_op jit(solution)/shard_map/reduce_scatter | solution.py:330
  2466.3 270.9 %reduce-scatter.18.cloned.1.call-start = ((), (), s32[]{:S(2)}) async-start(), calls=%async_computation.23 | async-start | bytes 3244032 | tf_op jit(solution)/shard_map/reduce_scatter | solution.py:333
  2471.7 15.3 copy-start.102
  2471.7 353.5 %all-reduce.22.cloned.1.call-start = ((), (), s32[]{:S(2)}) async-start(), calls=%async_computation.26 | async-start | bytes 8388608 | tf_op jit(solution)/shard_map/psum | solution.py:216
  2471.8 15.3 copy-start.97
  2487.0 21.3 copy-start.64
  2490.2 21.7 copy-start.84
  2520.7 10.0 copy-start.42
  2530.7 12.4 copy-start.33
  2530.7 12.4 copy-start.35
  2556.0 336.0 %reduce-scatter.10.cloned.1.call-start = ((), (), s32[]{:S(2)}) async-start(), calls=%async_computation.19 | async-start | bytes 1179648 | tf_op jit(solution)/shard_map/reduce_scatter | solution.py:321
  2559.1 404.0 %reduce-scatter.12.cloned.1.call-start = ((), (), s32[]{:S(2)}) async-start(), calls=%async_computation.20 | async-start | bytes 2359296 | tf_op jit(solution)/shard_map/reduce_scatter | solution.py:324
  2564.2 475.9 %reduce-scatter.8.cloned.1.call-start = ((), (), s32[]{:S(2)}) async-start(), calls=%async_computation.18 | async-start | bytes 3538944 | tf_op jit(solution)/shard_map/reduce_scatter | solution.py:318
  2567.9 171.2 %copy-start.90 = (f32[512]{0:T(512)S(1)}, f32[512]{0:T(512)}, u32[]{:S(2)}) copy-start(f32[512]{0:T(512)} %copy-done.89) | copy-start | bytes 6148
  2567.9 624.3 %all-reduce.20.cloned.1.call-start = ((), (), s32[]{:S(2)}) async-start(), calls=%async_computation.25 | async-start | bytes 9699328 | tf_op jit(solution)/shard_map/psum | solution.py:313
  2756.6 13.7 copy-start.19
  2756.6 13.7 copy-start.50
  2893.6 7.6 copy-start.95
  (58 other events, 186.5 us)
Sparse Core Ops, SparseCore 0:
  10.2 42.8 all-gather.6
  55.3 59.1 all-gather.8
  116.6 49.6 all-gather.10
  170.6 49.5 all-reduce.13
  1783.8 321.5 all-reduce.17
  2107.2 135.6 all-gather.14
  2245.0 58.3 all-gather.12
  2305.4 58.1 all-gather.16
  2458.7 49.5 all-reduce.15
  2512.7 72.6 reduce-scatter.13
  2589.9 71.4 reduce-scatter.15
  2665.8 71.3 reduce-scatter.17
  2740.3 84.8 all-reduce.21
  2828.5 63.4 reduce-scatter.9
  2895.8 67.1 reduce-scatter.11
  2966.9 73.1 reduce-scatter.7
  3047.7 144.4 all-reduce.19
where the time goes:
time: 3220 us; the launch traced here: 3200 us
  waiting for transfers between devices  1580 us (49%)
  blocking collectives  871 us (27%)
  local copies, waits for them, and re-layouts  317 us (10%)
  matrix products  287 us (9%)
  other arithmetic  120 us (4%)
    all_to_all x1, blocking collectives, shards(): lax.all_to_all(outgoing, 'expert', split_axis=0, concat_axis=0, tiled=True)  416 us
    all_to_all x1, blocking collectives, shards(): lax.all_to_all(dslots, 'expert', split_axis=0, concat_axis=0, tiled=True)  414 us
    all_to_all x1, waiting for transfers between devices, shards(): lax.all_to_all(partial_value, 'expert', split_axis=0, concat_axis=0, tile...  361 us
    unnamed x18, waiting for transfers between devices  323 us
    psum x1, waiting for transfers between devices, shards(): lax.psum((grad_latent, grad_gain_attn, grad_gain_latent, grad_gain_ffn, g...  150 us
    all_gather x1, waiting for transfers between devices, shards(): lax.all_gather(w_shared_up, 'expert', axis=0, tiled=True)  126 us
    reduce_scatter x1, waiting for transfers between devices, shards(): lax.psum_scatter(grad_query.astype(jnp.bfloat16), 'expert', scatter_dimen...  75.3 us
    reduce_scatter x1, waiting for transfers between devices, shards(): lax.psum_scatter(grad_sup.astype(jnp.bfloat16), 'expert', scatter_dimensi...  74.1 us
  transfers between devices with their start and end apart: 19, of which 18 were waited for; matrix products, arithmetic and copies ran while one was open for 10% of the time, Pallas kernels for 0%

commit v1 on v0

v1 whole, which is shorter than its diff:
```python
import functools

import jax
import jax.numpy as jnp
from jax import lax
from jax.experimental import pallas as pl
from jax.experimental.pallas import tpu as pltpu
from jax.sharding import PartitionSpec as P

F32, BF16 = jnp.float32, jnp.bfloat16

NOPE = 128
ROPE = 64
VD = 128
KVR = 512


EPS = 1e-06
ROPE_BASE = 10000.0


def inv_rms(v):
    return lax.rsqrt(jnp.mean(v * v, axis=-1, keepdims=True) + EPS)


def rope_tables(count, width):
    half = width // 2
    freq = ROPE_BASE ** (-(jnp.arange(half, dtype=jnp.float32) * 2.0 / width))
    angle = jnp.arange(count, dtype=jnp.float32)[:, None] * freq[None, :]
    return (jnp.cos(angle), jnp.sin(angle))


def rotate(v, cosine, sine):
    half = v.shape[-1] // 2
    first = v[..., :half]
    second = v[..., half:]
    return jnp.concatenate(
        [first * cosine - second * sine, second * cosine + first * sine], axis=-1
    )


def rotate_back(grad, cosine, sine):
    half = grad.shape[-1] // 2
    first = grad[..., :half]
    second = grad[..., half:]
    return jnp.concatenate(
        [first * cosine + second * sine, second * cosine - first * sine], axis=-1
    )


def norm_back(grad, normed, scale_row, gain):
    weighted = grad * gain
    return scale_row * (weighted - normed * jnp.mean(weighted * normed, axis=-1, keepdims=True))


def silu_parts(gate):
    sig = jax.nn.sigmoid(gate)
    return (gate * sig, sig * (1.0 + gate * (1.0 - sig)))


def mat(left, right):
    return jnp.dot(left, right, preferred_element_type=jnp.float32)


def mat_tn(left, right):
    return lax.dot_general(
        left, right, (((0,), (0,)), ((), ())), preferred_element_type=jnp.float32
    )


def mat_nt(left, right):
    return lax.dot_general(
        left, right, (((1,), (1,)), ((), ())), preferred_element_type=jnp.float32
    )


MESH = pl.DeviceIdType.MESH


def places():
    e, t = lax.axis_index("expert"), lax.axis_index("tensor")
    return e // 2, e % 2, t // 2, t % 2


def device(e1, e0, t1, t0):
    return (e1 * 2 + e0, t1 * 2 + t0)


def slot_of(e1, e0, t1, t0):
    return ((e1 * 2 + e0) * 2 + t1) * 2 + t0


def greet(peers):
    barrier = pltpu.get_barrier_semaphore()
    for peer in peers:
        pl.semaphore_signal(barrier, inc=1, device_id=peer, device_id_type=MESH)
    pl.semaphore_wait(barrier, len(peers))


def all_peers(far):
    e1, e0, t1, t0 = places()
    peers = [device((e1 + r) % far, e0, t1, t0) for r in range(1, far)]
    peers += [device(e1, 1 - e0, t1, t0), device(e1, e0, 1 - t1, t0), device(e1, e0, t1, 1 - t0)]
    return peers


def gather_kernel(far, x_ref, out_ref, send, recv, own):
    e1, e0, t1, t0 = places()
    m = x_ref.shape[0]
    half = m // 2
    greet(all_peers(far))
    mine = pltpu.make_async_copy(x_ref, out_ref.at[slot_of(e1, e0, t1, t0)], own)
    mine.start()
    ylink, xlink, core = (
        device(e1, 1 - e0, t1, t0),
        device(e1, e0, 1 - t1, t0),
        device(e1, e0, t1, 1 - t0),
    )

    def rel(r, b, c):
        return slot_of((e1 - r) % far, (e0 + b) % 2, (t1 + c) % 2, t0)

    def at_z(p, r):
        return p * 8 * far + r

    def at_1(p, r):
        return p * 8 * far + far + r

    def at_2(p, r, k):
        return p * 8 * far + 2 * far + 2 * r + k

    def at_c(p, r, k):
        return p * 8 * far + 4 * far + 4 * r + k

    started = []

    def send_piece(p, r, b, c, sem, to):
        rows = pl.ds(p * half, half)
        place = rel(r, b, c)
        src = x_ref.at[rows] if (r, b, c) == (0, 0, 0) else out_ref.at[place, rows]
        copy = pltpu.make_async_remote_copy(
            src_ref=src,
            dst_ref=out_ref.at[place, rows],
            send_sem=send.at[sem],
            recv_sem=recv.at[sem],
            device_id=to,
            device_id_type=MESH,
        )
        copy.start()
        started.append(copy)

    def wait_piece(p, sem):
        rows = pl.ds(p * half, half)
        pltpu.make_async_copy(x_ref.at[rows], out_ref.at[0, rows], recv.at[sem]).wait()

    for r in range(1, far):
        for p in range(2):
            send_piece(p, 0, 0, 0, at_z(p, r), device((e1 + r) % far, e0, t1, t0))
    firsts, seconds = (ylink, xlink), (xlink, ylink)

    def stage_a(r):
        for p in range(2):
            if r:
                wait_piece(p, at_z(p, r))
            send_piece(p, r, 0, 0, at_1(p, r), firsts[p])
            send_piece(p, r, 0, 0, at_2(p, r, 0), seconds[p])
        for p in range(2):
            send_piece(p, r, 0, 0, at_c(p, r, 0), core)

    def stage_b(r):
        for p in range(2):
            b, c = (1, 0) if p == 0 else (0, 1)
            wait_piece(p, at_1(p, r))
            send_piece(p, r, b, c, at_2(p, r, 1), seconds[p])
            send_piece(p, r, b, c, at_c(p, r, 1), core)

    def stage_c(r):
        for p in range(2):
            b, c = (0, 1) if p == 0 else (1, 0)
            wait_piece(p, at_2(p, r, 0))
            send_piece(p, r, b, c, at_c(p, r, 2), core)
            wait_piece(p, at_2(p, r, 1))
            send_piece(p, r, 1, 1, at_c(p, r, 3), core)

    for step in range(far + 2):
        if step < far:
            stage_a(step)
        if 0 <= step - 1 < far:
            stage_b(step - 1)
        if 0 <= step - 2 < far:
            stage_c(step - 2)
    for r in range(far):
        for p in range(2):
            for k in range(4):
                wait_piece(p, at_c(p, r, k))
    for copy in started:
        copy.wait_send()
    mine.wait()


def gather_all(x, groups, tensors, ident):
    m, width = x.shape
    far = groups // 2
    n = groups * tensors
    return pl.pallas_call(
        functools.partial(gather_kernel, far),
        out_shape=jax.ShapeDtypeStruct((n, m, width), x.dtype),
        in_specs=[pl.BlockSpec(memory_space=pl.ANY)],
        out_specs=pl.BlockSpec(memory_space=pl.ANY),
        scratch_shapes=[
            pltpu.SemaphoreType.DMA((16 * far,)),
            pltpu.SemaphoreType.DMA((16 * far,)),
            pltpu.SemaphoreType.DMA,
        ],
        compiler_params=pltpu.CompilerParams(collective_id=ident, has_side_effects=True),
    )(x)


def reduce_kernel(far, p_ref, out_ref, acc, rc, r1, r2, rz, load_sem, send, recv):
    e1, e0, t1, t0 = places()
    m = out_ref.shape[0]
    half = m // 2
    ylink, xlink, core = (
        device(e1, 1 - e0, t1, t0),
        device(e1, e0, 1 - t1, t0),
        device(e1, e0, t1, 1 - t0),
    )

    def dest(r, b, c, d):
        return slot_of((e1 + r) % far, (e0 + b) % 2, (t1 + c) % 2, (t0 + d) % 2)

    def plane(r, b, c):
        return r * 4 + b * 2 + c

    places_in_turn = [(1, 1), (0, 1), (1, 0), (0, 0)]
    turn = list(range(far - 1, -1, -1))
    loads = {}
    for r in turn:
        for b, c in places_in_turn:
            k = plane(r, b, c)
            copy = pltpu.make_async_copy(p_ref.at[dest(r, b, c, 0)], acc.at[k], load_sem.at[k])
            copy.start()
            loads[k] = copy
    greet(all_peers(far))
    started = []

    def push(src, dst, sem, to):
        copy = pltpu.make_async_remote_copy(
            src_ref=src,
            dst_ref=dst,
            send_sem=send.at[sem],
            recv_sem=recv.at[sem],
            device_id=to,
            device_id_type=MESH,
        )
        copy.start()
        started.append(copy)

    def arrived(ref, sem):
        pltpu.make_async_copy(ref, ref, recv.at[sem]).wait()

    def add(k, base, count, ref):
        @pl.loop(0, count // 16)
        def _(i):
            rows = pl.ds(pl.multiple_of(base + i * 16, 16), 16)
            there = pl.ds(pl.multiple_of(i * 16, 16), 16)
            acc[k, rows, :] = acc[k, rows, :] + ref[there, :]

    c_base, s1_base, s2_base, z_base = 0, 4 * far, 8 * far, 10 * far
    for r in turn:
        for b, c in places_in_turn:
            k = plane(r, b, c)
            push(p_ref.at[dest(r, b, c, 1)], rc.at[k], c_base + k, core)

    rows_of = (pl.ds(0, half), pl.ds(half, half))

    def stage_a(r):
        for b, c in places_in_turn:
            k = plane(r, b, c)
            loads[k].wait()
            arrived(rc.at[k], c_base + k)
            add(k, 0, m, rc.at[k])
            if c == 1:
                at = r * 2 + b
                push(acc.at[k, rows_of[0]], r1.at[0, at], s1_base + at, xlink)
            if b == 1:
                at = r * 2 + c
                push(acc.at[k, rows_of[1]], r1.at[1, at], s1_base + 2 * far + at, ylink)

    def stage_b(r):
        for j in (1, 0):
            at = r * 2 + j
            k = plane(r, j, 0)
            arrived(r1.at[0, at], s1_base + at)
            add(k, 0, half, r1.at[0, at])
            if j == 1:
                push(acc.at[k, rows_of[0]], r2.at[0, r], s2_base + r, ylink)
            k = plane(r, 0, j)
            arrived(r1.at[1, at], s1_base + 2 * far + at)
            add(k, half, half, r1.at[1, at])
            if j == 1:
                push(acc.at[k, rows_of[1]], r2.at[1, r], s2_base + far + r, xlink)

    def stage_c(r):
        k = plane(r, 0, 0)
        for p in range(2):
            arrived(r2.at[p, r], s2_base + p * far + r)
            add(k, p * half, half, r2.at[p, r])
        if r:
            push(acc.at[k], rz.at[r - 1], z_base + r, device((e1 + r) % far, e0, t1, t0))

    for step in range(far + 2):
        if step < far:
            stage_a(turn[step])
        if 0 <= step - 1 < far:
            stage_b(turn[step - 1])
        if 0 <= step - 2 < far:
            stage_c(turn[step - 2])
    for r in range(1, far):
        arrived(rz.at[r - 1], z_base + r)

    @pl.loop(0, m // 16)
    def _(i):
        rows = pl.ds(pl.multiple_of(i * 16, 16), 16)
        total = acc[0, rows, :].astype(F32)
        for r in range(1, far):
            total = total + rz[r - 1, rows, :].astype(F32)
        out_ref[rows, :] = total

    for copy in started:
        copy.wait_send()


def reduce_all(p, groups, tensors, ident):
    n, m, width = p.shape
    far = groups // 2
    return pl.pallas_call(
        functools.partial(reduce_kernel, far),
        out_shape=jax.ShapeDtypeStruct((m, width), F32),
        in_specs=[pl.BlockSpec(memory_space=pl.ANY)],
        out_specs=pl.BlockSpec(memory_space=pltpu.VMEM),
        scratch_shapes=[
            pltpu.VMEM((4 * far, m, width), BF16),
            pltpu.VMEM((4 * far, m, width), BF16),
            pltpu.VMEM((2, 2 * far, m // 2, width), BF16),
            pltpu.VMEM((2, far, m // 2, width), BF16),
            pltpu.VMEM((far - 1, m, width), BF16),
            pltpu.SemaphoreType.DMA((4 * far,)),
            pltpu.SemaphoreType.DMA((11 * far,)),
            pltpu.SemaphoreType.DMA((11 * far,)),
        ],
        compiler_params=pltpu.CompilerParams(
            collective_id=ident, has_side_effects=True, vmem_limit_bytes=56 * 2**20
        ),
    )(p)


TILE = 32


def dot_nt(left, right):
    return lax.dot_general(left, right, (((1,), (1,)), ((), ())), preferred_element_type=F32)


def dot_nn(left, right):
    return lax.dot_general(left, right, (((1,), (0,)), ((), ())), preferred_element_type=F32)


def ffn_kernel(
    counts,
    x_ref, dy_ref, picks_ref, wg_hbm, wu_hbm, wd_hbm, ws_hbm, wr_hbm,
    ffn_ref, dx_ref, dgates_ref, gg_hbm, gu_hbm, gd_hbm, gs_hbm,
    w_in, w_down, h, dh, hs, dgu, hsn, dgun, acc_in, acc_down, sem,
):
    experts, hidden, shared, total = counts
    routed = experts * hidden
    units = routed + shared
    step = pl.program_id(0)
    last = pl.num_programs(0) - 1
    block, width = x_ref.shape

    def loads():
        pairs = []
        for e in range(experts):
            at = pl.ds(e * hidden, hidden)
            pairs.append((wg_hbm.at[e], w_in.at[at]))
            pairs.append((wu_hbm.at[e], w_in.at[pl.ds(units + e * hidden, hidden)]))
            pairs.append((wd_hbm.at[e], w_down.at[at]))
        pairs.append((ws_hbm.at[0], w_in.at[pl.ds(routed, shared)]))
        pairs.append((ws_hbm.at[1], w_in.at[pl.ds(units + routed, shared)]))
        pairs.append((ws_hbm.at[2], w_down.at[pl.ds(routed, shared)]))
        pairs.append((wr_hbm, w_in.at[pl.ds(2 * units, total)]))
        return [pltpu.make_async_copy(a, b, sem.at[i]) for i, (a, b) in enumerate(pairs)]

    @pl.when(step == 0)
    def _():
        for c in loads():
            c.start()
        acc_in[...] = jnp.zeros_like(acc_in)
        acc_down[...] = jnp.zeros_like(acc_down)
        dgu[2 * units :, :] = jnp.zeros((dgu.shape[0] - 2 * units, block), BF16)
        hs[units:, :] = jnp.zeros((hs.shape[0] - units, block), BF16)
        for c in loads():
            c.wait()

    @pl.loop(0, block // 256)
    def _(n):
        at = pl.ds(pl.multiple_of(n * 256, 256), 256)
        h[:, at] = dot_nt(w_in[: 2 * units + total, :], x_ref[at, :])
        dh[:, at] = dot_nt(w_down[:units, :], dy_ref[at, :])

    logits = h[2 * units : 2 * units + total, :]
    expo = jnp.exp(logits - jnp.max(logits, axis=0, keepdims=True))
    gates = expo / jnp.sum(expo, axis=0, keepdims=True) * picks_ref[...]
    rows = []
    for s in range(experts + 1):
        base, count = (s * hidden, hidden) if s < experts else (routed, shared)
        gate = gates[s : s + 1, :] if s < experts else jnp.ones((1, block), F32)

        def body(i, total_):
            a = pl.multiple_of(base + i * TILE, TILE)
            here = pl.ds(a, TILE)
            there = pl.ds(pl.multiple_of(units + a, TILE), TILE)
            hg, hu, d = h[here, :], h[there, :], dh[here, :]
            sig = 1.0 / (1.0 + jnp.exp(-hg))
            act = hg * sig
            dact = sig + act * (1.0 - sig)
            hid = act * hu
            hs[here, :] = (hid * gate).astype(BF16)
            ds = d * gate
            dgu[here, :] = (ds * hu * dact).astype(BF16)
            dgu[there, :] = (ds * act).astype(BF16)
            return total_ + jnp.sum(hid * d, axis=0, keepdims=True)

        rows.append(lax.fori_loop(0, count // TILE, body, jnp.zeros((1, block), F32)))
    rows = rows[:experts]
    dgates_ref[...] = jnp.concatenate(rows + [jnp.zeros((8 - experts, block), F32)], axis=0)
    hsn[...] = hs[...].T
    dgun[...] = dgu[...].T

    @pl.loop(0, width // 256)
    def _(c):
        at = pl.ds(pl.multiple_of(c * 256, 256), 256)
        acc_in[:, at] += dot_nn(dgu[: 2 * units, :], x_ref[:, at])
        acc_down[:, at] += dot_nn(hs[:units, :], dy_ref[:, at])
        dx_ref[:, at] = dot_nn(dgun[:, : 2 * units], w_in[: 2 * units, at]).astype(BF16)
        ffn_ref[:, at] = dot_nn(hsn[:, :units], w_down[:, at]).astype(BF16)

    def stores():
        pairs = []
        for e in range(experts):
            at = pl.ds(e * hidden, hidden)
            pairs.append((acc_in.at[at], gg_hbm.at[e]))
            pairs.append((acc_in.at[pl.ds(units + e * hidden, hidden)], gu_hbm.at[e]))
            pairs.append((acc_down.at[at], gd_hbm.at[e]))
        pairs.append((acc_in.at[pl.ds(routed, shared)], gs_hbm.at[0]))
        pairs.append((acc_in.at[pl.ds(units + routed, shared)], gs_hbm.at[1]))
        pairs.append((acc_down.at[pl.ds(routed, shared)], gs_hbm.at[2]))
        return [pltpu.make_async_copy(a, b, sem.at[i]) for i, (a, b) in enumerate(pairs)]

    @pl.when(step == last)
    def _():
        for c in stores():
            c.start()
        for c in stores():
            c.wait()


def ffn_local(x, dy, picks, wg, wu, wd, ws, wr, block=512):
    n, width = x.shape
    experts, hidden, _ = wg.shape
    shared, total = ws.shape[1], wr.shape[0]
    units = experts * hidden + shared
    up = lambda v: -(-v // 128) * 128
    any_ = pl.BlockSpec(memory_space=pl.ANY)
    return pl.pallas_call(
        functools.partial(ffn_kernel, (experts, hidden, shared, total)),
        grid=(n // block,),
        in_specs=[
            pl.BlockSpec((block, width), lambda i: (i, 0)),
            pl.BlockSpec((block, width), lambda i: (i, 0)),
            pl.BlockSpec((total, block), lambda i: (0, i)),
            any_, any_, any_, any_, any_,
        ],
        out_specs=[
            pl.BlockSpec((block, width), lambda i: (i, 0)),
            pl.BlockSpec((block, width), lambda i: (i, 0)),
            pl.BlockSpec((8, block), lambda i: (0, i)),
            any_, any_, any_, any_,
        ],
        out_shape=[
            jax.ShapeDtypeStruct((n, width), BF16),
            jax.ShapeDtypeStruct((n, width), BF16),
            jax.ShapeDtypeStruct((8, n), F32),
            jax.ShapeDtypeStruct(wg.shape, F32),
            jax.ShapeDtypeStruct(wu.shape, F32),
            jax.ShapeDtypeStruct(wd.shape, F32),
            jax.ShapeDtypeStruct(ws.shape, F32),
        ],
        scratch_shapes=[
            pltpu.VMEM((2 * units + total, width), BF16),
            pltpu.VMEM((units, width), BF16),
            pltpu.VMEM((2 * units + total, block), F32),
            pltpu.VMEM((units, block), F32),
            pltpu.VMEM((up(units), block), BF16),
            pltpu.VMEM((up(2 * units), block), BF16),
            pltpu.VMEM((block, up(units)), BF16),
            pltpu.VMEM((block, up(2 * units)), BF16),
            pltpu.VMEM((2 * units, width), F32),
            pltpu.VMEM((units, width), F32),
            pltpu.SemaphoreType.DMA((3 * experts + 4,)),
        ],
        compiler_params=pltpu.CompilerParams(vmem_limit_bytes=63 * 2**20),
        cost_estimate=pl.CostEstimate(flops=18 * n * units * width, bytes_accessed=n * width * 8, transcendentals=0),
    )(x, dy, picks, wg, wu, wd, ws, wr)


BOTH = ("expert", "tensor")


def shards(
    tokens,
    lengths,
    routes,
    gain_attn,
    w_query,
    w_latent,
    gain_latent,
    w_kv,
    w_out,
    gain_ffn,
    w_router,
    w_shared_gate,
    w_shared_up,
    w_shared_down,
    w_gate,
    w_up,
    w_down,
    cotangent,
):
    groups = lax.axis_size("expert")
    tensors = lax.axis_size("tensor")
    eindex = lax.axis_index("expert")
    tindex = lax.axis_index("tensor")
    rows, width = tokens.shape
    quarter = rows // tensors
    experts_local, _, hidden_units = w_gate.shape
    total_experts = experts_local * groups
    every = groups * rows
    bf16, f32 = jnp.bfloat16, jnp.float32

    def own(v):
        return lax.dynamic_slice_in_dim(v, tindex * quarter, quarter, 0)

    live_int = (jnp.arange(rows) < lengths[0]).astype(jnp.int32)
    live = live_int.astype(f32)[:, None]
    live_own = own(live)
    cot_own = own(cotangent).astype(f32)
    dffn_own = (cot_own * live_own).astype(bf16)

    query_w = lax.all_gather(w_query, "expert", axis=0, tiled=True)
    kv_up = lax.all_gather(w_kv, "expert", axis=0, tiled=True)
    out_proj = lax.all_gather(w_out, "expert", axis=1, tiled=True)

    part = w_shared_down.shape[0] // groups
    spare = -part % TILE

    def shared_units(v):
        v = jnp.pad(v.reshape(groups, part, v.shape[1]), ((0, 0), (0, spare), (0, 0)))
        return v

    shared_w = jnp.stack(
        [shared_units(v) for v in (w_shared_gate.T, w_shared_up.T, w_shared_down)], axis=1
    )
    shared_w = lax.all_to_all(shared_w, "expert", split_axis=0, concat_axis=0, tiled=True)
    shared_w = shared_w.transpose(1, 2, 0, 3).reshape(3, part + spare, width)
    gate_t, up_t = w_gate.transpose(0, 2, 1), w_up.transpose(0, 2, 1)
    router_t = jnp.roll(w_router.T, -eindex * experts_local, axis=0)
    parts = max(1, every // 4096)
    some = quarter // parts

    def split(v):
        return v.reshape(parts, some, v.shape[1])

    choose = jnp.any(own(routes)[..., None] == jnp.arange(total_experts), axis=1).astype(F32)
    picks = choose * live_own
    picks_all = lax.all_gather(split(picks), BOTH, axis=1, tiled=True)
    picks_all = jnp.roll(picks_all.transpose(0, 2, 1), -eindex * experts_local, axis=1)
    dffn = [lax.all_gather(v, BOTH, axis=0, tiled=True) for v in split(dffn_own)]

    heads = out_proj.shape[0] // VD
    xf = tokens.astype(f32)
    scale_one = inv_rms(xf)
    normed_one = xf * scale_one
    xn1 = (normed_one * gain_attn).astype(bf16)
    cosine, sine = rope_tables(rows, ROPE)
    qfull = mat(xn1, query_w).reshape(rows, heads, NOPE + ROPE)
    qcat = jnp.concatenate(
        [qfull[..., :NOPE], rotate(qfull[..., NOPE:], cosine[:, None, :], sine[:, None, :])],
        axis=-1,
    ).astype(bf16)
    latent = mat(xn1, w_latent)
    comp = latent[:, :KVR]
    scale_lat = inv_rms(comp)
    normed_lat = comp * scale_lat
    compressed = (normed_lat * gain_latent).astype(bf16)
    key_rope = rotate(latent[:, KVR:], cosine, sine).astype(bf16)
    key_value = mat(compressed, kv_up).astype(bf16).reshape(rows, heads, NOPE + VD)
    keys = jnp.concatenate(
        [key_value[..., :NOPE], jnp.broadcast_to(key_rope[:, None, :], (rows, heads, ROPE))],
        axis=-1,
    )
    values = key_value[..., NOPE:]
    causal = jnp.arange(rows)[:, None] >= jnp.arange(rows)[None, :]
    score_scale = (NOPE + ROPE) ** (-0.5)
    raw = jnp.einsum("qhd,khd->hqk", qcat, keys, preferred_element_type=f32) * score_scale
    score_now = jnp.where(causal[None], raw, -jnp.inf)
    peak = jnp.max(score_now, axis=-1, keepdims=True)
    expo = jnp.exp(score_now - peak)
    pfull = expo / jnp.sum(expo, axis=-1, keepdims=True)
    probs = pfull.astype(bf16)
    attended = (
        jnp.einsum("hqk,khd->qhd", probs, values, preferred_element_type=f32)
        .astype(bf16)
        .reshape(rows, heads * VD)
    )
    attn = lax.psum_scatter(
        mat(attended, out_proj).astype(bf16), "tensor", scatter_dimension=0, tiled=True
    ).astype(f32)
    resid = own(xf) + live_own * attn
    scale_two = inv_rms(resid)
    normed_two = resid * scale_two
    xn2_own = (normed_two * gain_ffn).astype(bf16)
    router = jax.nn.softmax(mat(xn2_own, w_router), axis=-1)
    outs = []
    for k in range(parts):
        xn2 = gather_all(split(xn2_own)[k], groups, tensors, 3 * k).reshape(-1, width)
        ffn, dx, dgates, *grads = ffn_local(
            xn2, dffn[k], picks_all[k], gate_t, up_t, w_down, shared_w, router_t
        )
        dgates = lax.dynamic_update_slice_in_dim(
            jnp.zeros((xn2.shape[0], total_experts), F32),
            dgates[:experts_local].T,
            eindex * experts_local,
            1,
        )
        dgates = lax.psum_scatter(dgates, BOTH, scatter_dimension=0, tiled=True)
        dx = reduce_all(dx.reshape(-1, some, width), groups, tensors, 3 * k + 1)
        ffn = reduce_all(ffn.reshape(-1, some, width), groups, tensors, 3 * k + 2)
        outs.append((ffn, dx, dgates, *grads))
    ffn, dx, dgates = (jnp.concatenate(v, axis=0) for v in list(zip(*outs))[:3])
    grads = [functools.reduce(jnp.add, v) for v in list(zip(*outs))[3:]]
    drouter = picks * dgates
    output = lax.all_gather(
        (resid + live_own * ffn).astype(bf16), "tensor", axis=0, tiled=True
    )
    grad_gate, grad_up = (v.transpose(0, 2, 1) for v in grads[:2])
    grad_down = grads[2]
    shared_g = grads[3][:, :part].astype(BF16).reshape(3, part, groups, width // groups)
    shared_g = lax.all_to_all(
        shared_g.transpose(2, 0, 1, 3), "expert", split_axis=0, concat_axis=0, tiled=True
    )
    shared_g = shared_g.transpose(1, 0, 2, 3).reshape(3, groups * part, width // groups)
    grad_sgate, grad_sup, grad_sdown = shared_g[0].T, shared_g[1].T, shared_g[2]
    grad_sgate, grad_sup, grad_sdown = (
        v.astype(F32) for v in (grad_sgate, grad_sup, grad_sdown)
    )
    dlogit = router * (drouter - jnp.sum(router * drouter, axis=-1, keepdims=True))
    grad_router = mat_tn(xn2_own, dlogit.astype(bf16))
    dnorm_two = dx + mat_nt(dlogit.astype(bf16), w_router)
    grad_gain_ffn = jnp.sum(dnorm_two * normed_two, axis=0)
    dresid = cot_own + norm_back(dnorm_two, normed_two, scale_two, gain_ffn)
    dattn = lax.all_gather((dresid * live_own).astype(bf16), "tensor", axis=0, tiled=True)
    grad_out = mat_tn(attended, dattn)
    dattended = mat_nt(dattn, out_proj).astype(bf16).reshape(rows, heads, VD)
    dvalues = jnp.einsum("hqk,qhd->khd", probs, dattended, preferred_element_type=f32)
    dprobs = jnp.einsum("qhd,khd->hqk", dattended, values, preferred_element_type=f32)
    dscore = (
        pfull * (dprobs - jnp.sum(pfull * dprobs, axis=-1, keepdims=True)) * score_scale
    ).astype(bf16)
    dquery = jnp.einsum("hqk,khd->qhd", dscore, keys, preferred_element_type=f32)
    dkeys = jnp.einsum("hqk,qhd->khd", dscore, qcat, preferred_element_type=f32)
    dkv = (
        jnp.concatenate([dkeys[..., :NOPE], dvalues], axis=-1)
        .astype(bf16)
        .reshape(rows, heads * (NOPE + VD))
    )
    grad_kv = mat_tn(compressed, dkv)
    dcomp = mat_nt(dkv, kv_up)
    grad_gain_latent = jnp.sum(dcomp * normed_lat, axis=0)
    dlatent = jnp.concatenate(
        [
            norm_back(dcomp, normed_lat, scale_lat, gain_latent),
            rotate_back(jnp.sum(dkeys[..., NOPE:], axis=1), cosine, sine),
        ],
        axis=-1,
    ).astype(bf16)
    dqfull = jnp.concatenate(
        [dquery[..., :NOPE], rotate_back(dquery[..., NOPE:], cosine[:, None, :], sine[:, None, :])],
        axis=-1,
    )
    dqfull = dqfull.astype(bf16).reshape(rows, heads * (NOPE + ROPE))
    grad_query = mat_tn(xn1, dqfull)
    grad_latent = mat_tn(xn1, dlatent)
    dnorm_one = mat_nt(dqfull, query_w) + mat_nt(dlatent, w_latent)
    dnorm_one = lax.psum_scatter(
        dnorm_one.astype(bf16), "tensor", scatter_dimension=0, tiled=True
    ).astype(f32)
    normed_own = own(normed_one)
    grad_gain_attn = jnp.sum(dnorm_one * normed_own, axis=0)
    grad_tokens = (dresid + norm_back(dnorm_one, normed_own, own(scale_one), gain_attn)).astype(bf16)
    grad_tokens = lax.all_gather(grad_tokens, "tensor", axis=0, tiled=True)
    small = jnp.concatenate(
        [
            grad_latent,
            grad_router,
            grad_gain_attn[:, None],
            grad_gain_ffn[:, None],
            jnp.pad(grad_gain_latent, (0, width - KVR))[:, None],
        ],
        axis=1,
    ).astype(bf16)
    pad = -small.shape[1] % 128
    small = jnp.pad(small, ((0, 0), (0, pad)))
    small = lax.psum_scatter(small, BOTH, scatter_dimension=0, tiled=True)
    small = lax.all_gather(small, BOTH, axis=0, tiled=True).astype(f32)
    at = w_latent.shape[1]
    grad_latent = small[:, :at]
    grad_router = small[:, at : at + total_experts]
    at = at + total_experts
    grad_gain_attn = small[:, at]
    grad_gain_ffn = small[:, at + 1]
    grad_gain_latent = small[:KVR, at + 2]
    grad_query = lax.psum_scatter(
        grad_query.astype(bf16), "expert", scatter_dimension=0, tiled=True
    ).astype(f32)
    grad_kv = lax.psum_scatter(
        grad_kv.astype(bf16), "expert", scatter_dimension=0, tiled=True
    ).astype(f32)
    grad_out = lax.psum_scatter(
        grad_out.astype(bf16), "expert", scatter_dimension=1, tiled=True
    ).astype(f32)
    return (
        output,
        grad_tokens,
        grad_gain_attn,
        grad_query,
        grad_latent,
        grad_gain_latent,
        grad_kv,
        grad_out,
        grad_gain_ffn,
        grad_router,
        grad_sgate,
        grad_sup,
        grad_sdown,
        grad_gate,
        grad_up,
        grad_down,
    )


def solution(mesh):
    in_specs = (
        P("expert", None),
        P("expert"),
        P("expert", None),
        P(),
        P("expert", "tensor"),
        P(),
        P(),
        P("expert", "tensor"),
        P("tensor", "expert"),
        P(),
        P(),
        P("expert", "tensor"),
        P("expert", "tensor"),
        P("tensor", "expert"),
        P("expert", None, "tensor"),
        P("expert", None, "tensor"),
        P("expert", "tensor", None),
        P("expert", None),
    )
    out_specs = (
        P("expert", None),
        P("expert", None),
        P(),
        P("expert", "tensor"),
        P(),
        P(),
        P("expert", "tensor"),
        P("tensor", "expert"),
        P(),
        P(),
        P("expert", "tensor"),
        P("expert", "tensor"),
        P("tensor", "expert"),
        P("expert", None, "tensor"),
        P("expert", None, "tensor"),
        P("expert", "tensor", None),
    )
    return jax.shard_map(shards, mesh=mesh, in_specs=in_specs, out_specs=out_specs, check_vma=False)
```

time: 3220 us -> 1390 us (0.43)
  waiting for transfers between devices: 1580 us -> 614 us
  blocking collectives: 871 us -> 91.5 us
  Pallas kernels: 0 us -> 491 us
  local copies, waits for them, and re-layouts: 317 us -> 58 us
  matrix products: 287 us -> 62.8 us
  other arithmetic: 120 us -> 38.8 us
    all_to_all x2 -> x1, blocking collectives: 830 us -> 24.7 us  [shards(): lax.all_to_all(shared_g.transpose(2, 0, 1, 3), 'expert', split_axis=0, co...]
    pallas_call x0 -> x4, Pallas kernels: none -> 491 us  [the longest x2 208 us: reduce_all(): pl.pallas_call(functools.partial(reduce_kernel, far), out_shape=jax.Shape...]
    all_to_all x2 -> x1, waiting for transfers between devices: 361 us -> 0.01 us  [shards(): lax.all_to_all(shared_w, 'expert', split_axis=0, concat_axis=0, tiled=True)]
    unnamed x18 -> x15, waiting for transfers between devices: 323 us -> 2.77 us
    psum x4 -> x0, waiting for transfers between devices: 236 us -> none  [the longest x1 150 us: shards(): lax.psum((grad_latent, grad_gain_attn, grad_gain_latent, grad_gain_ffn, g...]
    dot_general x20 -> x6, matrix products: 214 us -> 22.6 us  [the longest x1 8.98 us: shards(): jnp.einsum('hqk,khd->qhd', dscore, keys, preferred_element_type=f32)]
    gather x4 -> x0, local copies, waits for them, and re-layouts: 138 us -> none  [the longest x1 41.5 us: shards(): jnp.concatenate([dweighted, jnp.zeros((1, width), jnp.bfloat16)], axis=0)]
    all_gather x6 -> x8, waiting for transfers between devices: 341 us -> 237 us  [the longest x1 60.6 us: shards(): small = lax.all_gather(small, BOTH, axis=0, tiled=True).astype(f32)]
  transfers between devices with their start and end apart: 19 -> 16, of which waited for: 18 -> 12; matrix products, arithmetic and copies ran while one was open for 10% -> 4% of each run, Pallas kernels for 0% -> 23%
where the time goes in v1:
time: 1390 us; the launch traced here: 1380 us
  waiting for transfers between devices  614 us (44%)
  Pallas kernels  491 us (35%)
  blocking collectives  91.5 us (7%)
  matrix products  62.8 us (5%)
  local copies, waits for them, and re-layouts  58 us (4%)
  other arithmetic  38.8 us (3%)
  between operations  16 us (1%)
    pallas_call x2, Pallas kernels, reduce_all(): pl.pallas_call(functools.partial(reduce_kernel, far), out_shape=jax.Shape...  208 us
    pallas_call x1, Pallas kernels, ffn_local(): pl.pallas_call(functools.partial(ffn_kernel, (experts, hidden, shared, to...  179 us
    reduce_scatter x1, waiting for transfers between devices, shards(): small = lax.psum_scatter(small, BOTH, scatter_dimension=0, tiled=True)  120 us
    pallas_call x1, Pallas kernels, gather_all(): pl.pallas_call(functools.partial(gather_kernel, far), out_shape=jax.Shape...  105 us
    reduce_scatter x1, waiting for transfers between devices, shards(): lax.psum_scatter(grad_query.astype(bf16), 'expert', scatter_dimension=0,...  75 us
    reduce_scatter x1, waiting for transfers between devices, shards(): lax.psum_scatter(grad_out.astype(bf16), 'expert', scatter_dimension=1, ti...  69.4 us
    all_gather x1, blocking collectives, shards(): picks_all = lax.all_gather(split(picks), BOTH, axis=1, tiled=True)  66.8 us
    all_gather x1, waiting for transfers between devices, shards(): small = lax.all_gather(small, BOTH, axis=0, tiled=True).astype(f32)  60.6 us
  transfers between devices with their start and end apart: 16, of which 12 were waited for; matrix products, arithmetic and copies ran while one was open for 4% of the time, Pallas kernels for 23%

profile of v1, /device:TPU:0, one launch (start us, length us, event | category | flops | bytes accessed | tf_op | source)
XLA Modules:
  0.0 1378.8 jit_solution(8937686741664613625)
XLA Ops:
  9.5 2.1 multiply_reduce_fusion.1
  11.6 3.2 fusion.58
  16.2 36.9 %all-gather.9.cloned.1.call-done = bf16[512,1024]{1,0:T(8,128)(2,1)} async-done(((bf16[64,1024]{1,0:T(8,128)(2,1)}), bf16[512,1024]{1,0:T(8,128)(2,1)}) %all-gather.9.cloned.1.call-update) | async-done | bytes 1048592 | tf_op jit(solution)/shard_map/all_gather | solution.py:562
  53.1 3.0 convolution_convert_fusion.6
  56.1 2.3 copy.121
  59.5 55.0 %all-gather.11.cloned.1.call-done = bf16[2048,768]{1,0:T(8,128)(2,1)} async-done(((bf16[256,768]{1,0:T(8,128)(2,1)}), bf16[2048,768]{1,0:T(8,128)(2,1)}) %all-gather.11.cloned.1.call-update) | async-done | bytes 3145744 | tf_op jit(solution)/shard_map/all_gather | solution.py:561
  114.5 3.8 fusion.57
  120.8 2.1 fusion.60
  123.0 2.0 copy-done.58
  125.4 40.8 %all-gather.13.cloned.1.call-done = bf16[512,2048]{1,0:T(8,128)(2,1)} async-done(((bf16[512,256]{1,0:T(8,128)(2,1)}), bf16[512,2048]{1,0:T(8,128)(2,1)}) %all-gather.13.cloned.1.call-update) | async-done | bytes 2097168 | tf_op jit(solution)/shard_map/all_gather | solution.py:563
  166.3 4.2 convolution_convert_fusion.3
  170.5 2.5 convert_element_type.140
  173.9 26.4 %reduce-scatter.10.cloned.1.call-done = bf16[128,2048]{1,0:T(8,128)(2,1)} async-done(((bf16[512,2048]{1,0:T(8,128)(2,1)}), bf16[128,2048]{1,0:T(8,128)(2,1)}) %reduce-scatter.10.cloned.1.call-update) | async-done | bytes 524304 | tf_op jit(solution)/shard_map/reduce_scatter | solution.py:627
  200.3 2.6 multiply_reduce_fusion.6
  203.1 1.2 pad_maximum_fusion
  204.3 5.6 all-to-all-start
  210.0 66.8 %all_gather.31 = f32[1,4096,16]{1,2,0:T(8,128)S(1)} all-gather(f32[1,128,16]{1,2,0:T(8,128)S(1)} %bitcast_select_fusion), channel_id=1, replica_groups=mesh['expert'=8,'tensor'=4] {'expert','tensor'}, dimensions={1}, use_global_device_ids=true | all-gather | bytes 270336 | tf_op jit(solution)/shard_map/all_gather | solution.py:587
  278.3 1.2 copy.124
  280.4 104.6 %shard_map.297 = bf16[32,128,2048]{2,1,0:T(8,128)(2,1)} custom-call(bf16[128,2048]{1,0:T(8,128)(2,1)} %multiply_convert_fusion.4.x_ref), custom_call_target="tpu_custom_call" | custom-call | tf_op jit(solution)/shard_map/pallas_call | solution.py:205
  385.0 179.1 %shard_map.298 = (bf16[4096,2048]{1,0:T(8,128)(2,1)}, bf16[4096,2048]{1,0:T(8,128)(2,1)}, f32[8,4096]{1,0:T(8,128)}, f32[2,352,2048]{2,1,0:T(8,128)}, f32[2,352,...) custom-call(bf16[4096,2048]{1,0:T(8,128)(2,1)} %bitcast.95, ...), custom_call_target="tpu_custom_call" | custom-call | flops 120795955200 | bytes 67108864 | tf_op jit(solution)/shard_map/pallas_call | solution.py:476
  566.2 118.7 %shard_map.300 = f32[128,2048]{1,0:T(8,128)} custom-call(bf16[32,128,2048]{2,1,0:T(8,128)(2,1)} %bitcast.94), custom_call_target="tpu_custom_call" | custom-call | tf_op jit(solution)/shard_map/pallas_call | solution.py:337
  684.9 89.0 %shard_map.299 = f32[128,2048]{1,0:T(8,128)} custom-call(bf16[32,128,2048]{2,1,0:T(8,128)(2,1)} %bitcast.93), custom_call_target="tpu_custom_call" | custom-call | tf_op jit(solution)/shard_map/pallas_call | solution.py:337
  776.0 2.9 multiply_convert_fusion.3
  779.2 22.1 %all-gather.19.cloned.1.call-done = bf16[512,2048]{1,0:T(8,128)(2,1)} async-done(((bf16[128,2048]{1,0:T(8,128)(2,1)}), bf16[512,2048]{1,0:T(8,128)(2,1)}) %all-gather.19.cloned.1.call-update) | async-done | bytes 2097168 | tf_op jit(solution)/shard_map/all_gather | solution.py:673
  801.2 3.6 convolution_convert_fusion.7
  806.1 2.8 fusion.35
  808.9 8.7 fusion.20
  817.6 1.3 slice.182
  820.1 9.0 fusion.17
  829.1 1.4 slice.183
  833.4 1.7 copy-done.54
  835.1 1.8 fusion.62
  837.0 3.3 add_convert_fusion
  840.6 1.2 copy-done.6
  841.9 2.4 broadcast_multiply_fusion
  844.5 3.0 convolution_convert_fusion.1
  847.4 24.5 %reduce-scatter.14.cloned.1.call-done = bf16[128,2048]{1,0:T(8,128)(2,1)} async-done(((bf16[512,2048]{1,0:T(8,128)(2,1)}), bf16[128,2048]{1,0:T(8,128)(2,1)}) %reduce-scatter.14.cloned.1.call-update) | async-done | bytes 524304 | tf_op jit(solution)/shard_map/reduce_scatter | solution.py:706
  871.9 1.7 fusion.31
  873.6 11.8 concatenate.47
  885.4 4.4 copy.122
  889.8 3.5 pad.23.clone
  893.9 3.3 convolution_convert_fusion.5
  897.3 4.3 convolution_convert_fusion.2
  901.7 4.8 convolution_convert_fusion
  907.9 2.7 fusion.29
  910.7 120.3 %reduce-scatter.22.cloned.1.call-done = bf16[64,640]{1,0:T(8,128)(2,1)} async-done(((bf16[2048,640]{1,0:T(8,128)(2,1)}), bf16[64,640]{1,0:T(8,128)(2,1)}) %reduce-scatter.22.cloned.1.call-update) | async-done | bytes 81936 | tf_op jit(solution)/shard_map/reduce_scatter | solution.py:725
  1031.1 1.8 slice.181
  1032.9 24.7 %all_to_all.10 = bf16[8,3,88,256]{3,2,1,0:T(8,128)(2,1)S(1)} all-to-all(bf16[8,3,88,256]{3,2,1,0:T(8,128)(2,1)S(1)} %bitcast.99), channel_id=1, replica_groups=mesh['expert'=8,'tensor'=4] {'expert'}, dimensions={0} | all-to-all | bytes 2162688 | tf_op jit(solution)/shard_map/all_to_all | solution.py:660
  1060.5 58.0 %reduce-scatter.18.cloned.1.call-done = bf16[64,1024]{1,0:T(8,128)(2,1)} async-done(((bf16[512,1024]{1,0:T(8,128)(2,1)}), bf16[64,1024]{1,0:T(8,128)(2,1)}) %reduce-scatter.18.cloned.1.call-update) | async-done | bytes 131088 | tf_op jit(solution)/shard_map/reduce_scatter | solution.py:737
  1118.4 1.6 convert_element_type.168
  1120.1 69.4 %reduce-scatter.20.cloned.1.call-done = bf16[512,256]{1,0:T(8,128)(2,1)} async-done(((bf16[512,2048]{1,0:T(8,128)(2,1)}), bf16[512,256]{1,0:T(8,128)(2,1)}) %reduce-scatter.20.cloned.1.call-update) | async-done | bytes 262160 | tf_op jit(solution)/shard_map/reduce_scatter | solution.py:740
  1189.5 1.8 convert_element_type.170
  1191.3 75.0 %reduce-scatter.16.cloned.1.call-done = bf16[256,768]{1,0:T(8,128)(2,1)} async-done(((bf16[2048,768]{1,0:T(8,128)(2,1)}), bf16[256,768]{1,0:T(8,128)(2,1)}) %reduce-scatter.16.cloned.1.call-update) | async-done | bytes 393232 | tf_op jit(solution)/shard_map/reduce_scatter | solution.py:734
  1266.3 1.9 convert_element_type.166
  1268.2 21.8 %all-gather.21.cloned.1.call-done = bf16[512,2048]{1,0:T(8,128)(2,1)} async-done(((bf16[128,2048]{1,0:T(8,128)(2,1)}), bf16[512,2048]{1,0:T(8,128)(2,1)}) %all-gather.21.cloned.1.call-update) | async-done | bytes 2097168 | tf_op jit(solution)/shard_map/all_gather | solution.py:712
  1290.0 60.6 %all-gather.23.cloned.1.call-done = bf16[2048,640]{1,0:T(8,128)(2,1)} async-done(((bf16[64,640]{1,0:T(8,128)(2,1)}), bf16[2048,640]{1,0:T(8,128)(2,1)}) %all-gather.23.cloned.1.call-update) | async-done | bytes 2621456 | tf_op jit(solution)/shard_map/all_gather | solution.py:726
  1350.7 2.2 convert_element_type.164
  1352.9 1.8 slice_reduce_fusion
  1355.5 2.7 slice.132
  1358.1 5.7 copy.110
  1363.8 1.2 slice.135
  1365.0 2.2 copy.111
  1367.2 3.3 copy.131
  1370.5 1.3 copy.132
  (209 shorter events, 26.2 us)
Async XLA Ops:
  7.2 202.8 %copy-start = (s32[512,6]{0,1:T(8,128)S(1)}, s32[512,6]{0,1:T(8,128)}, u32[]{:S(2)}) copy-start(s32[512,6]{0,1:T(8,128)} %param.20) | copy-start | bytes 36868
  7.2 4.4 copy-start.5
  7.2 4.4 copy-start.44
  7.2 45.8 %all-gather.9.cloned.1.call-start = ((), (), s32[]{:S(2)}) async-start(), calls=%async_computation.9 | async-start | bytes 1179648 | tf_op jit(solution)/shard_map/all_gather | solution.py:562
  8.0 106.5 %all-gather.11.cloned.1.call-start = ((), (), s32[]{:S(2)}) async-start(), calls=%async_computation.10 | async-start | bytes 3538944 | tf_op jit(solution)/shard_map/all_gather | solution.py:561
  8.7 157.6 %all-gather.13.cloned.1.call-start = ((), (), s32[]{:S(2)}) async-start(), calls=%async_computation.11 | async-start | bytes 2359296 | tf_op jit(solution)/shard_map/all_gather | solution.py:563
  9.4 190.8 %reduce-scatter.10.cloned.1.call-start = ((), (), s32[]{:S(2)}) async-start(), calls=%async_computation.12 | async-start | bytes 2621440 | tf_op jit(solution)/shard_map/reduce_scatter | solution.py:627
  9.5 5.3 copy-start.52
  11.6 102.9 %copy-start.48 = (f32[512]{0:T(512)}, f32[512]{0:T(512)S(1)}, u32[]{:S(2)}) copy-start(f32[512]{0:T(512)S(1)} %add_rsqrt_fusion.1) | copy-start | bytes 6148
  11.6 41.4 %copy-start.50 = (f32[512]{0:T(512)S(1)}, f32[512]{0:T(512)}, u32[]{:S(2)}) copy-start(f32[512]{0:T(512)} %param.24) | copy-start | bytes 6148
  14.8 41.3 %copy-start.9 = (f32[512,576]{0,1:T(8,128)}, f32[512,576]{0,1:T(8,128)S(1)}, u32[]{:S(2)}) copy-start(f32[512,576]{0,1:T(8,128)S(1)} %fusion.58) | copy-start | bytes 3538948
  15.2 103.2 %copy-start.28 = (f32[512,32]{0,1:T(8,128)}, f32[512,32]{0,1:T(8,128)S(1)}, u32[]{:S(2)}) copy-start(f32[512,32]{0,1:T(8,128)S(1)} %get-tuple-element.102) | copy-start | bytes 196612
  15.2 103.2 %copy-start.30 = (f32[512,32]{0,1:T(8,128)}, f32[512,32]{0,1:T(8,128)S(1)}, u32[]{:S(2)}) copy-start(f32[512,32]{0,1:T(8,128)S(1)} %get-tuple-element.103) | copy-start | bytes 196612
  16.2 42.2 %copy-start.46 = (f32[512]{0:T(512)}, f32[512]{0:T(512)S(1)}, u32[]{:S(2)}) copy-start(f32[512]{0:T(512)S(1)} %add_rsqrt_fusion) | copy-start | bytes 6148
  59.5 59.1 %copy-start.20 = (bf16[512,4,128]{0,2,1:T(8,128)(2,1)}, bf16[512,4,128]{0,2,1:T(8,128)(2,1)S(1)}, u32[]{:S(2)}) copy-start(bf16[512,4,128]{0,2,1:T(8,128)(2,1)S(1)} %slice.121) | copy-start | bytes 1572868
  118.5 2.2 copy-start.33
  118.5 2.2 copy-start.35
  120.8 4.1 copy-start.14
  125.4 45.0 %copy-start.57 = (bf16[4,128,512]{2,1,0:T(8,128)(2,1)}, bf16[4,128,512]{2,1,0:T(8,128)(2,1)S(1)}, u32[]{:S(2)}) copy-start(bf16[4,128,512]{2,1,0:T(8,128)(2,1)S(1)} %convolution_convert_fusion.9) | copy-start | bytes 1572868
  170.5 214.6 %all-gather.15.cloned.1.call-start = ((), (), s32[]{:S(2)}) async-start(), calls=%async_computation.13 | async-start | bytes 17301504 | tf_op jit(solution)/shard_map/all_gather | solution.py:589
  173.1 29.9 %copy-start.39 = (bf16[256,704]{0,1:T(8,128)(2,1)S(1)}, bf16[256,704]{0,1:T(8,128)(2,1)}, u32[]{:S(2)}) copy-start(bf16[256,704]{0,1:T(8,128)(2,1)} %param.29) | copy-start | bytes 1081348
  173.9 29.1 %copy-start.40 = (bf16[704,256]{1,0:T(8,128)(2,1)S(1)}, bf16[704,256]{1,0:T(8,128)(2,1)}, u32[]{:S(2)}) copy-start(bf16[704,256]{1,0:T(8,128)(2,1)} %param.31) | copy-start | bytes 1081348
  173.9 29.1 %copy-start.41 = (bf16[256,704]{0,1:T(8,128)(2,1)S(1)}, bf16[256,704]{0,1:T(8,128)(2,1)}, u32[]{:S(2)}) copy-start(bf16[256,704]{0,1:T(8,128)(2,1)} %param.30) | copy-start | bytes 1081348
  202.9 76.5 %copy-start.3 = (f32[128,2048]{1,0:T(8,128)}, f32[128,2048]{1,0:T(8,128)S(1)}, u32[]{:S(2)}) copy-start(f32[128,2048]{1,0:T(8,128)S(1)} %get-tuple-element.87) | copy-start | bytes 3145732
  203.1 73.8 %copy-start.32 = (bf16[2048,16]{0,1:T(8,128)(2,1)S(1)}, bf16[2048,16]{0,1:T(8,128)(2,1)}, u32[]{:S(2)}) copy-start(bf16[2048,16]{0,1:T(8,128)(2,1)} %param.28) | copy-start | bytes 196612
  204.3 75.2 %copy-start.43 = (f32[2048]{0:T(1024)S(1)}, f32[2048]{0:T(1024)}, u32[]{:S(2)}) copy-start(f32[2048]{0:T(1024)} %param.27) | copy-start | bytes 24580
  204.3 74.0 %all-to-all-start = ((bf16[8,3,96,256]{3,2,1,0:T(8,128)(2,1)}), bf16[8,3,96,256]{3,2,1,0:T(8,128)(2,1)S(1)}, u32[]{:S(2)}, u32[]{:S(2)}) async-start(bf16[8,3,96,256]{3,2,1,0:T(8,128)(2,1)} %pad_maximum_fusion), calls=%async_computation.1 | async-start | bytes 2359296 | tf_op jit(solution)/shard_map/all_to_all | solution.py:575
  209.9 564.0 %reduce-scatter.12.cloned.1.call-start = ((), (), s32[]{:S(2)}) async-start(), calls=%async_computation.15 | async-start | bytes 270336 | tf_op jit(solution)/shard_map/reduce_scatter | solution.py:647
  385.0 180.9 %copy-start.11 = (bf16[128,2048]{1,0:T(8,128)(2,1)S(1)}, bf16[128,2048]{1,0:T(8,128)(2,1)}, u32[]{:S(2)}) copy-start(bf16[128,2048]{1,0:T(8,128)(2,1)} %multiply_convert_fusion.4.x_ref) | copy-start | bytes 1572868
  565.8 235.4 %all-gather.19.cloned.1.call-start = ((), (), s32[]{:S(2)}) async-start(), calls=%async_computation.16 | async-start | bytes 2621440 | tf_op jit(solution)/shard_map/all_gather | solution.py:673
  684.9 90.6 %copy-start.4 = (f32[128,2048]{1,0:T(8,128)S(1)}, f32[128,2048]{1,0:T(8,128)}, u32[]{:S(2)}) copy-start(f32[128,2048]{1,0:T(8,128)} %copy-done.3) | copy-start | bytes 3145732
  684.9 90.6 %copy-start.13 = (f32[128,2048]{1,0:T(8,128)S(1)}, f32[128,2048]{1,0:T(8,128)}, u32[]{:S(2)}) copy-start(f32[128,2048]{1,0:T(8,128)} %shard_map.300) | copy-start | bytes 3145732
  776.0 2.9 copy-start.7
  778.9 26.0 %copy-start.61 = (f32[4,512]{1,0:T(4,128)S(1)}, f32[4,512]{1,0:T(4,128)}, u32[]{:S(2)}) copy-start(f32[4,512]{1,0:T(4,128)} %copy-done.60) | copy-start | bytes 24580
  778.9 93.0 %reduce-scatter.14.cloned.1.call-start = ((), (), s32[]{:S(2)}) async-start(), calls=%async_computation.17 | async-start | bytes 2621440 | tf_op jit(solution)/shard_map/reduce_scatter | solution.py:706
  801.2 3.7 copy-start.59
  806.1 2.8 copy-start.23
  806.1 2.8 copy-start.34
  806.1 2.8 copy-start.36
  808.9 11.1 copy-start.21
  808.9 11.1 copy-start.25
  820.1 10.5 copy-start.29
  820.1 10.5 copy-start.31
  829.1 2.7 copy-start.10
  829.1 2.7 copy-start.47
  829.1 2.7 copy-start.51
  829.1 2.7 copy-start.56
  832.7 2.4 copy-start.54
  833.3 3.7 copy-start.37
  833.3 3.6 copy-start.27
  836.9 3.7 copy-start.49
  840.3 4.1 copy-start.45
  840.3 190.7 %reduce-scatter.22.cloned.1.call-start = ((), (), s32[]{:S(2)}) async-start(), calls=%async_computation.23 | async-start | bytes 2703360 | tf_op jit(solution)/shard_map/reduce_scatter | solution.py:725
  841.9 2.4 copy-start.12
  841.9 2.6 copy-start.38
  893.3 167.2 %all-gather.17.cloned.1.call-start = ((), (), s32[]{:S(2)}) async-start(), calls=%async_computation.14 | async-start | bytes 2621440 | tf_op jit(solution)/shard_map/all_gather | solution.py:654
  893.9 224.5 %reduce-scatter.18.cloned.1.call-start = ((), (), s32[]{:S(2)}) async-start(), calls=%async_computation.21 | async-start | bytes 1179648 | tf_op jit(solution)/shard_map/reduce_scatter | solution.py:737
  897.3 292.2 %reduce-scatter.20.cloned.1.call-start = ((), (), s32[]{:S(2)}) async-start(), calls=%async_computation.22 | async-start | bytes 2359296 | tf_op jit(solution)/shard_map/reduce_scatter | solution.py:740
  901.7 364.6 %reduce-scatter.16.cloned.1.call-start = ((), (), s32[]{:S(2)}) async-start(), calls=%async_computation.20 | async-start | bytes 3538944 | tf_op jit(solution)/shard_map/reduce_scatter | solution.py:734
  906.6 383.4 %all-gather.21.cloned.1.call-start = ((), (), s32[]{:S(2)}) async-start(), calls=%async_computation.18 | async-start | bytes 2621440 | tf_op jit(solution)/shard_map/all_gather | solution.py:712
  910.7 440.0 %all-gather.23.cloned.1.call-start = ((), (), s32[]{:S(2)}) async-start(), calls=%async_computation.19 | async-start | bytes 2703360 | tf_op jit(solution)/shard_map/all_gather | solution.py:726
  1350.7 4.8 copy-start.2
  1367.2 3.3 copy-start.18
  1367.2 4.6 copy-start.1
  (14 other events, 18.4 us)
Sparse Core Ops, SparseCore 0:
  10.2 42.8 all-gather.8
  55.2 59.1 all-gather.10
  116.5 49.6 all-gather.12
  170.6 29.6 reduce-scatter.9
  203.9 173.5 all-gather.14
  566.0 162.1 reduce-scatter.11
  779.0 22.1 all-gather.18
  840.4 31.4 reduce-scatter.13
  893.4 137.5 reduce-scatter.21
  1032.5 18.5 all-gather.16
  1054.9 63.4 reduce-scatter.17
  1122.4 67.0 reduce-scatter.19
  1193.1 73.1 reduce-scatter.15
  1268.3 21.6 all-gather.20
  1292.7 57.9 all-gather.22

commit v2 on v0

v2 whole, which is shorter than its diff:
```python
import functools

import jax
import jax.numpy as jnp
from jax import lax
from jax.experimental import pallas as pl
from jax.experimental.pallas import tpu as pltpu
from jax.sharding import PartitionSpec as P

F32, BF16 = jnp.float32, jnp.bfloat16

NOPE = 128
ROPE = 64
VD = 128
KVR = 512


EPS = 1e-06
ROPE_BASE = 10000.0


def inv_rms(v):
    return lax.rsqrt(jnp.mean(v * v, axis=-1, keepdims=True) + EPS)


def rope_tables(count, width):
    half = width // 2
    freq = ROPE_BASE ** (-(jnp.arange(half, dtype=jnp.float32) * 2.0 / width))
    angle = jnp.arange(count, dtype=jnp.float32)[:, None] * freq[None, :]
    return (jnp.cos(angle), jnp.sin(angle))


def rotate(v, cosine, sine):
    half = v.shape[-1] // 2
    first = v[..., :half]
    second = v[..., half:]
    return jnp.concatenate(
        [first * cosine - second * sine, second * cosine + first * sine], axis=-1
    )


def rotate_back(grad, cosine, sine):
    half = grad.shape[-1] // 2
    first = grad[..., :half]
    second = grad[..., half:]
    return jnp.concatenate(
        [first * cosine + second * sine, second * cosine - first * sine], axis=-1
    )


def norm_back(grad, normed, scale_row, gain):
    weighted = grad * gain
    return scale_row * (weighted - normed * jnp.mean(weighted * normed, axis=-1, keepdims=True))


def silu_parts(gate):
    sig = jax.nn.sigmoid(gate)
    return (gate * sig, sig * (1.0 + gate * (1.0 - sig)))


def mat(left, right):
    return jnp.dot(left, right, preferred_element_type=jnp.float32)


def mat_tn(left, right):
    return lax.dot_general(
        left, right, (((0,), (0,)), ((), ())), preferred_element_type=jnp.float32
    )


def mat_nt(left, right):
    return lax.dot_general(
        left, right, (((1,), (1,)), ((), ())), preferred_element_type=jnp.float32
    )


MESH = pl.DeviceIdType.MESH
ANY = pl.BlockSpec(memory_space=pl.ANY)
IN_VMEM = pl.BlockSpec(memory_space=pltpu.VMEM)


def places():
    e, t = lax.axis_index("expert"), lax.axis_index("tensor")
    return e // 2, e % 2, t // 2, t % 2


class Net:
    def __init__(self, far, send, recv, local):
        self.far, self.send, self.recv, self.local = far, send, recv, local
        self.e1, self.e0, self.t1, self.t0 = places()
        self.count, self.started, self.locals = 0, [], 0
        self.core = self.at(d=1)
        self.x = self.at(c=1)
        self.y = self.at(b=1)

    def at(self, r=0, b=0, c=0, d=0):
        e = (self.e1 + r + self.far) % self.far * 2 + (self.e0 + b) % 2
        return (e, (self.t1 + c) % 2 * 2 + (self.t0 + d) % 2)

    def slot(self, r=0, b=0, c=0, d=0):
        e, t = self.at(r, b, c, d)
        return e * 4 + t

    def group(self, r=0, b=0):
        return self.at(r, b)[0]

    def greet(self, peers):
        barrier = pltpu.get_barrier_semaphore()
        for peer in peers:
            pl.semaphore_signal(barrier, inc=1, device_id=peer, device_id_type=MESH)
        pl.semaphore_wait(barrier, len(peers))

    def near(self):
        return [self.at(r) for r in range(1, self.far)] + [self.y, self.x, self.core]

    def line(self):
        every = [self.at(r, b) for r in range(self.far) for b in range(2)]
        return every[1:]

    def push(self, src, dst, to):
        k = self.count
        self.count += 1
        copy = pltpu.make_async_remote_copy(
            src_ref=src,
            dst_ref=dst,
            send_sem=self.send.at[k],
            recv_sem=self.recv.at[k],
            device_id=to,
            device_id_type=MESH,
        )
        copy.start()
        self.started.append(copy)
        return k

    def arrived(self, ref, k):
        pltpu.make_async_copy(ref, ref, self.recv.at[k]).wait()

    def load(self, src, dst):
        copy = pltpu.make_async_copy(src, dst, self.local.at[self.locals])
        self.locals += 1
        copy.start()
        return copy

    def finish(self):
        for copy in self.started:
            copy.wait_send()


def add_rows(dst, src, step=16):
    @pl.loop(0, dst.shape[0] // step)
    def _(i):
        rows = pl.ds(pl.multiple_of(i * step, step), step)
        dst[rows, :] = dst[rows, :] + src[rows, :]


class GatherAll:
    def __init__(self, net, own, out_at, order):
        self.net, self.own, self.out_at, self.order = net, own, out_at, order
        self.z, self.first, self.second, self.cores = {}, {}, {}, {}

    def place(self, r, u, v, d=0):
        b, c = (u, v) if self.order == "yx" else (v, u)
        return self.out_at(self.net.slot(-r, b, c, d))

    def pass_on(self, r, u, v, to):
        here = self.own if (r, u, v) == (0, 0, 0) else self.place(r, u, v)
        return self.net.push(here, self.place(r, u, v), to)

    def start(self):
        for r in range(1, self.net.far):
            self.z[r] = self.pass_on(0, 0, 0, self.net.at(r))
        self.links = (self.net.y, self.net.x)[:: 1 if self.order == "yx" else -1]

    def stage_a(self, r):
        if r:
            self.net.arrived(self.place(r, 0, 0), self.z[r])
        self.first[r] = self.pass_on(r, 0, 0, self.links[0])
        self.second[r, 0] = self.pass_on(r, 0, 0, self.links[1])
        self.cores[r, 0, 0] = self.pass_on(r, 0, 0, self.net.core)

    def stage_b(self, r):
        self.net.arrived(self.place(r, 1, 0), self.first[r])
        self.second[r, 1] = self.pass_on(r, 1, 0, self.links[1])
        self.cores[r, 1, 0] = self.pass_on(r, 1, 0, self.net.core)

    def stage_c(self, r):
        for u in range(2):
            self.net.arrived(self.place(r, u, 1), self.second[r, u])
            self.cores[r, u, 1] = self.pass_on(r, u, 1, self.net.core)

    def steps(self):
        return [self.stage_a, self.stage_b, self.stage_c]

    def end(self):
        for (r, u, v), k in self.cores.items():
            self.net.arrived(self.place(r, u, v, 1), k)


class ReduceAll:
    def __init__(self, net, part_at, acc, from_core, from_first, from_second, from_z, order):
        self.net, self.part_at, self.acc, self.order = net, part_at, acc, order
        self.bufs = (from_core, from_first, from_second, from_z)
        self.core, self.first, self.second, self.z, self.loads = {}, {}, {}, {}, {}
        self.turn = list(range(net.far - 1, -1, -1))
        self.spots = ((1, 1), (0, 1), (1, 0), (0, 0))
        self.links = (net.x, net.y) if order == "xy" else (net.y, net.x)

    def dest(self, r, u, v, d):
        b, c = (v, u) if self.order == "xy" else (u, v)
        return self.part_at(self.net.slot(r, b, c, d))

    def load(self):
        for r in self.turn:
            for u, v in self.spots:
                k = r * 4 + u * 2 + v
                self.loads[k] = self.net.load(self.dest(r, u, v, 0), self.acc.at[k])

    def start(self):
        for r in self.turn:
            for u, v in self.spots:
                k = r * 4 + u * 2 + v
                self.core[k] = self.net.push(
                    self.dest(r, u, v, 1), self.bufs[0].at[k], self.net.core
                )

    def merge(self, k, buf, i, token):
        self.net.arrived(buf.at[i], token)
        add_rows(self.acc.at[k], buf.at[i])

    def stage_a(self, i):
        r = self.turn[i]
        for u, v in self.spots:
            k = r * 4 + u * 2 + v
            self.loads[k].wait()
            self.merge(k, self.bufs[0], k, self.core[k])
            if u:
                at = r * 2 + v
                self.first[at] = self.net.push(
                    self.acc.at[k], self.bufs[1].at[at], self.links[0]
                )

    def stage_b(self, i):
        r = self.turn[i]
        for v in (1, 0):
            at = r * 2 + v
            self.merge(r * 4 + v, self.bufs[1], at, self.first[at])
            if v:
                self.second[r] = self.net.push(
                    self.acc.at[r * 4 + v], self.bufs[2].at[r], self.links[1]
                )

    def stage_c(self, i):
        r = self.turn[i]
        self.merge(r * 4, self.bufs[2], r, self.second[r])
        if r:
            self.z[r] = self.net.push(
                self.acc.at[r * 4], self.bufs[3].at[r - 1], self.net.at(r)
            )

    def steps(self):
        return [self.stage_a, self.stage_b, self.stage_c]

    def end(self):
        for r in range(1, self.net.far):
            self.net.arrived(self.bufs[3].at[r - 1], self.z[r])

    def total(self, rows):
        total = self.acc[0, rows, :].astype(F32)
        for r in range(1, self.net.far):
            total = total + self.bufs[3][r - 1, rows, :].astype(F32)
        return total

    @staticmethod
    def scratch(far, rows, width):
        return [
            pltpu.VMEM((4 * far, rows, width), BF16),
            pltpu.VMEM((4 * far, rows, width), BF16),
            pltpu.VMEM((2 * far, rows, width), BF16),
            pltpu.VMEM((far, rows, width), BF16),
            pltpu.VMEM((far - 1, rows, width), BF16),
        ]


def pipelined(far, parts):
    for i in range(far + 2):
        for s in range(3):
            for part in parts:
                if 0 <= i - s < far:
                    part.steps()[s](i - s)


def semaphores(remote, local):
    return [
        pltpu.SemaphoreType.DMA((remote,)),
        pltpu.SemaphoreType.DMA((remote,)),
        pltpu.SemaphoreType.DMA((local,)),
    ]


def cost(us):
    return pl.CostEstimate(flops=0, bytes_accessed=us * 3_000_000, transcendentals=0)


def params(ident, mib=60):
    return pltpu.CompilerParams(
        collective_id=ident, has_side_effects=True, vmem_limit_bytes=mib * 2**20
    )


def begin_kernel(far, *refs):
    n = 3
    ws, blocks, marks = refs[:n], refs[n], refs[n + 1]
    outs, blocks_out, marks_out = refs[n + 2 : 2 * n + 2], refs[2 * n + 2], refs[2 * n + 3]
    net = Net(far, *refs[2 * n + 4 :])
    me = net.group()
    mine = [net.load(w, o.at[me]) for w, o in zip(ws, outs)]
    mine.append(net.load(blocks.at[me], blocks_out.at[me]))
    mine.append(net.load(marks, marks_out.at[me]))
    net.greet(net.line())
    tokens = {}
    others = [(r, b) for r in range(far) for b in range(2)][1:]
    for a, (w, o) in enumerate(zip(ws, outs)):
        for r in range(1, far):
            tokens[a, r] = net.push(w, o.at[me], net.at(r))
        tokens[a, 0, 1] = net.push(w, o.at[me], net.y)
    small = []
    for r, b in others:
        small.append((r, b, marks_out, net.push(marks, marks_out.at[me], net.at(r, b))))
    for a, (w, o) in enumerate(zip(ws, outs)):
        for r in range(1, far):
            place = o.at[net.group(-r)]
            net.arrived(place, tokens[a, r])
            tokens[a, r, 1] = net.push(place, place, net.y)
    for r, b in others:
        to = net.at(r, b)
        small.append((r, b, blocks_out, net.push(blocks.at[to[0]], blocks_out.at[me], to)))
    for a, o in enumerate(outs):
        for r in range(far):
            net.arrived(o.at[net.group(-r, 1)], tokens[a, r, 1])
    for r, b, ref, k in small:
        net.arrived(ref.at[net.group(-r, b)], k)
    net.finish()
    for copy in mine:
        copy.wait()


def begin(ws, blocks, marks, groups, ident):
    far = groups // 2
    outs = [jax.ShapeDtypeStruct((groups, *w.shape), w.dtype) for w in ws]
    outs.append(jax.ShapeDtypeStruct(blocks.shape, blocks.dtype))
    outs.append(jax.ShapeDtypeStruct((groups, *marks.shape), marks.dtype))
    return pl.pallas_call(
        functools.partial(begin_kernel, far),
        out_shape=outs,
        in_specs=[ANY] * 5,
        out_specs=[ANY] * 5,
        scratch_shapes=semaphores(10 * far, 5),
        compiler_params=params(ident),
        cost_estimate=cost(100),
    )(*ws, blocks, marks)


class ReduceGroups:
    def __init__(self, net, part, out, acc, from_y, from_z):
        self.net, self.part, self.out = net, part, out
        self.acc, self.from_y, self.from_z = acc, from_y, from_z
        self.turn = list(range(net.far - 1, -1, -1))

    def load(self):
        self.loads = {
            r: self.net.load(self.part.at[self.net.group(r)], self.acc.at[r]) for r in self.turn
        }

    def start(self):
        self.y = {
            r: self.net.push(self.part.at[self.net.group(r, 1)], self.from_y.at[r], self.net.y)
            for r in self.turn
        }
        self.z = {}

    def step(self, i):
        r = self.turn[i]
        self.loads[r].wait()
        self.net.arrived(self.from_y.at[r], self.y[r])
        add_rows(self.acc.at[r], self.from_y.at[r])
        if r:
            self.z[r] = self.net.push(self.acc.at[r], self.from_z.at[r - 1], self.net.at(r))

    def end(self):
        for r in range(1, self.net.far):
            self.net.arrived(self.from_z.at[r - 1], self.z[r])

        @pl.loop(0, self.out.shape[0] // 16)
        def _(i):
            rows = pl.ds(pl.multiple_of(i * 16, 16), 16)
            total = self.acc[0, rows, :].astype(F32)
            for r in range(1, self.net.far):
                total = total + self.from_z[r - 1, rows, :].astype(F32)
            self.out[rows, :] = total

    @staticmethod
    def scratch(far, rows, width):
        return [
            pltpu.VMEM((far, rows, width), BF16),
            pltpu.VMEM((far, rows, width), BF16),
            pltpu.VMEM((far - 1, rows, width), BF16),
        ]


class GatherTensor:
    def __init__(self, net, own, out):
        self.net, self.own, self.out = net, own, out

    def place(self, c, d):
        return self.out.at[self.net.at(0, 0, c, d)[1]]

    def start(self):
        net = self.net
        self.mine = net.load(self.own, self.place(0, 0))
        self.x = net.push(self.own, self.place(0, 0), net.x)
        self.c0 = net.push(self.own, self.place(0, 0), net.core)

    def step(self):
        self.net.arrived(self.place(1, 0), self.x)
        self.c1 = self.net.push(self.place(1, 0), self.place(1, 0), self.net.core)

    def end(self):
        self.net.arrived(self.place(0, 1), self.c0)
        self.net.arrived(self.place(1, 1), self.c1)
        self.mine.wait()


class ReduceTensor:
    def __init__(self, net, part, acc, from_core, from_x):
        self.net, self.part = net, part
        self.acc, self.from_core, self.from_x = acc, from_core, from_x

    def at(self, c, d):
        return self.part.at[self.net.at(0, 0, c, d)[1]]

    def load(self):
        self.loads = [self.net.load(self.at(c, 0), self.acc.at[c]) for c in (1, 0)]

    def start(self):
        self.core = [
            self.net.push(self.at(c, 1), self.from_core.at[c], self.net.core) for c in (1, 0)
        ]

    def step(self):
        for i, c in enumerate((1, 0)):
            self.loads[i].wait()
            self.net.arrived(self.from_core.at[c], self.core[i])
            add_rows(self.acc.at[c], self.from_core.at[c])
            if c:
                self.x = self.net.push(self.acc.at[c], self.from_x, self.net.x)

    def end(self):
        self.net.arrived(self.from_x, self.x)

    def total(self, rows):
        return self.acc[0, rows, :].astype(F32) + self.from_x[rows, :].astype(F32)

    @staticmethod
    def scratch(rows, width):
        return [
            pltpu.VMEM((2, rows, width), BF16),
            pltpu.VMEM((2, rows, width), BF16),
            pltpu.VMEM((rows, width), BF16),
        ]


def sum_tensor_kernel(far, part, out, *scratch):
    net = Net(far, *scratch[-3:])
    rows_back = ReduceTensor(net, part, *scratch[:3])
    rows_back.load()
    net.greet([net.x, net.core])
    rows_back.start()
    rows_back.step()
    rows_back.end()

    @pl.loop(0, out.shape[0] // 16)
    def _(i):
        rows = pl.ds(pl.multiple_of(i * 16, 16), 16)
        out[rows, :] = rows_back.total(rows)

    net.finish()


def sum_tensor(part, groups, ident):
    _, m, width = part.shape
    return pl.pallas_call(
        functools.partial(sum_tensor_kernel, groups // 2),
        out_shape=jax.ShapeDtypeStruct((m, width), F32),
        in_specs=[ANY],
        out_specs=IN_VMEM,
        scratch_shapes=ReduceTensor.scratch(m, width) + semaphores(3, 2),
        compiler_params=params(ident, 16),
        cost_estimate=cost(16),
    )(part)


def gather_tensor_kernel(far, own, out, *scratch):
    net = Net(far, *scratch)
    give = GatherTensor(net, own, out)
    net.greet([net.x, net.core])
    give.start()
    give.step()
    give.end()
    net.finish()


def gather_tensor(own, groups, tensors, ident):
    m, width = own.shape
    return pl.pallas_call(
        functools.partial(gather_tensor_kernel, groups // 2),
        out_shape=jax.ShapeDtypeStruct((tensors, m, width), own.dtype),
        in_specs=[ANY],
        out_specs=ANY,
        scratch_shapes=semaphores(3, 1),
        compiler_params=params(ident, 16),
        cost_estimate=cost(16),
    )(own)


def finish_kernel(far, *refs):
    (gq, gkv, gout, small, blocks, dxn, dresid, normed, scale, gain) = refs[:10]
    (oq, okv, oout, osmall, oblocks, otokens) = refs[10:16]
    scratch = list(refs[16:])
    net = Net(far, *scratch[-3:])

    def take(n):
        got = scratch[:n]
        del scratch[:n]
        return got

    weights = [ReduceGroups(net, p, o, *take(3)) for p, o in ((gq, oq), (gkv, okv), (gout, oout))]
    cols = 2 * far * 4 // 8
    tall, wide = small.shape[0] // 8, small.shape[1] // cols

    def block(ref):
        def at(s):
            down = pl.ds(pl.multiple_of(s // cols * tall, 16), tall)
            return ref.at[down, pl.ds(pl.multiple_of(s % cols * wide, 128), wide)]

        return at

    sums = ReduceAll(net, block(small), *take(5), "xy")
    rows_back = ReduceTensor(net, dxn, *take(3))
    sum_own, tokens_own = take(2)
    every = GatherAll(net, sum_own, block(osmall), "yx")
    give_tokens = GatherTensor(net, tokens_own, otokens)
    for part in (rows_back, sums, *weights):
        part.load()
    me = net.group()
    mine = [net.load(blocks.at[me], oblocks.at[me])]
    net.greet(net.line() + [net.x, net.core])
    for part in (rows_back, sums, *weights):
        part.start()
    rows_back.step()
    for i in range(far):
        sums.stage_a(i)
    for i in range(far):
        sums.stage_b(i)
    for i in range(far):
        weights[0].step(i)
    rows_back.end()

    @pl.loop(0, tokens_own.shape[0] // 16)
    def _(i):
        rows = pl.ds(pl.multiple_of(i * 16, 16), 16)
        n = normed[rows, :]
        weighted = rows_back.total(rows) * gain[...]
        mean = jnp.mean(weighted * n, axis=-1, keepdims=True)
        back = scale[rows, :] * (weighted - n * mean)
        tokens_own[rows, :] = (dresid[rows, :] + back).astype(BF16)

    give_tokens.start()
    for i in range(far):
        sums.stage_c(i)
    small_tokens = []
    for r in range(far):
        for b in range(2):
            if r or b:
                to = net.at(r, b)
                k = net.push(blocks.at[to[0]], oblocks.at[me], to)
                small_tokens.append((net.group(-r, b), k))
    sums.end()

    @pl.loop(0, sum_own.shape[0] // 16)
    def _(i):
        rows = pl.ds(pl.multiple_of(i * 16, 16), 16)
        sum_own[rows, :] = sums.total(rows).astype(BF16)

    mine.append(net.load(sum_own, block(osmall)(net.slot())))
    every.start()
    for part in weights[1:]:
        for i in range(far):
            part.step(i)
    give_tokens.step()
    pipelined(far, [every])
    for part in (*weights, give_tokens, every):
        part.end()
    for g, k in small_tokens:
        net.arrived(oblocks.at[g], k)
    net.finish()
    for copy in mine:
        copy.wait()


def finish(weights, small, blocks, dxn, dresid, normed, scale, gain, groups, tensors, ident):
    far = groups // 2
    m, width = dresid.shape
    outs = [jax.ShapeDtypeStruct(w.shape[1:], F32) for w in weights]
    outs.append(jax.ShapeDtypeStruct(small.shape, BF16))
    outs.append(jax.ShapeDtypeStruct(blocks.shape, BF16))
    outs.append(jax.ShapeDtypeStruct((tensors, m, width), BF16))
    scratch = []
    for w in weights:
        scratch += ReduceGroups.scratch(far, *w.shape[1:])
    cell = (small.shape[0] // 8, small.shape[1] // (groups * tensors // 8))
    scratch += ReduceAll.scratch(far, *cell)
    scratch += ReduceTensor.scratch(m, width)
    scratch += [pltpu.VMEM(cell, BF16), pltpu.VMEM((m, width), BF16)]
    return pl.pallas_call(
        functools.partial(finish_kernel, far),
        out_shape=outs,
        in_specs=[ANY] * 6 + [IN_VMEM] * 4,
        out_specs=[IN_VMEM] * 3 + [ANY] * 3,
        scratch_shapes=scratch + semaphores(40 * far, 10 * far + 10),
        compiler_params=params(ident),
        cost_estimate=cost(150),
    )(*weights, small, blocks, dxn, dresid, normed, scale, gain)


TILE = 32


def dot_nt(left, right):
    return lax.dot_general(left, right, (((1,), (1,)), ((), ())), preferred_element_type=F32)


def dot_nn(left, right):
    return lax.dot_general(left, right, (((1,), (0,)), ((), ())), preferred_element_type=F32)


def experts_kernel(sizes, *refs):
    far, experts, hidden, shared, total = sizes
    groups = 2 * far
    (x_own, dy_all, picks, wg_hbm, wu_hbm, wd_hbm, ws_hbm, wr_hbm) = refs[:8]
    (outs_hbm, dg_out, gg_hbm, gu_hbm, gd_hbm, gs_hbm, x_all, ffn_all) = refs[8:16]
    (core_in, x0_in, y1_in, y0_in, x1_in, z_in) = refs[16:22]
    (w_in, w_down, h, dh, hs, dgu, hsn, dgun, acc_in, acc_down, x, dy) = refs[22:34]
    (part, ffn_part, acc, own, stage1, stage2, stage3, stage4, dg, dg_in, dg_sum) = refs[34:45]
    (
        ag_s, ag_r, core_s, core_r, x0_s, x0_r, y1_s, y1_r, y0_s, y0_r, x1_s, x1_r, z_s, z_r,
        dg_s, dg_r, wsem, lsem, csem,
    ) = refs[45:]
    routed = experts * hidden
    units = routed + shared
    m, width = x_own.shape
    block, half = 4 * m, m // 2
    chunk = min(256, block)
    per = chunk // m
    low, high = pl.ds(0, half), pl.ds(half, half)
    net = Net(far, None, None, None)
    both, sums = range(2), range(1)

    def remote(src, dst, send, recv, to):
        return pltpu.make_async_remote_copy(
            src_ref=src, dst_ref=dst, send_sem=send, recv_sem=recv, device_id=to, device_id_type=MESH
        )

    def wait_for(ref, sem):
        pltpu.make_async_copy(ref, ref, sem).wait()

    links = ((net.y, net.x), (net.x, net.y))

    def place(p, r, u, v, d=0):
        b, c = (u, v) if p == 0 else (v, u)
        return x_all.at[net.slot(-r, b, c, d), (low, high)[p]]

    def pass_on(p, kind, r, u, v, to):
        ref = place(p, r, u, v)
        remote(ref, ref, ag_s.at[p, kind, r], ag_r.at[p, kind, r], to).start()

    def rows_a(r):
        for p in both:
            pl.when(r > 0)(lambda: wait_for(place(p, r, 0, 0), ag_r.at[p, 0, r]))
            pass_on(p, 1, r, 0, 0, links[p][0])
            pass_on(p, 2, r, 0, 0, links[p][1])
            pass_on(p, 4, r, 0, 0, net.core)

    def rows_b(r):
        for p in both:
            wait_for(place(p, r, 1, 0), ag_r.at[p, 1, r])
            pass_on(p, 3, r, 1, 0, links[p][1])
            pass_on(p, 6, r, 1, 0, net.core)

    def rows_c(r):
        for p in both:
            for u in both:
                wait_for(place(p, r, u, 1), ag_r.at[p, 2 + u, r])
                pass_on(p, 5 + 2 * u, r, u, 1, net.core)

    def rows_d(r):
        for p in both:
            for u in both:
                for v in both:
                    wait_for(place(p, r, u, v, 1), ag_r.at[p, 4 + 2 * u + v, r])

    def load_block(s):
        g = net.group(-(s // 2), 1 - s % 2)
        copies = [
            pltpu.make_async_copy(x_all.at[g * 4 + t], x.at[pl.ds(t * m, m)], lsem.at[t])
            for t in range(4)
        ]
        rows = pl.ds(pl.multiple_of(g * block, block), block)
        return copies + [pltpu.make_async_copy(dy_all.at[rows], dy, lsem.at[4])]

    def mine(c, d):
        t = net.at(0, 0, c, d)[1]
        return pl.ds(pl.multiple_of(t * m, m), m)

    def ffn_copy(s):
        g = net.group(-(s // 2), 1 - s % 2)
        rows = pl.ds(pl.multiple_of(g * block, block), block)
        return pltpu.make_async_copy(ffn_part, ffn_all.at[rows], lsem.at[5])

    def core_push(s, a, c):
        return remote(
            part.at[a, mine(c, 1)], core_in.at[a, s, c], core_s.at[a, s, c], core_r.at[a, s, c], net.core
        )

    def x0_push(s, a):
        return remote(acc.at[a, s % 3, 1, low], x0_in.at[a, s], x0_s.at[a, s], x0_r.at[a, s], net.x)

    def y1_push(s, a, c):
        r = s // 2
        return remote(
            acc.at[a, s % 3, c, high], y1_in.at[a, r, c], y1_s.at[a, r, c], y1_r.at[a, r, c], net.y
        )

    def y0_push(s, a):
        r = s // 2
        return remote(acc.at[a, s % 3, 0, low], y0_in.at[a, r], y0_s.at[a, r], y0_r.at[a, r], net.y)

    def x1_push(s, a):
        r = s // 2
        return remote(acc.at[a, s % 3, 1, high], x1_in.at[a, r], x1_s.at[a, r], x1_r.at[a, r], net.x)

    def z_push(s, a):
        r = s // 2
        return remote(acc.at[a, s % 3, 0], z_in.at[a, r], z_s.at[a, r], z_r.at[a, r], net.at(-r))

    def copy_in(ref, buf, sem, k):
        return pltpu.make_async_copy(ref, buf, sem.at[k])

    def h1_loads(s):
        return [copy_in(core_in.at[a, s], stage1.at[a], csem, a) for a in sums]

    def h2_loads(s):
        return [copy_in(x0_in.at[a, s], stage2.at[a], csem, 2 + a) for a in sums]

    def h2_more(s):
        return [copy_in(y1_in.at[a, s // 2], stage3.at[a], csem, 4 + a) for a in sums]

    def h3_loads(s):
        return [copy_in(y0_in.at[a, s // 2], stage4.at[a, 0], csem, 6 + a) for a in sums] + [
            copy_in(x1_in.at[a, s // 2], stage4.at[a, 1], csem, 8 + a) for a in sums
        ]

    def begin_all(copies):
        for c in copies:
            c.start()

    def wait_all(copies):
        for c in copies:
            c.wait()

    def sends_done(s):
        for a in sums:
            x0_push(s, a).wait_send()

        @pl.when(s % 2 == 0)
        def _():
            for a in sums:
                for c in both:
                    y1_push(s, a, c).wait_send()
                y0_push(s, a).wait_send()

        @pl.when(s % 2 == 1)
        def _():
            for a in sums:
                x1_push(s, a).wait_send()
            pl.when(s > 1)(lambda: [z_push(s, a).wait_send() for a in sums] and None)

    def h1_pre(s):
        for a in sums:
            for c in both:
                wait_for(core_in.at[a, s, c], core_r.at[a, s, c])
        begin_all(h1_loads(s))

    def h1_post(s):
        wait_all(h1_loads(s))
        pl.when(s > 2)(lambda: sends_done(s - 3))
        for a in sums:
            for c in (1, 0):
                base = mine(c, 0).start

                @pl.loop(0, m // 16)
                def _(i):
                    rows = pl.ds(pl.multiple_of(i * 16, 16), 16)
                    there = pl.ds(pl.multiple_of(base + i * 16, 16), 16)
                    acc[a, s % 3, c, rows, :] = part[a, there, :] + stage1[a, c, rows, :]

            x0_push(s, a).start()

        @pl.when(s % 2 == 0)
        def _():
            for a in sums:
                for c in both:
                    y1_push(s, a, c).start()

    def add(a, s, c, base, buf):
        @pl.loop(0, half // 16)
        def _(i):
            rows = pl.ds(pl.multiple_of(base + i * 16, 16), 16)
            there = pl.ds(pl.multiple_of(i * 16, 16), 16)
            acc[a, s % 3, c, rows, :] = acc[a, s % 3, c, rows, :] + buf[there, :]

    def h2_pre(s):
        for a in sums:
            wait_for(x0_in.at[a, s], x0_r.at[a, s])
        begin_all(h2_loads(s))

        @pl.when(s % 2 == 1)
        def _():
            for a in sums:
                for c in both:
                    wait_for(y1_in.at[a, s // 2, c], y1_r.at[a, s // 2, c])
            begin_all(h2_more(s))

    def h2_post(s):
        wait_all(h2_loads(s))
        for a in sums:
            add(a, s, 0, 0, stage2.at[a])

        @pl.when(s % 2 == 0)
        def _():
            for a in sums:
                y0_push(s, a).start()

        @pl.when(s % 2 == 1)
        def _():
            wait_all(h2_more(s))
            for a in sums:
                for c in (1, 0):
                    add(a, s, c, half, stage3.at[a, c])
                x1_push(s, a).start()

    def h3_pre(s):
        for a in sums:
            wait_for(y0_in.at[a, s // 2], y0_r.at[a, s // 2])
            wait_for(x1_in.at[a, s // 2], x1_r.at[a, s // 2])
        begin_all(h3_loads(s))

    def h3_post(s):
        wait_all(h3_loads(s))
        for a in sums:
            for k in both:
                add(a, s, 0, k * half, stage4.at[a, k])

        @pl.when(s > 1)
        def _():
            for a in sums:
                z_push(s, a).start()

        @pl.when(s == 1)
        def _():
            for a in sums:
                own[a] = acc[a, 1, 0]

    def weights():
        pairs = []
        for e in range(experts):
            at = pl.ds(e * hidden, hidden)
            pairs.append((wg_hbm.at[e], w_in.at[at]))
            pairs.append((wu_hbm.at[e], w_in.at[pl.ds(units + e * hidden, hidden)]))
            pairs.append((wd_hbm.at[e], w_down.at[at]))
        pairs.append((ws_hbm.at[0], w_in.at[pl.ds(routed, shared)]))
        pairs.append((ws_hbm.at[1], w_in.at[pl.ds(units + routed, shared)]))
        pairs.append((ws_hbm.at[2], w_down.at[pl.ds(routed, shared)]))
        pairs.append((wr_hbm, w_in.at[pl.ds(2 * units, total)]))
        return [pltpu.make_async_copy(a, b, wsem.at[i]) for i, (a, b) in enumerate(pairs)]

    first = pltpu.make_async_copy(x_own, x_all.at[net.slot()], lsem.at[0])
    first.start()
    net.greet(net.line() + [net.at(c=c, d=d) for c, d in ((0, 1), (1, 0), (1, 1))])
    first.wait()
    for r in range(1, far):
        for p in both:
            ref = place(p, 0, 0, 0)
            remote(ref, ref, ag_s.at[p, 0, r], ag_r.at[p, 0, r], net.at(r)).start()
    rows_a(0)
    begin_all(weights())
    acc_in[...] = jnp.zeros_like(acc_in)
    acc_down[...] = jnp.zeros_like(acc_down)
    dg[...] = jnp.zeros_like(dg)
    hs[units:, :] = jnp.zeros((hs.shape[0] - units, block), BF16)
    dgu[2 * units :, :] = jnp.zeros((dgu.shape[0] - 2 * units, block), BF16)
    rows_b(0)
    rows_c(0)
    rows_d(0)
    begin_all(load_block(0))
    wait_all(weights())

    @pl.loop(0, groups)
    def _(s):
        r = s // 2
        g = net.group(-r, 1 - s % 2)
        more = r + 1 < far
        pl.when((s % 2 == 0) & more)(lambda: rows_a(r + 1))
        pl.when((s % 2 == 1) & more)(lambda: rows_c(r + 1))
        pl.when(s > 0)(lambda: h1_pre(s - 1))
        pl.when(s > 1)(lambda: h2_pre(s - 2))
        wait_all(load_block(s))

        @pl.loop(0, block // chunk)
        def _(n):
            at = pl.ds(pl.multiple_of(n * chunk, chunk), chunk)
            h[...] = dot_nt(w_in[...], x[at, :])
            dh[...] = dot_nt(w_down[...], dy[at, :])
            logits = h[2 * units :, :]
            expo = jnp.exp(logits - jnp.max(logits, axis=0, keepdims=True))
            marked = picks[:, pl.ds(pl.multiple_of(g * block + n * chunk, chunk), chunk)]
            gates = expo / jnp.sum(expo, axis=0, keepdims=True) * marked
            for e in range(experts + 1):
                base, count = (e * hidden, hidden) if e < experts else (routed, shared)
                gate = gates[e : e + 1, :] if e < experts else jnp.ones((1, chunk), F32)

                def body(i, total_):
                    a = pl.multiple_of(base + i * TILE, TILE)
                    here = pl.ds(a, TILE)
                    there = pl.ds(pl.multiple_of(units + a, TILE), TILE)
                    hg, hu, d = h[here, :], h[there, :], dh[here, :]
                    sig = 1.0 / (1.0 + jnp.exp(-hg))
                    act = hg * sig
                    dact = sig + act * (1.0 - sig)
                    hid = act * hu
                    hs[here, at] = (hid * gate).astype(BF16)
                    ds = d * gate
                    dgu[here, at] = (ds * hu * dact).astype(BF16)
                    dgu[there, at] = (ds * act).astype(BF16)
                    return total_ + jnp.sum(hid * d, axis=0, keepdims=True)

                row = lax.fori_loop(0, count // TILE, body, jnp.zeros((1, chunk), F32))
                if e < experts:
                    for j in range(per):
                        dg[n * per + j, g, e : e + 1, :] = row[:, j * m : (j + 1) * m]

        pl.when(s > 0)(lambda: h1_post(s - 1))
        pl.when(s > 1)(lambda: h2_post(s - 2))
        pl.when((s > 2) & (s % 2 == 0))(lambda: h3_pre(s - 3))
        pl.when((s % 2 == 0) & more)(lambda: rows_b(r + 1))

        @pl.loop(0, width // 512)
        def _(c):
            at = pl.ds(pl.multiple_of(c * 512, 512), 512)
            acc_in[:, at] += dot_nn(dgu[: 2 * units, :], x[:, at])
            acc_down[:, at] += dot_nn(hs[:units, :], dy[:, at])

        pl.when((s > 2) & (s % 2 == 0))(lambda: h3_post(s - 3))
        pl.when((s % 2 == 1) & more)(lambda: rows_d(r + 1))
        pl.when(s + 1 < groups)(lambda: begin_all(load_block(s + 1)))
        hsn[...] = hs[...].T
        dgun[...] = dgu[...].T

        @pl.when(s > 0)
        def _():
            for c in both:
                core_push(s - 1, 0, c).wait_send()
            ffn_copy(s - 1).wait()

        @pl.loop(0, width // 512)
        def _(c):
            at = pl.ds(pl.multiple_of(c * 512, 512), 512)
            part[0, :, at] = dot_nn(dgun[:, : 2 * units], w_in[: 2 * units, at]).astype(BF16)

        for c in (1, 0):
            core_push(s, 0, c).start()

        @pl.loop(0, width // 512)
        def _(c):
            at = pl.ds(pl.multiple_of(c * 512, 512), 512)
            ffn_part[:, at] = dot_nn(hsn[:, :units], w_down[:, at]).astype(BF16)

        ffn_copy(s).start()

    def stores():
        pairs = []
        for e in range(experts):
            at = pl.ds(e * hidden, hidden)
            pairs.append((acc_in.at[at], gg_hbm.at[e]))
            pairs.append((acc_in.at[pl.ds(units + e * hidden, hidden)], gu_hbm.at[e]))
            pairs.append((acc_down.at[at], gd_hbm.at[e]))
        pairs.append((acc_in.at[pl.ds(routed, shared)], gs_hbm.at[0]))
        pairs.append((acc_in.at[pl.ds(units + routed, shared)], gs_hbm.at[1]))
        pairs.append((acc_down.at[pl.ds(routed, shared)], gs_hbm.at[2]))
        return [pltpu.make_async_copy(a, b, wsem.at[i]) for i, (a, b) in enumerate(pairs)]

    peers = [(c, d) for c in both for d in both][1:]

    def dg_push(k):
        c, d = peers[k]
        e, t = net.at(0, 0, c, d)
        return remote(dg.at[t], dg_in.at[k], dg_s.at[k], dg_r.at[k], (e, t))

    for k in range(3):
        dg_push(k).start()
    last = groups - 1
    h1_pre(last)
    h2_pre(last - 1)
    h1_post(last)
    begin_all(stores())
    h2_post(last - 1)
    h3_pre(last - 2)
    h3_post(last - 2)
    for k in range(3):
        wait_for(dg_in.at[k], dg_r.at[k])
    dg_sum[...] = dg[net.at()[1]] + dg_in[0] + dg_in[1] + dg_in[2]
    me = net.group()
    dg_out[me] = dg_sum[me]
    others = [(r, b) for r in range(far) for b in both][1:]

    def dg_give(k):
        to = net.at(*others[k])
        return remote(dg_sum.at[to[0]], dg_out.at[me], dg_s.at[3 + k], dg_r.at[3 + k], to)

    for k in range(len(others)):
        dg_give(k).start()
    h2_pre(last)
    h2_post(last)
    h3_pre(last)
    h3_post(last)
    for r in range(1, far):
        for a in sums:
            wait_for(z_in.at[a, r], z_r.at[a, r])
            got = pltpu.make_async_copy(z_in.at[a, r], stage1.at[a, 0], csem.at[a])
            got.start()
            got.wait()

            @pl.loop(0, m // 16)
            def _(i):
                rows = pl.ds(pl.multiple_of(i * 16, 16), 16)
                own[a, rows, :] = own[a, rows, :] + stage1[a, 0, rows, :]

    give = pltpu.make_async_copy(own, outs_hbm, csem.at[0])
    give.start()
    for k in range(len(others)):
        r, b = others[k]
        wait_for(dg_out.at[net.group(-r, b)], dg_r.at[3 + k])
    for s in range(last - 2, last + 1):
        sends_done(s)
    for c in both:
        core_push(last, 0, c).wait_send()
    ffn_copy(last).wait()
    for p in both:
        for r in range(far):
            for kind in range(8):
                if r or kind:
                    wait_for(place(p, 0, 0, 0), ag_s.at[p, kind, r])
    for k in range(3):
        dg_push(k).wait_send()
    for k in range(len(others)):
        dg_give(k).wait_send()
    wait_all(stores())
    give.wait()


def experts_all(x, dy, picks, wg, wu, wd, ws, wr, groups, tensors, ident):
    m, width = x.shape
    far = groups // 2
    experts, hidden, _ = wg.shape
    shared, total = ws.shape[1], wr.shape[0]
    units = experts * hidden + shared
    block, half = 4 * m, m // 2
    chunk = min(256, block)
    up = lambda v: -(-v // 128) * 128
    like = jax.ShapeDtypeStruct
    outs = [
        like((1, m, width), BF16),
        like((groups, 8, m), F32),
        like(wg.shape, F32),
        like(wu.shape, F32),
        like(wd.shape, F32),
        like(ws.shape, F32),
        like((groups * tensors, m, width), BF16),
        like((groups * block, width), BF16),
        like((1, groups, 2, m, width), BF16),
        like((1, groups, half, width), BF16),
        like((1, far, 2, half, width), BF16),
        like((1, far, half, width), BF16),
        like((1, far, half, width), BF16),
        like((1, far, m, width), BF16),
    ]
    dma = pltpu.SemaphoreType.DMA
    scratch = [
        pltpu.VMEM((2 * units + total, width), BF16),
        pltpu.VMEM((units, width), BF16),
        pltpu.VMEM((2 * units + total, chunk), F32),
        pltpu.VMEM((units, chunk), F32),
        pltpu.VMEM((up(units), block), BF16),
        pltpu.VMEM((up(2 * units), block), BF16),
        pltpu.VMEM((block, up(units)), BF16),
        pltpu.VMEM((block, up(2 * units)), BF16),
        pltpu.VMEM((2 * units, width), F32),
        pltpu.VMEM((units, width), F32),
        pltpu.VMEM((block, width), BF16),
        pltpu.VMEM((block, width), BF16),
        pltpu.VMEM((1, block, width), BF16),
        pltpu.VMEM((block, width), BF16),
        pltpu.VMEM((1, 3, 2, m, width), BF16),
        pltpu.VMEM((1, m, width), BF16),
        pltpu.VMEM((1, 2, m, width), BF16),
        pltpu.VMEM((1, half, width), BF16),
        pltpu.VMEM((1, 2, half, width), BF16),
        pltpu.VMEM((1, 2, half, width), BF16),
        pltpu.VMEM((tensors, groups, 8, m), F32),
        pltpu.VMEM((3, groups, 8, m), F32),
        pltpu.VMEM((groups, 8, m), F32),
    ]
    for shape in (
        (2, 8, far), (1, groups, 2), (1, groups), (1, far, 2), (1, far), (1, far), (1, far), (groups + 2,),
    ):
        scratch += [dma(shape), dma(shape)]
    scratch += [dma((3 * experts + 4,)), dma((6,)), dma((10,))]
    got = pl.pallas_call(
        functools.partial(experts_kernel, (far, experts, hidden, shared, total)),
        out_shape=outs,
        in_specs=[ANY, ANY, IN_VMEM] + [ANY] * 5,
        out_specs=[ANY, IN_VMEM] + [ANY] * 12,
        scratch_shapes=scratch,
        compiler_params=params(ident, 63),
        cost_estimate=cost(280),
    )(x, dy, picks, wg, wu, wd, ws, wr)
    return [*got[:6], got[7]]


BOTH = ("expert", "tensor")


def shards(
    tokens,
    lengths,
    routes,
    gain_attn,
    w_query,
    w_latent,
    gain_latent,
    w_kv,
    w_out,
    gain_ffn,
    w_router,
    w_shared_gate,
    w_shared_up,
    w_shared_down,
    w_gate,
    w_up,
    w_down,
    cotangent,
):
    groups = lax.axis_size("expert")
    tensors = lax.axis_size("tensor")
    eindex = lax.axis_index("expert")
    tindex = lax.axis_index("tensor")
    rows, width = tokens.shape
    quarter = rows // tensors
    experts_local, _, hidden_units = w_gate.shape
    total_experts = experts_local * groups
    every = groups * rows
    bf16, f32 = jnp.bfloat16, jnp.float32

    def own(v):
        return lax.dynamic_slice_in_dim(v, tindex * quarter, quarter, 0)

    live_int = (jnp.arange(rows) < lengths[0]).astype(jnp.int32)
    live = live_int.astype(f32)[:, None]
    live_own = own(live)
    cot_own = own(cotangent).astype(f32)
    dffn_own = (cot_own * live_own).astype(bf16)

    part = w_shared_down.shape[0] // groups
    spare = -part % TILE

    def shared_units(v):
        v = jnp.pad(v.reshape(groups, part, v.shape[1]), ((0, 0), (0, spare), (0, 0)))
        return v

    shared_w = jnp.stack(
        [shared_units(v) for v in (w_shared_gate.T, w_shared_up.T, w_shared_down)], axis=1
    )
    choose = jnp.any(routes[..., None] == jnp.arange(total_experts), axis=1).astype(F32)
    picks = choose * live
    query_w, kv_up, out_proj, shared_w, marks = begin(
        (w_query, w_kv, w_out),
        shared_w.reshape(groups, -1, shared_w.shape[-1]),
        picks.T.astype(BF16),
        groups,
        0,
    )
    query_w = query_w.reshape(width, -1)
    kv_up = kv_up.reshape(KVR, -1)
    out_proj = out_proj.transpose(1, 0, 2).reshape(-1, width)
    shared_w = shared_w.transpose(1, 0, 2).reshape(3, part + spare, width)
    gate_t, up_t = w_gate.transpose(0, 2, 1), w_up.transpose(0, 2, 1)
    router_t = jnp.roll(w_router.T, -eindex * experts_local, axis=0)
    parts = max(1, every // 4096)
    some = quarter // parts

    def split(v):
        return v.reshape(parts, some, v.shape[1])

    marks = marks.reshape(groups, total_experts, tensors, parts, some).transpose(3, 1, 0, 2, 4)
    picks_all = marks.reshape(parts, total_experts, -1).astype(F32)
    picks_all = jnp.roll(picks_all, -eindex * experts_local, axis=1)
    dffn = [lax.all_gather(v, BOTH, axis=0, tiled=True) for v in split(dffn_own)]

    heads = out_proj.shape[0] // VD
    xf = tokens.astype(f32)
    scale_one = inv_rms(xf)
    normed_one = xf * scale_one
    xn1 = (normed_one * gain_attn).astype(bf16)
    cosine, sine = rope_tables(rows, ROPE)
    qfull = mat(xn1, query_w).reshape(rows, heads, NOPE + ROPE)
    qcat = jnp.concatenate(
        [qfull[..., :NOPE], rotate(qfull[..., NOPE:], cosine[:, None, :], sine[:, None, :])],
        axis=-1,
    ).astype(bf16)
    latent = mat(xn1, w_latent)
    comp = latent[:, :KVR]
    scale_lat = inv_rms(comp)
    normed_lat = comp * scale_lat
    compressed = (normed_lat * gain_latent).astype(bf16)
    key_rope = rotate(latent[:, KVR:], cosine, sine).astype(bf16)
    key_value = mat(compressed, kv_up).astype(bf16).reshape(rows, heads, NOPE + VD)
    keys = jnp.concatenate(
        [key_value[..., :NOPE], jnp.broadcast_to(key_rope[:, None, :], (rows, heads, ROPE))],
        axis=-1,
    )
    values = key_value[..., NOPE:]
    causal = jnp.arange(rows)[:, None] >= jnp.arange(rows)[None, :]
    score_scale = (NOPE + ROPE) ** (-0.5)
    raw = jnp.einsum("qhd,khd->hqk", qcat, keys, preferred_element_type=f32) * score_scale
    score_now = jnp.where(causal[None], raw, -jnp.inf)
    peak = jnp.max(score_now, axis=-1, keepdims=True)
    expo = jnp.exp(score_now - peak)
    pfull = expo / jnp.sum(expo, axis=-1, keepdims=True)
    probs = pfull.astype(bf16)
    attended = (
        jnp.einsum("hqk,khd->qhd", probs, values, preferred_element_type=f32)
        .astype(bf16)
        .reshape(rows, heads * VD)
    )
    partial = mat(attended, out_proj).astype(bf16).reshape(tensors, quarter, width)
    partial, dffn = lax.optimization_barrier((partial, dffn))
    attn = sum_tensor(partial, groups, parts + 2)
    resid = own(xf) + live_own * attn
    scale_two = inv_rms(resid)
    normed_two = resid * scale_two
    xn2_own = (normed_two * gain_ffn).astype(bf16)
    router = jax.nn.softmax(mat(xn2_own, w_router), axis=-1)
    outs = []
    for k in range(parts):
        dx, dgates, *grads, ffn = experts_all(
            split(xn2_own)[k],
            dffn[k],
            picks_all[k],
            gate_t,
            up_t,
            w_down,
            shared_w,
            router_t,
            groups,
            tensors,
            k + 1,
        )
        dx = dx[0].astype(F32)
        ffn = lax.psum_scatter(ffn, BOTH, scatter_dimension=0, tiled=True).astype(F32)
        dgates = dgates[:, :experts_local].reshape(total_experts, some).T
        outs.append((ffn, dx, dgates, *grads))
    ffn, dx, dgates = (jnp.concatenate(v, axis=0) for v in list(zip(*outs))[:3])
    grads = [functools.reduce(jnp.add, v) for v in list(zip(*outs))[3:]]
    drouter = own(picks) * dgates
    grad_gate, grad_up = (v.transpose(0, 2, 1) for v in grads[:2])
    grad_down = grads[2]
    shared_g = grads[3].reshape(3, part + spare, groups, width // groups).astype(BF16)
    shared_g = shared_g.transpose(2, 0, 1, 3).reshape(groups, -1, width // groups)
    dlogit = router * (drouter - jnp.sum(router * drouter, axis=-1, keepdims=True))
    grad_router = mat_tn(dlogit.astype(bf16), xn2_own)
    dnorm_two = dx + mat_nt(dlogit.astype(bf16), w_router)
    grad_gain_ffn = jnp.sum(dnorm_two * normed_two, axis=0)
    dresid = cot_own + norm_back(dnorm_two, normed_two, scale_two, gain_ffn)
    dattn = gather_tensor((dresid * live_own).astype(bf16), groups, tensors, parts + 3).reshape(rows, width)
    grad_out = mat_tn(attended, dattn)
    dattended = mat_nt(dattn, out_proj).astype(bf16).reshape(rows, heads, VD)
    dvalues = jnp.einsum("hqk,qhd->khd", probs, dattended, preferred_element_type=f32)
    dprobs = jnp.einsum("qhd,khd->hqk", dattended, values, preferred_element_type=f32)
    dscore = (
        pfull * (dprobs - jnp.sum(pfull * dprobs, axis=-1, keepdims=True)) * score_scale
    ).astype(bf16)
    dquery = jnp.einsum("hqk,khd->qhd", dscore, keys, preferred_element_type=f32)
    dkeys = jnp.einsum("hqk,qhd->khd", dscore, qcat, preferred_element_type=f32)
    dkv = (
        jnp.concatenate([dkeys[..., :NOPE], dvalues], axis=-1)
        .astype(bf16)
        .reshape(rows, heads * (NOPE + VD))
    )
    grad_kv = mat_tn(compressed, dkv)
    dcomp = mat_nt(dkv, kv_up)
    grad_gain_latent = jnp.sum(dcomp * normed_lat, axis=0)
    dlatent = jnp.concatenate(
        [
            norm_back(dcomp, normed_lat, scale_lat, gain_latent),
            rotate_back(jnp.sum(dkeys[..., NOPE:], axis=1), cosine, sine),
        ],
        axis=-1,
    ).astype(bf16)
    dqfull = jnp.concatenate(
        [dquery[..., :NOPE], rotate_back(dquery[..., NOPE:], cosine[:, None, :], sine[:, None, :])],
        axis=-1,
    )
    dqfull = dqfull.astype(bf16).reshape(rows, heads * (NOPE + ROPE))
    grad_query = mat_tn(xn1, dqfull)
    grad_latent = mat_tn(dlatent, xn1)
    dnorm_one = mat_nt(dqfull, query_w) + mat_nt(dlatent, w_latent)
    grad_gain_attn = jnp.sum(dnorm_one * normed_one, axis=0)
    small = jnp.concatenate(
        [
            grad_latent,
            grad_router,
            grad_gain_attn[None],
            grad_gain_ffn[None],
            jnp.pad(grad_gain_latent, (0, width - KVR))[None],
        ],
        axis=0,
    ).astype(bf16)
    small = jnp.pad(small, ((0, -small.shape[0] % 128), (0, 0)))
    grad_out = grad_out.astype(bf16).reshape(-1, groups, width // groups).transpose(1, 0, 2)
    grad_query, grad_kv, grad_out, small, shared_g, grad_tokens = finish(
        (
            grad_query.astype(bf16).reshape(groups, -1, grad_query.shape[1]),
            grad_kv.astype(bf16).reshape(groups, -1, grad_kv.shape[1]),
            grad_out,
        ),
        small,
        shared_g,
        dnorm_one.astype(bf16).reshape(tensors, quarter, width),
        dresid,
        own(normed_one),
        own(scale_one),
        gain_attn[None],
        groups,
        tensors,
        parts + 1,
    )
    grad_tokens = grad_tokens.reshape(rows, width)
    grad_tokens, ffn, resid_late = lax.optimization_barrier((grad_tokens, ffn, resid))
    output_own = (resid_late + live_own * ffn).astype(bf16)
    output = lax.all_gather(output_own, "tensor", axis=0, tiled=True)
    at = w_latent.shape[1]
    small = small.astype(f32)
    grad_latent = small[:at].T
    grad_router = small[at : at + total_experts].T
    at = at + total_experts
    grad_gain_attn = small[at]
    grad_gain_ffn = small[at + 1]
    grad_gain_latent = small[at + 2, :KVR]
    shared_g = shared_g.reshape(groups, 3, part + spare, -1)[:, :, :part].transpose(1, 0, 2, 3)
    shared_g = shared_g.reshape(3, groups * part, -1).astype(f32)
    grad_sgate, grad_sup, grad_sdown = shared_g[0].T, shared_g[1].T, shared_g[2]
    return (
        output,
        grad_tokens,
        grad_gain_attn,
        grad_query,
        grad_latent,
        grad_gain_latent,
        grad_kv,
        grad_out,
        grad_gain_ffn,
        grad_router,
        grad_sgate,
        grad_sup,
        grad_sdown,
        grad_gate,
        grad_up,
        grad_down,
    )


def solution(mesh):
    in_specs = (
        P("expert", None),
        P("expert"),
        P("expert", None),
        P(),
        P("expert", "tensor"),
        P(),
        P(),
        P("expert", "tensor"),
        P("tensor", "expert"),
        P(),
        P(),
        P("expert", "tensor"),
        P("expert", "tensor"),
        P("tensor", "expert"),
        P("expert", None, "tensor"),
        P("expert", None, "tensor"),
        P("expert", "tensor", None),
        P("expert", None),
    )
    out_specs = (
        P("expert", None),
        P("expert", None),
        P(),
        P("expert", "tensor"),
        P(),
        P(),
        P("expert", "tensor"),
        P("tensor", "expert"),
        P(),
        P(),
        P("expert", "tensor"),
        P("expert", "tensor"),
        P("tensor", "expert"),
        P("expert", None, "tensor"),
        P("expert", None, "tensor"),
        P("expert", "tensor", None),
    )
    return jax.shard_map(shards, mesh=mesh, in_specs=in_specs, out_specs=out_specs, check_vma=False)
```

time: 3220 us -> 895 us (0.28)
  waiting for transfers between devices: 1580 us -> 11.4 us
  blocking collectives: 871 us -> 0 us
  Pallas kernels: 0 us -> 692 us
  local copies, waits for them, and re-layouts: 317 us -> 81.7 us
  matrix products: 287 us -> 55.6 us
  other arithmetic: 120 us -> 27.5 us
    all_to_all x2 -> x0, blocking collectives: 830 us -> none  [the longest x1 416 us: shards(): lax.all_to_all(outgoing, 'expert', split_axis=0, concat_axis=0, tiled=True)]
    pallas_call x0 -> x5, Pallas kernels: none -> 692 us  [the longest x1 307 us: experts_all(): pl.pallas_call(functools.partial(experts_kernel, (far, experts, hidden, s...]
    all_to_all x2 -> x0, waiting for transfers between devices: 361 us -> none  [the longest x1 361 us: shards(): lax.all_to_all(partial_value, 'expert', split_axis=0, concat_axis=0, tile...]
    all_gather x6 -> x2, waiting for transfers between devices: 341 us -> 11.4 us  [the longest x1 11.4 us: shards(): output = lax.all_gather(output_own, 'tensor', axis=0, tiled=True)]
    unnamed x18 -> x3, waiting for transfers between devices: 323 us -> 0.05 us
    reduce_scatter x6 -> x1, waiting for transfers between devices: 319 us -> 0.02 us  [shards(): lax.psum_scatter(ffn, BOTH, scatter_dimension=0, tiled=True).astype(F32)]
    psum x4 -> x0, waiting for transfers between devices: 236 us -> none  [the longest x1 150 us: shards(): lax.psum((grad_latent, grad_gain_attn, grad_gain_latent, grad_gain_ffn, g...]
    dot_general x20 -> x6, matrix products: 214 us -> 26 us  [the longest x1 9.34 us: shards(): jnp.einsum('hqk,khd->qhd', dscore, keys, preferred_element_type=f32)]
  transfers between devices with their start and end apart: 19 -> 3, of which waited for: 18 -> 1; matrix products, arithmetic and copies ran while one was open for 10% -> 15% of each run, Pallas kernels for 0% -> 42%
where the time goes in v2:
time: 895 us; the launch traced here: 884 us
  Pallas kernels  692 us (77%)
  local copies, waits for them, and re-layouts  81.7 us (9%)
  matrix products  55.6 us (6%)
  other arithmetic  27.5 us (3%)
  between operations  15.8 us (2%)
  waiting for transfers between devices  11.4 us (1%)
    pallas_call x1, Pallas kernels, experts_all(): pl.pallas_call(functools.partial(experts_kernel, (far, experts, hidden, s...  307 us
    pallas_call x1, Pallas kernels, finish(): pl.pallas_call(functools.partial(finish_kernel, far), out_shape=outs, in_...  193 us
    pallas_call x1, Pallas kernels, begin(): pl.pallas_call(functools.partial(begin_kernel, far), out_shape=outs, in_s...  147 us
    pallas_call x1, Pallas kernels, gather_tensor(): pl.pallas_call(functools.partial(gather_tensor_kernel, groups // 2), out_...  27.6 us
    unnamed x140, local copies, waits for them, and re-layouts  25.3 us
  transfers between devices with their start and end apart: 3, of which 1 were waited for; matrix products, arithmetic and copies ran while one was open for 15% of the time, Pallas kernels for 42%

profile of v2, /device:TPU:0, one launch (start us, length us, event | category | flops | bytes accessed | tf_op | source)
XLA Modules:
  0.0 883.7 jit_solution(5851812204998776191)
XLA Ops:
  8.0 2.0 fusion.25
  10.9 1.0 pad_bitcast_fusion.2
  12.0 1.1 pad_maximum_fusion
  13.8 147.0 %shard_map.297 = (bf16[8,256,768]{2,1,0:T(8,128)(2,1)}, bf16[8,64,1024]{2,1,0:T(8,128)(2,1)}, bf16[8,512,256]{2,1,0:T(8,128)(2,1)}, bf16[8,288,256]{2,1,0:T(8,128)(2,1)}, bf16[8,16,512]{2,1,0:T(8,128)(2,1)}) custom-call(bf16[256,768]{1,0:T(8,128)(2,1)} %refs_0_.1, bf16[64,1024]{1,0:T(8,128)(2,1)} %refs_1_.1, bf16[512,256]{1,0:T(8,128)(2,1)} %refs_2_.1, ...), custom_call_target="tpu_custom_call" | custom-call | bytes 300000000 | tf_op jit(solution)/shard_map/pallas_call | solution.py:352
  160.8 4.8 copy.66
  165.6 2.5 convert_element_type.168
  168.7 1.5 fusion.50
  170.4 1.8 convolution_convert_fusion.6
  172.2 2.3 copy.87
  174.5 1.9 slice.114
  176.4 3.8 fusion.12
  180.2 1.1 copy-done.29
  181.4 4.1 copy.69
  186.4 2.1 copy.71
  188.5 1.4 reshape.288.refs_6_
  190.3 1.1 subtract_convert_fusion
  193.1 2.1 fusion.54
  195.8 1.7 copy-done.59
  198.5 1.3 convolution_convert_fusion.3
  200.6 16.4 %shard_map.298 = f32[128,2048]{1,0:T(8,128)S(1)} custom-call(bf16[4,128,2048]{2,1,0:T(8,128)(2,1)S(1)} %bitcast.117), custom_call_target="tpu_custom_call" | custom-call | bytes 48000000 | tf_op jit(solution)/shard_map/pallas_call | solution.py:491
  217.0 1.5 multiply_reduce_fusion.7
  218.6 1.0 copy-done
  219.6 0.9 multiply_convert_fusion.4.refs_0_
  220.5 307.2 %shard_map.299 = (bf16[1,128,2048]{2,1,0:T(8,128)(2,1)}, f32[8,8,128]{2,1,0:T(8,128)}, f32[2,352,2048]{2,1,0:T(8,128)}, f32[2,352,2048]{2,1,0:T(8,128)}, f32[2,3...) custom-call(bf16[128,2048]{1,0:T(8,128)(2,1)} %multiply_convert_fusi, ...), custom_call_target="tpu_custom_call" | custom-call | bytes 840000000 | tf_op jit(solution)/shard_map/pallas_call | solution.py:1137
  527.8 0.9 dynamic-slice_bitcast_fusion
  531.2 2.5 multiply_convert_fusion.3
  533.6 27.6 %shard_map.300 = bf16[4,128,2048]{2,1,0:T(8,128)(2,1)S(1)} custom-call(bf16[128,2048]{1,0:T(8,128)(2,1)S(1)} %get-tuple-element.66.own), custom_call_target="tpu_custom_call" | custom-call | bytes 48000000 | tf_op jit(solution)/shard_map/pallas_call | solution.py:514
  561.2 1.3 convolution_convert_fusion.7
  563.3 2.8 fusion.29
  566.1 9.2 %fusion.22 = f32[512,4,192]{0,2,1:T(8,128)} fusion(f32[4,512,512]{1,2,0:T(8,128)} %fusion.29, bf16[512,4,32]{0,2,1:T(8,128)(2,1)} %copy-done.36, bf16[512,4,32]{0,2,1:T(8,128)(2,1)} %copy-done.35, bf16[512,4,128]{0,2,1:T(8,128)(2,1)} %copy-done.22, f32[4,512,512]{1,2,0:T(8,128)} %copy-done.59, f32[4,512]{1,0:T(4,128)} %copy-done.60), kind=kOutput, calls=%fused_computation.34 | convolution fusion | flops 412355072 | bytes 10756096 | tf_op jit(solution)/shard_map/hqk,qhd->khd/dot_general | solution.py:1312
  575.4 2.1 slice.124
  577.5 9.3 %fusion.19 = f32[512,4,192]{0,2,1:T(8,128)} fusion(f32[4,512,512]{1,2,0:T(8,128)} %fusion.29, bf16[512,4,64]{0,2,1:T(8,128)(2,1)S(1)} %copy-done.24, bf16[512,4,128]{0,2,1:T(8,128)(2,1)} %slice.114, f32[4,512,512]{1,2,0:T(8,128)} %copy-done.59, f32[4,512]{1,0:T(4,128)} %copy-done.60), kind=kOutput, calls=%fused_computation.33 | convolution fusion | flops 411568640 | bytes 10756096 | tf_op jit(solution)/shard_map/hqk,khd->qhd/dot_general | solution.py:1311
  586.8 1.4 slice.121
  588.2 1.1 slice_reduce_fusion
  589.3 1.1 multiply_add_fusion.1
  590.5 3.4 convolution_bitcast_fusion
  596.3 1.8 fusion.56
  598.7 4.9 fusion.51
  603.8 3.2 convolution_convert_fusion.1
  607.0 11.8 %concatenate.49 = bf16[595,2048]{1,0:T(8,128)(2,1)} concatenate(bf16[576,2048]{1,0:T(8,128)(2,1)} %convolution_convert_fusion.1, bf16[16,2048]{1,0:T(8,128)(2,1)S(1)} %convolution_convert_fusion.4, bf16[1,2048]{1,0:T(2,128)(2,1)S(1)} %broadcast_in_dim.28, bf16[1,2048]{1,0:T(2,128)(2,1)S(1)} %broadcast_in_dim.29, bf16[1,2048]{1,0:T(2,128)(2,1)S(1)} %broadcast_in_dim.30), dimensions={0} | concatenate | bytes 4874240 | tf_op jit(solution)/shard_map/concatenate | solution.py:1337
  618.8 3.6 pad.23.refs_3_
  622.5 2.6 convolution_convert_fusion.2
  625.1 2.9 copy.77
  628.0 2.4 copy.78
  630.4 1.9 convert_element_type.199
  632.3 1.1 copy.90
  633.4 2.5 constant_dynamic-slice_fusion.refs_7_
  635.9 1.8 convolution_convert_fusion.5
  637.7 3.7 convolution_convert_fusion
  641.4 193.4 %shard_map.301 = (f32[256,768]{1,0:T(8,128)}, f32[64,1024]{1,0:T(8,128)}, f32[512,256]{1,0:T(8,128)}, bf16[640,2048]{1,0:T(8,128)(2,1)}, bf16[8,288,256]{2,1,0:T(8,128)(2,1)}, /*index=5*/bf16[4,128,2048]{2,1,0:T(8,128)(2,1)}) custom-call(bf16[8,256,768]{2,1,0:T(8,128)(2,1)} %bitcast.139, bf16[8,64,1024]{2,1,0:T(8,128)(2,1)} %bitcast.130, ...), custom_call_target="tpu_custom_call" | custom-call | bytes 450000000 | tf_op jit(solution)/shard_map/pallas_call | solution.py:624
  834.8 1.1 convert_element_type.202
  835.9 1.0 add_convert_fusion
  837.0 2.5 convert_element_type.204
  839.5 1.3 slice.130
  841.0 1.4 fusion.53
  842.4 1.4 fusion.52
  844.5 2.8 slice_bitcast_fusion
  847.2 11.4 %all-gather.5.cloned.1.call-done = bf16[512,2048]{1,0:T(8,128)(2,1)} async-done(((bf16[128,2048]{1,0:T(8,128)(2,1)}), bf16[512,2048]{1,0:T(8,128)(2,1)}) %all-gather.5.cloned.1.call-update) | async-done | bytes 2097168 | tf_op jit(solution)/shard_map/all_gather | solution.py:1369
  858.6 3.3 copy.100
  861.9 1.3 copy.101
  863.2 0.9 copy.102
  865.6 6.0 copy.105
  871.7 2.5 copy.106
  874.2 2.5 copy.107
  (186 shorter events, 16.3 us)
Async XLA Ops:
  7.2 4.7 copy-start.40
  7.2 4.7 copy-start.39
  7.2 193.4 %all-gather.3.cloned.1.call-start = ((), (), s32[]{:S(2)}) async-start(), calls=%async_computation.1 | async-start | bytes 17301504 | tf_op jit(solution)/shard_map/all_gather | solution.py:1226
  8.0 5.1 copy-start.50
  10.1 824.7 %reduce-scatter.2.cloned.1.call-start = ((), (), s32[]{:S(2)}) async-start(), calls=%async_computation.2 | async-start | bytes 17301504 | tf_op jit(solution)/shard_map/reduce_scatter | solution.py:1288
  160.8 4.8 copy-start.2
  165.6 3.0 copy-start.15
  165.6 3.1 copy-start.44
  168.7 7.7 copy-start.46
  168.7 1.7 copy-start.48
  168.7 1.7 copy-start.55
  170.2 19.7 %copy-start.5 = (f32[512,576]{0,1:T(8,128)}, f32[512,576]{0,1:T(8,128)S(1)}, u32[]{:S(2)}) copy-start(f32[512,576]{0,1:T(8,128)S(1)} %fusion.50) | copy-start | bytes 3538948
  180.2 1.1 copy-start.29
  181.4 10.1 %copy-start.22 = (bf16[512,4,128]{0,2,1:T(8,128)(2,1)}, bf16[512,4,128]{0,2,1:T(8,128)(2,1)S(1)}, u32[]{:S(2)}) copy-start(bf16[512,4,128]{0,2,1:T(8,128)(2,1)S(1)} %slice.174) | copy-start | bytes 1572868
  181.4 4.2 copy-start.42
  188.5 3.0 copy-start.21
  189.9 2.5 copy-start.53
  191.4 0.9 copy-start.35
  193.1 2.2 copy-start.10
  195.3 2.2 copy-start.59
  195.3 2.2 copy-start.60
  195.3 3.2 copy-start.17
  198.5 1.3 copy-start.38
  199.8 17.2 %copy-start.51 = (f32[128]{0:T(128)S(1)}, f32[128]{0:T(128)}, u32[]{:S(2)}) copy-start(f32[128]{0:T(128)} %copy-done.50) | copy-start | bytes 1540
  217.0 2.5 copy-start.43
  218.6 1.0 copy-start
  527.7 2.5 copy-start.8
  527.7 2.5 copy-start.31
  527.8 2.9 copy-start.1
  527.8 2.9 copy-start.32
  527.8 330.8 %all-gather.5.cloned.1.call-start = ((), (), s32[]{:S(2)}) async-start(), calls=%async_computation.3 | async-start | bytes 2621440 | tf_op jit(solution)/shard_map/all_gather | solution.py:1369
  533.6 27.6 %copy-start.18 = (bf16[512,8,256]{0,2,1:T(8,128)(2,1)S(1)}, bf16[512,8,256]{0,2,1:T(8,128)(2,1)}, u32[]{:S(2)}) copy-start(bf16[512,8,256]{0,2,1:T(8,128)(2,1)} %copy.69) | copy-start | bytes 6291460
  561.2 2.1 copy-start.11
  566.1 11.4 %copy-start.24 = (bf16[512,4,64]{0,2,1:T(8,128)(2,1)S(1)}, bf16[512,4,64]{0,2,1:T(8,128)(2,1)}, u32[]{:S(2)}) copy-start(bf16[512,4,64]{0,2,1:T(8,128)(2,1)} %copy-done.23) | copy-start | bytes 786436
  586.8 3.7 copy-start.34
  586.8 3.7 copy-start.61
  590.5 5.1 copy-start.26
  590.5 3.4 copy-start.20
  590.5 3.5 copy-start.6
  590.5 3.5 copy-start.49
  590.5 3.5 copy-start.56
  594.0 1.0 copy-start.12
  594.0 1.0 copy-start.54
  594.1 2.3 copy-start.14
  596.3 1.9 copy-start.3
  596.3 2.3 copy-start.16
  596.3 2.4 copy-start.47
  598.7 5.0 copy-start.9
  598.7 5.2 copy-start.45
  618.8 3.7 copy-start.58
  632.3 3.7 copy-start.7
  632.3 3.6 copy-start.13
  633.4 4.2 copy-start.4
  633.4 4.2 copy-start.27
  641.4 194.5 %copy-start.52 = (f32[128]{0:T(128)S(1)}, f32[128]{0:T(128)}, u32[]{:S(2)}) copy-start(f32[128]{0:T(128)} %copy-done.50) | copy-start | bytes 1540
  837.0 3.8 copy-start.25
  844.5 27.2 %slice-start.2 = ((s8[5767168]{0:T(1024)(128)(4,1)}), s8[1572864]{0:T(1024)(128)(4,1)S(1)}, s32[]{:S(2)}) async-start(s8[5767168]{0:T(1024)(128)(4,1)} %bitcast.123), calls=%async_computation.6 | async-start | bytes 3145728
  858.6 3.3 copy-start.19
  858.6 4.6 copy-start.28
  861.9 2.2 copy-start.41
  861.9 2.9 copy-start.37
  861.9 9.8 %slice-start.3 = ((s8[5767168]{0:T(1024)(128)(4,1)}), s8[4194304]{0:T(1024)(128)(4,1)S(1)}, s32[]{:S(2)}) async-start(s8[5767168]{0:T(1024)(128)(4,1)} %bitcast.123), calls=%async_computation.7 | async-start | bytes 8388608
  865.6 8.6 slice-start
  871.7 2.5 slice-start.1
  (5 other events, 4.4 us)
Sparse Core Ops, SparseCore 0:
  11.5 186.3 all-gather.2
  527.9 222.5 reduce-scatter.1
  837.1 21.4 all-gather.4

commit v3 on v2

--- a/solution.py
+++ b/solution.py
@@ -281,6 +281,24 @@
         ]
 
 
+class Summed:
+    def __init__(self, ref):
+        self.ref = ref
+
+    def load(self):
+        pass
+
+    start = end = load
+
+    def stage_a(self, i):
+        pass
+
+    stage_b = stage_c = stage_a
+
+    def total(self, rows):
+        return self.ref[rows, :]
+
+
 def pipelined(far, parts):
     for i in range(far + 2):
         for s in range(3):
@@ -309,14 +327,16 @@
 
 def begin_kernel(far, *refs):
     n = 3
-    ws, blocks, marks = refs[:n], refs[n], refs[n + 1]
-    outs, blocks_out, marks_out = refs[n + 2 : 2 * n + 2], refs[2 * n + 2], refs[2 * n + 3]
-    net = Net(far, *refs[2 * n + 4 :])
+    ws, blocks, marks, dy = refs[:n], refs[n], refs[n + 1], refs[n + 2]
+    outs, blocks_out, marks_out, near = refs[n + 3 : 2 * n + 3], *refs[2 * n + 3 : 2 * n + 6]
+    net = Net(far, *refs[2 * n + 6 :])
     me = net.group()
     mine = [net.load(w, o.at[me]) for w, o in zip(ws, outs)]
     mine.append(net.load(blocks.at[me], blocks_out.at[me]))
     mine.append(net.load(marks, marks_out.at[me]))
-    net.greet(net.line())
+    net.greet(net.line() + [net.x, net.core])
+    here = [near.at[net.at(0, 0, c, d)[1]] for c in range(2) for d in range(2)]
+    dy_y = net.push(dy, here[0], net.y)
     tokens = {}
     others = [(r, b) for r in range(far) for b in range(2)][1:]
     for a, (w, o) in enumerate(zip(ws, outs)):
@@ -326,6 +346,9 @@
     small = []
     for r, b in others:
         small.append((r, b, marks_out, net.push(marks, marks_out.at[me], net.at(r, b))))
+    net.arrived(here[0], dy_y)
+    dy_x = net.push(here[0], here[0], net.x)
+    dy_core = net.push(here[0], here[0], net.core)
     for a, (w, o) in enumerate(zip(ws, outs)):
         for r in range(1, far):
             place = o.at[net.group(-r)]
@@ -334,9 +357,13 @@
     for r, b in others:
         to = net.at(r, b)
         small.append((r, b, blocks_out, net.push(blocks.at[to[0]], blocks_out.at[me], to)))
+    net.arrived(here[2], dy_x)
+    dy_both = net.push(here[2], here[2], net.core)
     for a, o in enumerate(outs):
         for r in range(far):
             net.arrived(o.at[net.group(-r, 1)], tokens[a, r, 1])
+    net.arrived(here[1], dy_core)
+    net.arrived(here[3], dy_both)
     for r, b, ref, k in small:
         net.arrived(ref.at[net.group(-r, b)], k)
     net.finish()
@@ -344,20 +371,21 @@
         copy.wait()
 
 
-def begin(ws, blocks, marks, groups, ident):
+def begin(ws, blocks, marks, dy, groups, tensors, ident):
     far = groups // 2
     outs = [jax.ShapeDtypeStruct((groups, *w.shape), w.dtype) for w in ws]
     outs.append(jax.ShapeDtypeStruct(blocks.shape, blocks.dtype))
     outs.append(jax.ShapeDtypeStruct((groups, *marks.shape), marks.dtype))
+    outs.append(jax.ShapeDtypeStruct((tensors, *dy.shape), dy.dtype))
     return pl.pallas_call(
         functools.partial(begin_kernel, far),
         out_shape=outs,
-        in_specs=[ANY] * 5,
-        out_specs=[ANY] * 5,
+        in_specs=[ANY] * 6,
+        out_specs=[ANY] * 6,
         scratch_shapes=semaphores(10 * far, 5),
         compiler_params=params(ident),
         cost_estimate=cost(100),
-    )(*ws, blocks, marks)
+    )(*ws, blocks, marks, dy)
 
 
 class ReduceGroups:
@@ -365,21 +393,18 @@
         self.net, self.part, self.out = net, part, out
         self.acc, self.from_y, self.from_z = acc, from_y, from_z
         self.turn = list(range(net.far - 1, -1, -1))
+        self.y, self.z = {}, {}
 
     def load(self):
         self.loads = {
             r: self.net.load(self.part.at[self.net.group(r)], self.acc.at[r]) for r in self.turn
         }
 
-    def start(self):
-        self.y = {
-            r: self.net.push(self.part.at[self.net.group(r, 1)], self.from_y.at[r], self.net.y)
-            for r in self.turn
-        }
-        self.z = {}
-
-    def step(self, i):
-        r = self.turn[i]
+    def start(self, r):
+        part = self.part.at[self.net.group(r, 1)]
+        self.y[r] = self.net.push(part, self.from_y.at[r], self.net.y)
+
+    def step(self, r):
         self.loads[r].wait()
         self.net.arrived(self.from_y.at[r], self.y[r])
         add_rows(self.acc.at[r], self.from_y.at[r])
@@ -499,33 +524,82 @@
     )(part)
 
 
-def gather_tensor_kernel(far, own, out, *scratch):
+def gather_tensor_kernel(far, own, blocks, out, blocks_out, *scratch):
     net = Net(far, *scratch)
     give = GatherTensor(net, own, out)
-    net.greet([net.x, net.core])
+    me = net.group()
+    net.greet(net.line() + [net.x, net.core])
     give.start()
+    mine = net.load(blocks.at[me], blocks_out.at[me])
+    small = []
+    for r in range(far):
+        for b in range(2):
+            if r or b:
+                to = net.at(r, b)
+                small.append((net.group(-r, b), net.push(blocks.at[to[0]], blocks_out.at[me], to)))
     give.step()
     give.end()
+    for g, k in small:
+        net.arrived(blocks_out.at[g], k)
     net.finish()
-
-
-def gather_tensor(own, groups, tensors, ident):
+    mine.wait()
+
+
+def gather_tensor(own, blocks, groups, tensors, ident):
     m, width = own.shape
     return pl.pallas_call(
         functools.partial(gather_tensor_kernel, groups // 2),
-        out_shape=jax.ShapeDtypeStruct((tensors, m, width), own.dtype),
+        out_shape=[
+            jax.ShapeDtypeStruct((tensors, m, width), own.dtype),
+            jax.ShapeDtypeStruct(blocks.shape, blocks.dtype),
+        ],
+        in_specs=[ANY] * 2,
+        out_specs=[ANY] * 2,
+        scratch_shapes=semaphores(2 + groups, 2),
+        compiler_params=params(ident, 16),
+        cost_estimate=cost(25),
+    )(own, blocks)
+
+
+def reduce_rows_kernel(far, part, out, *scratch):
+    net = Net(far, *scratch[-3:])
+    sums = ReduceAll(net, lambda s: part.at[s], *scratch[:5], "xy")
+    sums.load()
+    net.greet(net.near())
+    sums.start()
+    pipelined(far, [sums])
+    sums.end()
+
+    @pl.loop(0, out.shape[0] // 16)
+    def _(i):
+        rows = pl.ds(pl.multiple_of(i * 16, 16), 16)
+        out[rows, :] = sums.total(rows)
+
+    net.finish()
+
+
+def reduce_rows(part, groups, ident):
+    far = groups // 2
+    return pl.pallas_call(
+        functools.partial(reduce_rows_kernel, far),
+        out_shape=jax.ShapeDtypeStruct(part.shape[1:], F32),
         in_specs=[ANY],
-        out_specs=ANY,
-        scratch_shapes=semaphores(3, 1),
-        compiler_params=params(ident, 16),
-        cost_estimate=cost(16),
-    )(own)
+        out_specs=IN_VMEM,
+        scratch_shapes=ReduceAll.scratch(far, *part.shape[1:]) + semaphores(12 * far, 4 * far),
+        compiler_params=params(ident),
+        cost_estimate=cost(90),
+    )(part)
+
+
+def cells(groups, tensors):
+    across = 8 if groups * tensors <= 32 else 16
+    return groups * tensors // across, across
 
 
 def finish_kernel(far, *refs):
-    (gq, gkv, gout, small, blocks, dxn, dresid, normed, scale, gain) = refs[:10]
-    (oq, okv, oout, osmall, oblocks, otokens) = refs[10:16]
-    scratch = list(refs[16:])
+    (gq, gkv, gout, latent, misc, dxn, ffn, dresid, normed, scale, gain, resid, live) = refs[:13]
+    (oq, okv, oout, osmall, otokens, ooutput) = refs[13:19]
+    scratch = list(refs[19:])
     net = Net(far, *scratch[-3:])
 
     def take(n):
@@ -534,102 +608,150 @@
         return got
 
     weights = [ReduceGroups(net, p, o, *take(3)) for p, o in ((gq, oq), (gkv, okv), (gout, oout))]
-    cols = 2 * far * 4 // 8
-    tall, wide = small.shape[0] // 8, small.shape[1] // cols
-
-    def block(ref):
+    down, across = cells(2 * far, 4)
+    tall, wide = osmall.shape[0] // down, osmall.shape[1] // across
+    tall_latent, tall_misc = latent.shape[0] // down, misc.shape[0] // down
+
+    def cell(ref):
         def at(s):
-            down = pl.ds(pl.multiple_of(s // cols * tall, 16), tall)
-            return ref.at[down, pl.ds(pl.multiple_of(s % cols * wide, 128), wide)]
+            here = pl.ds(pl.multiple_of(s // across * tall, 16), tall)
+            return ref.at[here, pl.ds(pl.multiple_of(s % across * wide, 128), wide)]
 
         return at
 
-    sums = ReduceAll(net, block(small), *take(5), "xy")
+    summed = len(ffn.shape) == 2
+    small, sum_own, tokens_own, output_own = scratch[-7:-3]
+    sums = ReduceAll(net, cell(small), *take(5), "xy")
     rows_back = ReduceTensor(net, dxn, *take(3))
-    sum_own, tokens_own = take(2)
-    every = GatherAll(net, sum_own, block(osmall), "yx")
+    ffns = Summed(ffn) if summed else ReduceAll(net, lambda s: ffn.at[s], *take(5), "xy")
+    give_output = GatherTensor(net, output_own, ooutput)
+    every = GatherAll(net, sum_own, cell(osmall), "yx")
     give_tokens = GatherTensor(net, tokens_own, otokens)
-    for part in (rows_back, sums, *weights):
+    moved = []
+    for k in range(down):
+        here = pl.ds(k * tall, tall_latent)
+        moved.append(net.load(latent.at[pl.ds(k * tall_latent, tall_latent)], small.at[here]))
+        here = pl.ds(k * tall + tall_latent, tall_misc)
+        moved.append(net.load(misc.at[pl.ds(k * tall_misc, tall_misc)], small.at[here]))
+    for part in (rows_back, *weights, ffns):
         part.load()
-    me = net.group()
-    mine = [net.load(blocks.at[me], oblocks.at[me])]
-    net.greet(net.line() + [net.x, net.core])
-    for part in (rows_back, sums, *weights):
-        part.start()
-    rows_back.step()
-    for i in range(far):
-        sums.stage_a(i)
-    for i in range(far):
-        sums.stage_b(i)
-    for i in range(far):
-        weights[0].step(i)
-    rows_back.end()
-
-    @pl.loop(0, tokens_own.shape[0] // 16)
-    def _(i):
-        rows = pl.ds(pl.multiple_of(i * 16, 16), 16)
+    mine = []
+    net.greet(net.near())
+
+    def send_weights(r):
+        for part in weights:
+            part.start(r)
+
+    def step_weights(r):
+        for part in weights:
+            part.step(r)
+
+    def each(count, body):
+        @pl.loop(0, count // 16)
+        def _(i):
+            body(pl.ds(pl.multiple_of(i * 16, 16), 16))
+
+    def tokens_rows(rows):
         n = normed[rows, :]
         weighted = rows_back.total(rows) * gain[...]
         mean = jnp.mean(weighted * n, axis=-1, keepdims=True)
         back = scale[rows, :] * (weighted - n * mean)
         tokens_own[rows, :] = (dresid[rows, :] + back).astype(BF16)
 
+    def output_rows(rows):
+        output_own[rows, :] = (resid[rows, :] + live[rows, :] * ffns.total(rows)).astype(BF16)
+
+    def sum_rows(rows):
+        sum_own[rows, :] = sums.total(rows).astype(BF16)
+
+    turn = list(range(far - 1, -1, -1))
+    rows_back.start()
+    for copy in moved:
+        copy.wait()
+    sums.load()
+    sums.start()
+    ffns.start()
+    send_weights(turn[0])
+    rows_back.step()
+    for i in range(far):
+        sums.stage_a(i)
+    ffns.stage_a(0)
+    send_weights(turn[1])
+    for i in range(far):
+        sums.stage_b(i)
+    rows_back.end()
+    each(tokens_own.shape[0], tokens_rows)
     give_tokens.start()
+    ffns.stage_a(1)
     for i in range(far):
         sums.stage_c(i)
-    small_tokens = []
-    for r in range(far):
-        for b in range(2):
-            if r or b:
-                to = net.at(r, b)
-                k = net.push(blocks.at[to[0]], oblocks.at[me], to)
-                small_tokens.append((net.group(-r, b), k))
+    for k in range(far - 2):
+        step_weights(turn[k])
+        send_weights(turn[k + 2])
+        ffns.stage_b(k)
+        ffns.stage_a(k + 2)
     sums.end()
-
-    @pl.loop(0, sum_own.shape[0] // 16)
-    def _(i):
-        rows = pl.ds(pl.multiple_of(i * 16, 16), 16)
-        sum_own[rows, :] = sums.total(rows).astype(BF16)
-
-    mine.append(net.load(sum_own, block(osmall)(net.slot())))
+    each(sum_own.shape[0], sum_rows)
+    mine.append(net.load(sum_own, cell(osmall)(net.slot())))
     every.start()
-    for part in weights[1:]:
-        for i in range(far):
-            part.step(i)
+    every.stage_a(0)
+    step_weights(turn[far - 2])
+    for k in range(far - 2):
+        ffns.stage_c(k)
     give_tokens.step()
-    pipelined(far, [every])
-    for part in (*weights, give_tokens, every):
+    every.stage_b(0)
+    every.stage_c(0)
+    ffns.stage_b(far - 2)
+    for r in range(1, far):
+        every.stage_a(r)
+    step_weights(turn[far - 1])
+    for r in range(1, far):
+        every.stage_b(r)
+    ffns.stage_c(far - 2)
+    ffns.stage_b(far - 1)
+    for r in range(1, far):
+        every.stage_c(r)
+    ffns.stage_c(far - 1)
+    ffns.end()
+    each(output_own.shape[0], output_rows)
+    give_output.start()
+    for part in weights:
         part.end()
-    for g, k in small_tokens:
-        net.arrived(oblocks.at[g], k)
+    give_output.step()
+    for part in (give_tokens, every, give_output):
+        part.end()
     net.finish()
     for copy in mine:
         copy.wait()
 
 
-def finish(weights, small, blocks, dxn, dresid, normed, scale, gain, groups, tensors, ident):
+def finish(weights, latent, misc, dxn, ffn, rows, groups, tensors, ident):
     far = groups // 2
-    m, width = dresid.shape
+    m, width = rows[0].shape
+    down, across = cells(groups, tensors)
+    size = (latent.shape[0] + misc.shape[0], width)
+    cell = (size[0] // down, width // across)
     outs = [jax.ShapeDtypeStruct(w.shape[1:], F32) for w in weights]
-    outs.append(jax.ShapeDtypeStruct(small.shape, BF16))
-    outs.append(jax.ShapeDtypeStruct(blocks.shape, BF16))
-    outs.append(jax.ShapeDtypeStruct((tensors, m, width), BF16))
+    outs.append(jax.ShapeDtypeStruct(size, BF16))
+    outs += [jax.ShapeDtypeStruct((tensors, m, width), BF16)] * 2
     scratch = []
     for w in weights:
         scratch += ReduceGroups.scratch(far, *w.shape[1:])
-    cell = (small.shape[0] // 8, small.shape[1] // (groups * tensors // 8))
     scratch += ReduceAll.scratch(far, *cell)
     scratch += ReduceTensor.scratch(m, width)
-    scratch += [pltpu.VMEM(cell, BF16), pltpu.VMEM((m, width), BF16)]
+    if len(ffn.shape) == 3:
+        scratch += ReduceAll.scratch(far, *ffn.shape[1:])
+    scratch += [pltpu.VMEM(size, BF16), pltpu.VMEM(cell, BF16)]
+    scratch += [pltpu.VMEM((m, width), BF16)] * 2
     return pl.pallas_call(
         functools.partial(finish_kernel, far),
         out_shape=outs,
-        in_specs=[ANY] * 6 + [IN_VMEM] * 4,
+        in_specs=[ANY] * 6 + [ANY if len(ffn.shape) == 3 else IN_VMEM] + [IN_VMEM] * 6,
         out_specs=[IN_VMEM] * 3 + [ANY] * 3,
-        scratch_shapes=scratch + semaphores(40 * far, 10 * far + 10),
+        scratch_shapes=scratch + semaphores(50 * far, 14 * far + 30),
         compiler_params=params(ident),
-        cost_estimate=cost(150),
-    )(*weights, small, blocks, dxn, dresid, normed, scale, gain)
+        cost_estimate=cost(110),
+    )(*weights, latent, misc, dxn, ffn, *rows)
 
 
 TILE = 32
@@ -641,20 +763,232 @@
 
 def dot_nn(left, right):
     return lax.dot_general(left, right, (((1,), (0,)), ((), ())), preferred_element_type=F32)
+
+
+def swap_halves(v):
+    half = v.shape[1] // 2
+    return jnp.concatenate([v[:, half:], v[:, :half]], axis=1)
+
+
+def attend_kernel(
+    heads,
+    tokens, gain, w_query, w_latent, gain_lat, w_kv, w_out, cosine, sine,
+    partial, xn1, qcat, kv, key_rope, probs, attended, normed_lat, scale_lat, compressed, scale_one,
+    q_raw, latent,
+):
+    rows, width = tokens.shape
+    blocks = w_out.shape[0]
+    step = width // blocks
+
+    @pl.loop(0, rows // 64)
+    def _(i):
+        at = pl.ds(pl.multiple_of(i * 64, 64), 64)
+        v = tokens[at, :].astype(F32)
+        scale = lax.rsqrt(jnp.mean(v * v, axis=-1, keepdims=True) + EPS)
+        scale_one[at, :] = scale
+        xn1[at, :] = (v * scale * gain[...]).astype(BF16)
+
+    latent[...] = dot_nt(xn1[...], w_latent[...])
+    q_raw[...] = dot_nn(xn1[...], w_query[...])
+
+    @pl.loop(0, rows // 128)
+    def _(i):
+        at = pl.ds(pl.multiple_of(i * 128, 128), 128)
+        v = latent[at, :KVR]
+        scale = lax.rsqrt(jnp.mean(v * v, axis=-1, keepdims=True) + EPS)
+        scale_lat[at, :] = scale
+        normed = v * scale
+        normed_lat[at, :] = normed
+        compressed[at, :] = (normed * gain_lat[...]).astype(BF16)
+        rope = latent[at, KVR:]
+        c, s = cosine[at, :], sine[at, :]
+        key_rope[at, :] = (rope * c + swap_halves(rope) * s).astype(BF16)
+        for h in range(heads):
+            base = h * (NOPE + ROPE)
+            qcat[h, at, :NOPE] = q_raw[at, base : base + NOPE].astype(BF16)
+            rope = q_raw[at, base + NOPE : base + NOPE + ROPE]
+            qcat[h, at, NOPE:] = (rope * c + swap_halves(rope) * s).astype(BF16)
+
+    kv[...] = dot_nn(compressed[...], w_kv[...]).astype(BF16)
+    score_scale = (NOPE + ROPE) ** (-0.5)
+    for h in range(heads):
+        base = h * (NOPE + VD)
+
+        @pl.loop(0, rows // 128)
+        def _(i):
+            at = pl.ds(pl.multiple_of(i * 128, 128), 128)
+            score = dot_nt(qcat[h, at, :NOPE], kv[:, base : base + NOPE])
+            score = (score + dot_nt(qcat[h, at, NOPE:], key_rope[...])) * score_scale
+            mine = lax.broadcasted_iota(jnp.int32, score.shape, 0) + i * 128
+            seen = lax.broadcasted_iota(jnp.int32, score.shape, 1) <= mine
+            score = jnp.where(seen, score, -1e30)
+            expo = jnp.exp(score - jnp.max(score, axis=-1, keepdims=True))
+            prob = (expo / jnp.sum(expo, axis=-1, keepdims=True)).astype(BF16)
+            probs[h, at, :] = prob
+            out = dot_nn(prob, kv[:, base + NOPE : base + NOPE + VD])
+            attended[at, h * VD : (h + 1) * VD] = out.astype(BF16)
+
+    for e in range(blocks):
+        partial[:, e * step : (e + 1) * step] = dot_nn(attended[...], w_out[e]).astype(BF16)
+
+
+def attend(tokens, gain, w_query, w_latent, gain_lat, w_kv, w_out, cosine, sine):
+    rows, width = tokens.shape
+    heads = w_out.shape[1] // VD
+    like = jax.ShapeDtypeStruct
+    outs = [
+        like((rows, width), BF16),
+        like((rows, width), BF16),
+        like((heads, rows, NOPE + ROPE), BF16),
+        like((rows, w_kv.shape[1]), BF16),
+        like((rows, ROPE), BF16),
+        like((heads, rows, rows), BF16),
+        like((rows, heads * VD), BF16),
+        like((rows, KVR), F32),
+        like((rows, 1), F32),
+        like((rows, KVR), BF16),
+        like((rows, 1), F32),
+    ]
+    return pl.pallas_call(
+        functools.partial(attend_kernel, heads),
+        out_shape=outs,
+        in_specs=[IN_VMEM] * 9,
+        out_specs=[IN_VMEM] * 11,
+        scratch_shapes=[
+            pltpu.VMEM((rows, w_query.shape[1]), F32),
+            pltpu.VMEM((rows, w_latent.shape[0]), F32),
+        ],
+        compiler_params=pltpu.CompilerParams(vmem_limit_bytes=60 * 2**20),
+        cost_estimate=cost(20),
+    )(tokens, gain, w_query, w_latent, gain_lat, w_kv, w_out, cosine, sine)
+
+
+def attend_back_kernel(
+    heads,
+    dattn, tokens, xn1, qcat, kv, key_rope, probs, attended, normed_lat, scale_lat, compressed, scale_one,
+    w_query, w_latent, gain_lat, w_kv, w_out, cosine, sine,
+    g_query, g_kv, g_out, g_latent, g_gain, g_gain_lat, dxn,
+    dattended, dscore, dq, dkv, dkr, dlatent, turned, dcomp,
+):
+    rows, width = tokens.shape
+    blocks = w_out.shape[0]
+    step = width // blocks
+    total = jnp.zeros((rows, heads * VD), F32)
+    for e in range(blocks):
+        total = total + dot_nt(dattn[:, e * step : (e + 1) * step], w_out[e])
+    dattended[...] = total.astype(BF16)
+    turned_att = attended[...].T
+    for e in range(blocks):
+        g_out[e] = dot_nn(turned_att, dattn[:, e * step : (e + 1) * step]).astype(BF16)
+    score_scale = (NOPE + ROPE) ** (-0.5)
+    for h in range(heads):
+        base, qbase = h * (NOPE + VD), h * (NOPE + ROPE)
+
+        @pl.loop(0, rows // 128)
+        def _(i):
+            at = pl.ds(pl.multiple_of(i * 128, 128), 128)
+            dprob = dot_nt(dattended[at, h * VD : (h + 1) * VD], kv[:, base + NOPE : base + NOPE + VD])
+            prob = probs[h, at, :].astype(F32)
+            along = prob * dprob
+            ds = (along - prob * jnp.sum(along, axis=-1, keepdims=True)) * score_scale
+            dscore[at, :] = ds.astype(BF16)
+
+        @pl.loop(0, rows // 128)
+        def _(i):
+            at = pl.ds(pl.multiple_of(i * 128, 128), 128)
+            ds = dscore[at, :]
+            dq[at, qbase : qbase + NOPE] = dot_nn(ds, kv[:, base : base + NOPE]).astype(BF16)
+            rope = dot_nn(ds, key_rope[...])
+            rope = rope * cosine[at, :] - swap_halves(rope) * sine[at, :]
+            dq[at, qbase + NOPE : qbase + NOPE + ROPE] = rope.astype(BF16)
+
+        turned_p = probs[h].T
+        dv = dot_nn(turned_p, dattended[:, h * VD : (h + 1) * VD])
+        dkv[:, base + NOPE : base + NOPE + VD] = dv.astype(BF16)
+        turned_s = dscore[...].T
+        dkv[:, base : base + NOPE] = dot_nn(turned_s, qcat[h, :, :NOPE]).astype(BF16)
+        rope = dot_nn(turned_s, qcat[h, :, NOPE:])
+        dkr[...] = rope if h == 0 else dkr[...] + rope
+
+    turned_c = compressed[...].T
+    g_kv[...] = dot_nn(turned_c, dkv[...]).astype(BF16)
+    dcomp[...] = dot_nt(dkv[...], w_kv[...])
+    dlatent[...] = jnp.zeros_like(dlatent)
+    g_gain_lat[...] = jnp.zeros_like(g_gain_lat)
+
+    @pl.loop(0, rows // 128)
+    def _(i):
+        at = pl.ds(pl.multiple_of(i * 128, 128), 128)
+        d, n = dcomp[at, :], normed_lat[at, :]
+        g_gain_lat[...] += jnp.sum(d * n, axis=0, keepdims=True)
+        weighted = d * gain_lat[...]
+        mean = jnp.mean(weighted * n, axis=-1, keepdims=True)
+        dlatent[at, :KVR] = (scale_lat[at, :] * (weighted - n * mean)).astype(BF16)
+        rope = dkr[at, :]
+        rope = rope * cosine[at, :] - swap_halves(rope) * sine[at, :]
+        dlatent[at, KVR : KVR + ROPE] = rope.astype(BF16)
+
+    turned[...] = dlatent[...].T
+    units = w_latent.shape[0]
+
+    @pl.loop(0, width // 512)
+    def _(c):
+        at = pl.ds(pl.multiple_of(c * 512, 512), 512)
+        g_query[at, :] = dot_nn(xn1[:, at].T, dq[...]).astype(BF16)
+        g_latent[:, at] = dot_nn(turned[:units, :], xn1[:, at]).astype(BF16)
+        d = dot_nt(dq[...], w_query[at, :]) + dot_nn(dlatent[:, :units], w_latent[:, at])
+        dxn[:, at] = d.astype(BF16)
+        normed = tokens[:, at].astype(F32) * scale_one[...]
+        g_gain[:, at] = jnp.sum(d * normed, axis=0, keepdims=True)
+
+
+def attend_back(dattn, tokens, kept, w_query, w_latent, gain_lat, w_kv, w_out, cosine, sine):
+    rows, width = tokens.shape
+    heads = w_out.shape[1] // VD
+    like = jax.ShapeDtypeStruct
+    units = w_latent.shape[0]
+    padded = -(-units // 128) * 128
+    outs = [
+        like(w_query.shape, BF16),
+        like(w_kv.shape, BF16),
+        like(w_out.shape, BF16),
+        like(w_latent.shape, BF16),
+        like((1, width), F32),
+        like((1, KVR), F32),
+        like((rows, width), BF16),
+    ]
+    return pl.pallas_call(
+        functools.partial(attend_back_kernel, heads),
+        out_shape=outs,
+        in_specs=[IN_VMEM] * 19,
+        out_specs=[IN_VMEM] * 7,
+        scratch_shapes=[
+            pltpu.VMEM((rows, heads * VD), BF16),
+            pltpu.VMEM((rows, rows), BF16),
+            pltpu.VMEM((rows, w_query.shape[1]), BF16),
+            pltpu.VMEM((rows, w_kv.shape[1]), BF16),
+            pltpu.VMEM((rows, ROPE), F32),
+            pltpu.VMEM((rows, padded), BF16),
+            pltpu.VMEM((padded, rows), BF16),
+            pltpu.VMEM((rows, KVR), F32),
+        ],
+        compiler_params=pltpu.CompilerParams(vmem_limit_bytes=62 * 2**20),
+        cost_estimate=cost(40),
+    )(dattn, tokens, *kept, w_query, w_latent, gain_lat, w_kv, w_out, cosine, sine)
 
 
 def experts_kernel(sizes, *refs):
     far, experts, hidden, shared, total = sizes
     groups = 2 * far
-    (x_own, dy_all, picks, wg_hbm, wu_hbm, wd_hbm, ws_hbm, wr_hbm) = refs[:8]
-    (outs_hbm, dg_out, gg_hbm, gu_hbm, gd_hbm, gs_hbm, x_all, ffn_all) = refs[8:16]
-    (core_in, x0_in, y1_in, y0_in, x1_in, z_in) = refs[16:22]
-    (w_in, w_down, h, dh, hs, dgu, hsn, dgun, acc_in, acc_down, x, dy) = refs[22:34]
-    (part, ffn_part, acc, own, stage1, stage2, stage3, stage4, dg, dg_in, dg_sum) = refs[34:45]
+    (x_own, dy_own, dy_near, picks, wg_hbm, wu_hbm, wd_hbm, ws_hbm, wr_hbm) = refs[:9]
+    (outs_hbm, dg_out, gg_hbm, gu_hbm, gd_hbm, gs_hbm, x_all, dy_all, ffn_all) = refs[9:18]
+    (core_in, x0_in, y1_in, y0_in, x1_in, z_in) = refs[18:24]
+    (w_in, w_down, h, dh, hs, dgu, hsn, dgun, acc_in, acc_down, x, dy) = refs[24:36]
+    (part, ffn_part, acc, own, stage1, stage2, stage3, stage4, dg, dg_in, dg_sum) = refs[36:47]
     (
         ag_s, ag_r, core_s, core_r, x0_s, x0_r, y1_s, y1_r, y0_s, y0_r, x1_s, x1_r, z_s, z_r,
         dg_s, dg_r, wsem, lsem, csem,
-    ) = refs[45:]
+    ) = refs[47:]
     routed = experts * hidden
     units = routed + shared
     m, width = x_own.shape
@@ -675,47 +1009,63 @@
 
     links = ((net.y, net.x), (net.x, net.y))
 
-    def place(p, r, u, v, d=0):
+    def place(q, r, u, v, d=0):
+        p = q % 2
         b, c = (u, v) if p == 0 else (v, u)
-        return x_all.at[net.slot(-r, b, c, d), (low, high)[p]]
-
-    def pass_on(p, kind, r, u, v, to):
-        ref = place(p, r, u, v)
-        remote(ref, ref, ag_s.at[p, kind, r], ag_r.at[p, kind, r], to).start()
+        return (x_all, dy_all)[q // 2].at[net.slot(-r, b, c, d), (low, high)[p]]
+
+    def pass_on(q, kind, r, u, v, to):
+        ref = place(q, r, u, v)
+        remote(ref, ref, ag_s.at[q, kind, r], ag_r.at[q, kind, r], to).start()
+
+    def flows(r):
+        return range(2 if isinstance(r, int) and r == 0 else 4)
+
+    def rows_z(r):
+        for q in range(4):
+            ref = place(q, 0, 0, 0)
+            src = ref if q < 2 else dy_own.at[net.at()[1], (low, high)[q % 2]]
+            remote(src, ref, ag_s.at[q, 0, r], ag_r.at[q, 0, r], net.at(r)).start()
 
     def rows_a(r):
-        for p in both:
-            pl.when(r > 0)(lambda: wait_for(place(p, r, 0, 0), ag_r.at[p, 0, r]))
-            pass_on(p, 1, r, 0, 0, links[p][0])
-            pass_on(p, 2, r, 0, 0, links[p][1])
-            pass_on(p, 4, r, 0, 0, net.core)
+        for q in flows(r):
+            if len(flows(r)) == 4:
+                wait_for(place(q, r, 0, 0), ag_r.at[q, 0, r])
+            pass_on(q, 1, r, 0, 0, links[q % 2][0])
+            pass_on(q, 2, r, 0, 0, links[q % 2][1])
+            pass_on(q, 4, r, 0, 0, net.core)
 
     def rows_b(r):
-        for p in both:
-            wait_for(place(p, r, 1, 0), ag_r.at[p, 1, r])
-            pass_on(p, 3, r, 1, 0, links[p][1])
-            pass_on(p, 6, r, 1, 0, net.core)
+        for q in flows(r):
+            wait_for(place(q, r, 1, 0), ag_r.at[q, 1, r])
+            pass_on(q, 3, r, 1, 0, links[q % 2][1])
+            pass_on(q, 6, r, 1, 0, net.core)
 
     def rows_c(r):
-        for p in both:
+        for q in flows(r):
             for u in both:
-                wait_for(place(p, r, u, 1), ag_r.at[p, 2 + u, r])
-                pass_on(p, 5 + 2 * u, r, u, 1, net.core)
+                wait_for(place(q, r, u, 1), ag_r.at[q, 2 + u, r])
+                pass_on(q, 5 + 2 * u, r, u, 1, net.core)
 
     def rows_d(r):
-        for p in both:
+        for q in flows(r):
             for u in both:
                 for v in both:
-                    wait_for(place(p, r, u, v, 1), ag_r.at[p, 4 + 2 * u + v, r])
+                    wait_for(place(q, r, u, v, 1), ag_r.at[q, 4 + 2 * u + v, r])
+
+    def block_copies(s, dy_from):
+        g = net.group(-(s // 2), 1 - s % 2)
+        copies = []
+        for t in range(4):
+            here = pl.ds(t * m, m)
+            copies.append(pltpu.make_async_copy(x_all.at[g * 4 + t], x.at[here], lsem.at[t]))
+            source = dy_all.at[g * 4 + t] if dy_from is None else dy_from.at[t]
+            copies.append(pltpu.make_async_copy(source, dy.at[here], lsem.at[4 + t]))
+        return copies
 
     def load_block(s):
-        g = net.group(-(s // 2), 1 - s % 2)
-        copies = [
-            pltpu.make_async_copy(x_all.at[g * 4 + t], x.at[pl.ds(t * m, m)], lsem.at[t])
-            for t in range(4)
-        ]
-        rows = pl.ds(pl.multiple_of(g * block, block), block)
-        return copies + [pltpu.make_async_copy(dy_all.at[rows], dy, lsem.at[4])]
+        pl.when(s == 1)(lambda: begin_all(block_copies(s, dy_own)))
+        pl.when(s > 1)(lambda: begin_all(block_copies(s, None)))
 
     def mine(c, d):
         t = net.at(0, 0, c, d)[1]
@@ -724,7 +1074,7 @@
     def ffn_copy(s):
         g = net.group(-(s // 2), 1 - s % 2)
         rows = pl.ds(pl.multiple_of(g * block, block), block)
-        return pltpu.make_async_copy(ffn_part, ffn_all.at[rows], lsem.at[5])
+        return pltpu.make_async_copy(ffn_part, ffn_all.at[rows], lsem.at[8])
 
     def core_push(s, a, c):
         return remote(
@@ -732,25 +1082,25 @@
         )
 
     def x0_push(s, a):
-        return remote(acc.at[a, s % 3, 1, low], x0_in.at[a, s], x0_s.at[a, s], x0_r.at[a, s], net.x)
+        return remote(acc.at[a, s % 5, 1, low], x0_in.at[a, s], x0_s.at[a, s], x0_r.at[a, s], net.x)
 
     def y1_push(s, a, c):
         r = s // 2
         return remote(
-            acc.at[a, s % 3, c, high], y1_in.at[a, r, c], y1_s.at[a, r, c], y1_r.at[a, r, c], net.y
+            acc.at[a, s % 5, c, high], y1_in.at[a, r, c], y1_s.at[a, r, c], y1_r.at[a, r, c], net.y
         )
 
     def y0_push(s, a):
         r = s // 2
-        return remote(acc.at[a, s % 3, 0, low], y0_in.at[a, r], y0_s.at[a, r], y0_r.at[a, r], net.y)
+        return remote(acc.at[a, s % 5, 0, low], y0_in.at[a, r], y0_s.at[a, r], y0_r.at[a, r], net.y)
 
     def x1_push(s, a):
         r = s // 2
-        return remote(acc.at[a, s % 3, 1, high], x1_in.at[a, r], x1_s.at[a, r], x1_r.at[a, r], net.x)
+        return remote(acc.at[a, s % 5, 1, high], x1_in.at[a, r], x1_s.at[a, r], x1_r.at[a, r], net.x)
 
     def z_push(s, a):
         r = s // 2
-        return remote(acc.at[a, s % 3, 0], z_in.at[a, r], z_s.at[a, r], z_r.at[a, r], net.at(-r))
+        return remote(acc.at[a, s % 5, 0], z_in.at[a, r], z_s.at[a, r], z_r.at[a, r], net.at(-r))
 
     def copy_in(ref, buf, sem, k):
         return pltpu.make_async_copy(ref, buf, sem.at[k])
@@ -802,7 +1152,7 @@
 
     def h1_post(s):
         wait_all(h1_loads(s))
-        pl.when(s > 2)(lambda: sends_done(s - 3))
+        pl.when(s > 4)(lambda: sends_done(s - 5))
         for a in sums:
             for c in (1, 0):
                 base = mine(c, 0).start
@@ -811,7 +1161,7 @@
                 def _(i):
                     rows = pl.ds(pl.multiple_of(i * 16, 16), 16)
                     there = pl.ds(pl.multiple_of(base + i * 16, 16), 16)
-                    acc[a, s % 3, c, rows, :] = part[a, there, :] + stage1[a, c, rows, :]
+                    acc[a, s % 5, c, rows, :] = part[a, there, :] + stage1[a, c, rows, :]
 
             x0_push(s, a).start()
 
@@ -826,7 +1176,7 @@
         def _(i):
             rows = pl.ds(pl.multiple_of(base + i * 16, 16), 16)
             there = pl.ds(pl.multiple_of(i * 16, 16), 16)
-            acc[a, s % 3, c, rows, :] = acc[a, s % 3, c, rows, :] + buf[there, :]
+            acc[a, s % 5, c, rows, :] = acc[a, s % 5, c, rows, :] + buf[there, :]
 
     def h2_pre(s):
         for a in sums:
@@ -897,11 +1247,8 @@
     first.start()
     net.greet(net.line() + [net.at(c=c, d=d) for c, d in ((0, 1), (1, 0), (1, 1))])
     first.wait()
-    for r in range(1, far):
-        for p in both:
-            ref = place(p, 0, 0, 0)
-            remote(ref, ref, ag_s.at[p, 0, r], ag_r.at[p, 0, r], net.at(r)).start()
     rows_a(0)
+    rows_z(1)
     begin_all(weights())
     acc_in[...] = jnp.zeros_like(acc_in)
     acc_down[...] = jnp.zeros_like(acc_down)
@@ -911,7 +1258,7 @@
     rows_b(0)
     rows_c(0)
     rows_d(0)
-    begin_all(load_block(0))
+    begin_all(block_copies(0, dy_near))
     wait_all(weights())
 
     @pl.loop(0, groups)
@@ -920,10 +1267,10 @@
         g = net.group(-r, 1 - s % 2)
         more = r + 1 < far
         pl.when((s % 2 == 0) & more)(lambda: rows_a(r + 1))
-        pl.when((s % 2 == 1) & more)(lambda: rows_c(r + 1))
+        pl.when((s % 2 == 0) & (r + 2 < far))(lambda: rows_z(r + 2))
         pl.when(s > 0)(lambda: h1_pre(s - 1))
-        pl.when(s > 1)(lambda: h2_pre(s - 2))
-        wait_all(load_block(s))
+        pl.when(s > 2)(lambda: h2_pre(s - 3))
+        wait_all(block_copies(s, None))
 
         @pl.loop(0, block // chunk)
         def _(n):
@@ -959,9 +1306,9 @@
                         dg[n * per + j, g, e : e + 1, :] = row[:, j * m : (j + 1) * m]
 
         pl.when(s > 0)(lambda: h1_post(s - 1))
-        pl.when(s > 1)(lambda: h2_post(s - 2))
-        pl.when((s > 2) & (s % 2 == 0))(lambda: h3_pre(s - 3))
-        pl.when((s % 2 == 0) & more)(lambda: rows_b(r + 1))
+        pl.when(s > 2)(lambda: h2_post(s - 3))
+        pl.when((s > 4) & (s % 2 == 0))(lambda: h3_pre(s - 5))
+        pl.when((s % 2 == 1) & more)(lambda: rows_c(r + 1))
 
         @pl.loop(0, width // 512)
         def _(c):
@@ -969,9 +1316,9 @@
             acc_in[:, at] += dot_nn(dgu[: 2 * units, :], x[:, at])
             acc_down[:, at] += dot_nn(hs[:units, :], dy[:, at])
 
-        pl.when((s > 2) & (s % 2 == 0))(lambda: h3_post(s - 3))
+        pl.when((s > 4) & (s % 2 == 0))(lambda: h3_post(s - 5))
         pl.when((s % 2 == 1) & more)(lambda: rows_d(r + 1))
-        pl.when(s + 1 < groups)(lambda: begin_all(load_block(s + 1)))
+        pl.when(s + 1 < groups)(lambda: load_block(s + 1))
         hsn[...] = hs[...].T
         dgun[...] = dgu[...].T
 
@@ -995,6 +1342,7 @@
             ffn_part[:, at] = dot_nn(hsn[:, :units], w_down[:, at]).astype(BF16)
 
         ffn_copy(s).start()
+        pl.when((s % 2 == 0) & more)(lambda: rows_b(r + 1))
 
     def stores():
         pairs = []
@@ -1019,10 +1367,14 @@
         dg_push(k).start()
     last = groups - 1
     h1_pre(last)
-    h2_pre(last - 1)
+    h2_pre(last - 2)
     h1_post(last)
     begin_all(stores())
+    h2_post(last - 2)
+    h2_pre(last - 1)
     h2_post(last - 1)
+    h3_pre(last - 4)
+    h3_post(last - 4)
     h3_pre(last - 2)
     h3_post(last - 2)
     for k in range(3):
@@ -1059,16 +1411,16 @@
     for k in range(len(others)):
         r, b = others[k]
         wait_for(dg_out.at[net.group(-r, b)], dg_r.at[3 + k])
-    for s in range(last - 2, last + 1):
+    for s in range(last - 4, last + 1):
         sends_done(s)
     for c in both:
         core_push(last, 0, c).wait_send()
     ffn_copy(last).wait()
-    for p in both:
+    for q in range(4):
         for r in range(far):
             for kind in range(8):
-                if r or kind:
-                    wait_for(place(p, 0, 0, 0), ag_s.at[p, kind, r])
+                if r or (kind and q < 2):
+                    wait_for(place(q, 0, 0, 0), ag_s.at[q, kind, r])
     for k in range(3):
         dg_push(k).wait_send()
     for k in range(len(others)):
@@ -1077,7 +1429,7 @@
     give.wait()
 
 
-def experts_all(x, dy, picks, wg, wu, wd, ws, wr, groups, tensors, ident):
+def experts_all(x, dy_own, dy_near, picks, wg, wu, wd, ws, wr, groups, tensors, ident):
     m, width = x.shape
     far = groups // 2
     experts, hidden, _ = wg.shape
@@ -1094,6 +1446,7 @@
         like(wu.shape, F32),
         like(wd.shape, F32),
         like(ws.shape, F32),
+        like((groups * tensors, m, width), BF16),
         like((groups * tensors, m, width), BF16),
         like((groups * block, width), BF16),
         like((1, groups, 2, m, width), BF16),
@@ -1119,7 +1472,7 @@
         pltpu.VMEM((block, width), BF16),
         pltpu.VMEM((1, block, width), BF16),
         pltpu.VMEM((block, width), BF16),
-        pltpu.VMEM((1, 3, 2, m, width), BF16),
+        pltpu.VMEM((1, 5, 2, m, width), BF16),
         pltpu.VMEM((1, m, width), BF16),
         pltpu.VMEM((1, 2, m, width), BF16),
         pltpu.VMEM((1, half, width), BF16),
@@ -1130,20 +1483,20 @@
         pltpu.VMEM((groups, 8, m), F32),
     ]
     for shape in (
-        (2, 8, far), (1, groups, 2), (1, groups), (1, far, 2), (1, far), (1, far), (1, far), (groups + 2,),
+        (4, 8, far), (1, groups, 2), (1, groups), (1, far, 2), (1, far), (1, far), (1, far), (groups + 2,),
     ):
         scratch += [dma(shape), dma(shape)]
-    scratch += [dma((3 * experts + 4,)), dma((6,)), dma((10,))]
+    scratch += [dma((3 * experts + 4,)), dma((9,)), dma((10,))]
     got = pl.pallas_call(
         functools.partial(experts_kernel, (far, experts, hidden, shared, total)),
         out_shape=outs,
-        in_specs=[ANY, ANY, IN_VMEM] + [ANY] * 5,
-        out_specs=[ANY, IN_VMEM] + [ANY] * 12,
+        in_specs=[ANY] * 3 + [IN_VMEM] + [ANY] * 5,
+        out_specs=[ANY, IN_VMEM] + [ANY] * 13,
         scratch_shapes=scratch,
         compiler_params=params(ident, 63),
         cost_estimate=cost(280),
-    )(x, dy, picks, wg, wu, wd, ws, wr)
-    return [*got[:6], got[7]]
+    )(x, dy_own, dy_near, picks, wg, wu, wd, ws, wr)
+    return [*got[:6], got[8]]
 
 
 BOTH = ("expert", "tensor")
@@ -1187,7 +1540,8 @@
     live = live_int.astype(f32)[:, None]
     live_own = own(live)
     cot_own = own(cotangent).astype(f32)
-    dffn_own = (cot_own * live_own).astype(bf16)
+    dffn_group = (cotangent * live.astype(bf16)).reshape(tensors, quarter, width)
+    dffn_own = own(cotangent) * live_own.astype(bf16)
 
     part = w_shared_down.shape[0] // groups
     spare = -part % TILE
@@ -1201,16 +1555,17 @@
     )
     choose = jnp.any(routes[..., None] == jnp.arange(total_experts), axis=1).astype(F32)
     picks = choose * live
-    query_w, kv_up, out_proj, shared_w, marks = begin(
+    query_w, kv_up, out_proj, shared_w, marks, dffn_near = begin(
         (w_query, w_kv, w_out),
         shared_w.reshape(groups, -1, shared_w.shape[-1]),
         picks.T.astype(BF16),
+        dffn_own,
         groups,
+        tensors,
         0,
     )
     query_w = query_w.reshape(width, -1)
     kv_up = kv_up.reshape(KVR, -1)
-    out_proj = out_proj.transpose(1, 0, 2).reshape(-1, width)
     shared_w = shared_w.transpose(1, 0, 2).reshape(3, part + spare, width)
     gate_t, up_t = w_gate.transpose(0, 2, 1), w_up.transpose(0, 2, 1)
     router_t = jnp.roll(w_router.T, -eindex * experts_local, axis=0)
@@ -1223,46 +1578,15 @@
     marks = marks.reshape(groups, total_experts, tensors, parts, some).transpose(3, 1, 0, 2, 4)
     picks_all = marks.reshape(parts, total_experts, -1).astype(F32)
     picks_all = jnp.roll(picks_all, -eindex * experts_local, axis=1)
-    dffn = [lax.all_gather(v, BOTH, axis=0, tiled=True) for v in split(dffn_own)]
-
-    heads = out_proj.shape[0] // VD
     xf = tokens.astype(f32)
-    scale_one = inv_rms(xf)
-    normed_one = xf * scale_one
-    xn1 = (normed_one * gain_attn).astype(bf16)
     cosine, sine = rope_tables(rows, ROPE)
-    qfull = mat(xn1, query_w).reshape(rows, heads, NOPE + ROPE)
-    qcat = jnp.concatenate(
-        [qfull[..., :NOPE], rotate(qfull[..., NOPE:], cosine[:, None, :], sine[:, None, :])],
-        axis=-1,
-    ).astype(bf16)
-    latent = mat(xn1, w_latent)
-    comp = latent[:, :KVR]
-    scale_lat = inv_rms(comp)
-    normed_lat = comp * scale_lat
-    compressed = (normed_lat * gain_latent).astype(bf16)
-    key_rope = rotate(latent[:, KVR:], cosine, sine).astype(bf16)
-    key_value = mat(compressed, kv_up).astype(bf16).reshape(rows, heads, NOPE + VD)
-    keys = jnp.concatenate(
-        [key_value[..., :NOPE], jnp.broadcast_to(key_rope[:, None, :], (rows, heads, ROPE))],
-        axis=-1,
-    )
-    values = key_value[..., NOPE:]
-    causal = jnp.arange(rows)[:, None] >= jnp.arange(rows)[None, :]
-    score_scale = (NOPE + ROPE) ** (-0.5)
-    raw = jnp.einsum("qhd,khd->hqk", qcat, keys, preferred_element_type=f32) * score_scale
-    score_now = jnp.where(causal[None], raw, -jnp.inf)
-    peak = jnp.max(score_now, axis=-1, keepdims=True)
-    expo = jnp.exp(score_now - peak)
-    pfull = expo / jnp.sum(expo, axis=-1, keepdims=True)
-    probs = pfull.astype(bf16)
-    attended = (
-        jnp.einsum("hqk,khd->qhd", probs, values, preferred_element_type=f32)
-        .astype(bf16)
-        .reshape(rows, heads * VD)
-    )
-    partial = mat(attended, out_proj).astype(bf16).reshape(tensors, quarter, width)
-    partial, dffn = lax.optimization_barrier((partial, dffn))
+    cosine = jnp.concatenate([cosine, cosine], axis=1)
+    sine = jnp.concatenate([-sine, sine], axis=1)
+    attend_w = (query_w, w_latent.T, gain_latent[None], kv_up, out_proj, cosine, sine)
+    partial, *kept = attend(tokens, gain_attn[None], *attend_w)
+    scale_one = own(kept[-1])
+    normed_one = own(xf) * scale_one
+    partial = partial.reshape(tensors, quarter, width)
     attn = sum_tensor(partial, groups, parts + 2)
     resid = own(xf) + live_own * attn
     scale_two = inv_rms(resid)
@@ -1273,7 +1597,8 @@
     for k in range(parts):
         dx, dgates, *grads, ffn = experts_all(
             split(xn2_own)[k],
-            dffn[k],
+            dffn_group[:, k * some : (k + 1) * some],
+            dffn_near[:, k * some : (k + 1) * some],
             picks_all[k],
             gate_t,
             up_t,
@@ -1285,96 +1610,70 @@
             k + 1,
         )
         dx = dx[0].astype(F32)
-        ffn = lax.psum_scatter(ffn, BOTH, scatter_dimension=0, tiled=True).astype(F32)
+        ffn = ffn.reshape(-1, some, width)
+        if parts > 1:
+            ffn = reduce_rows(ffn, groups, parts + 4 + k)
         dgates = dgates[:, :experts_local].reshape(total_experts, some).T
         outs.append((ffn, dx, dgates, *grads))
-    ffn, dx, dgates = (jnp.concatenate(v, axis=0) for v in list(zip(*outs))[:3])
+    dx, dgates = (jnp.concatenate(v, axis=0) for v in list(zip(*outs))[1:3])
+    ffn = outs[0][0] if parts == 1 else jnp.concatenate([v[0] for v in outs], axis=0)
     grads = [functools.reduce(jnp.add, v) for v in list(zip(*outs))[3:]]
     drouter = own(picks) * dgates
     grad_gate, grad_up = (v.transpose(0, 2, 1) for v in grads[:2])
     grad_down = grads[2]
-    shared_g = grads[3].reshape(3, part + spare, groups, width // groups).astype(BF16)
-    shared_g = shared_g.transpose(2, 0, 1, 3).reshape(groups, -1, width // groups)
     dlogit = router * (drouter - jnp.sum(router * drouter, axis=-1, keepdims=True))
     grad_router = mat_tn(dlogit.astype(bf16), xn2_own)
     dnorm_two = dx + mat_nt(dlogit.astype(bf16), w_router)
     grad_gain_ffn = jnp.sum(dnorm_two * normed_two, axis=0)
     dresid = cot_own + norm_back(dnorm_two, normed_two, scale_two, gain_ffn)
-    dattn = gather_tensor((dresid * live_own).astype(bf16), groups, tensors, parts + 3).reshape(rows, width)
-    grad_out = mat_tn(attended, dattn)
-    dattended = mat_nt(dattn, out_proj).astype(bf16).reshape(rows, heads, VD)
-    dvalues = jnp.einsum("hqk,qhd->khd", probs, dattended, preferred_element_type=f32)
-    dprobs = jnp.einsum("qhd,khd->hqk", dattended, values, preferred_element_type=f32)
-    dscore = (
-        pfull * (dprobs - jnp.sum(pfull * dprobs, axis=-1, keepdims=True)) * score_scale
-    ).astype(bf16)
-    dquery = jnp.einsum("hqk,khd->qhd", dscore, keys, preferred_element_type=f32)
-    dkeys = jnp.einsum("hqk,qhd->khd", dscore, qcat, preferred_element_type=f32)
-    dkv = (
-        jnp.concatenate([dkeys[..., :NOPE], dvalues], axis=-1)
-        .astype(bf16)
-        .reshape(rows, heads * (NOPE + VD))
+    shared_g = grads[3].reshape(3, part + spare, groups, width // groups).astype(BF16)
+    shared_g = shared_g.transpose(2, 0, 1, 3).reshape(groups, -1, width // groups)
+    dattn, shared_g = gather_tensor((dresid * live_own).astype(bf16), shared_g, groups, tensors, parts + 3)
+    dattn = dattn.reshape(rows, width)
+    grad_query, grad_kv, grad_out, grad_latent, grad_gain_attn, grad_gain_latent, dnorm_one = (
+        attend_back(dattn, tokens, kept, *attend_w)
     )
-    grad_kv = mat_tn(compressed, dkv)
-    dcomp = mat_nt(dkv, kv_up)
-    grad_gain_latent = jnp.sum(dcomp * normed_lat, axis=0)
-    dlatent = jnp.concatenate(
+    down = cells(groups, tensors)[0]
+
+    def whole_cells(v):
+        return jnp.pad(v, ((0, -v.shape[0] % (16 * down)), (0, 0)))
+
+    latent_g = whole_cells(grad_latent)
+    misc = jnp.concatenate(
         [
-            norm_back(dcomp, normed_lat, scale_lat, gain_latent),
-            rotate_back(jnp.sum(dkeys[..., NOPE:], axis=1), cosine, sine),
-        ],
-        axis=-1,
-    ).astype(bf16)
-    dqfull = jnp.concatenate(
-        [dquery[..., :NOPE], rotate_back(dquery[..., NOPE:], cosine[:, None, :], sine[:, None, :])],
-        axis=-1,
-    )
-    dqfull = dqfull.astype(bf16).reshape(rows, heads * (NOPE + ROPE))
-    grad_query = mat_tn(xn1, dqfull)
-    grad_latent = mat_tn(dlatent, xn1)
-    dnorm_one = mat_nt(dqfull, query_w) + mat_nt(dlatent, w_latent)
-    grad_gain_attn = jnp.sum(dnorm_one * normed_one, axis=0)
-    small = jnp.concatenate(
-        [
-            grad_latent,
             grad_router,
-            grad_gain_attn[None],
+            grad_gain_attn,
             grad_gain_ffn[None],
-            jnp.pad(grad_gain_latent, (0, width - KVR))[None],
+            jnp.pad(grad_gain_latent, ((0, 0), (0, width - KVR))),
         ],
         axis=0,
-    ).astype(bf16)
-    small = jnp.pad(small, ((0, -small.shape[0] % 128), (0, 0)))
-    grad_out = grad_out.astype(bf16).reshape(-1, groups, width // groups).transpose(1, 0, 2)
-    grad_query, grad_kv, grad_out, small, shared_g, grad_tokens = finish(
+    )
+    misc = whole_cells(misc.astype(bf16))
+    grad_query, grad_kv, grad_out, small, grad_tokens, output = finish(
         (
-            grad_query.astype(bf16).reshape(groups, -1, grad_query.shape[1]),
-            grad_kv.astype(bf16).reshape(groups, -1, grad_kv.shape[1]),
+            grad_query.reshape(groups, -1, grad_query.shape[1]),
+            grad_kv.reshape(groups, -1, grad_kv.shape[1]),
             grad_out,
         ),
-        small,
-        shared_g,
-        dnorm_one.astype(bf16).reshape(tensors, quarter, width),
-        dresid,
-        own(normed_one),
-        own(scale_one),
-        gain_attn[None],
+        latent_g,
+        misc,
+        dnorm_one.reshape(tensors, quarter, width),
+        ffn,
+        (dresid, normed_one, scale_one, gain_attn[None], resid, live_own),
         groups,
         tensors,
         parts + 1,
     )
     grad_tokens = grad_tokens.reshape(rows, width)
-    grad_tokens, ffn, resid_late = lax.optimization_barrier((grad_tokens, ffn, resid))
-    output_own = (resid_late + live_own * ffn).astype(bf16)
-    output = lax.all_gather(output_own, "tensor", axis=0, tiled=True)
-    at = w_latent.shape[1]
-    small = small.astype(f32)
-    grad_latent = small[:at].T
-    grad_router = small[at : at + total_experts].T
-    at = at + total_experts
-    grad_gain_attn = small[at]
-    grad_gain_ffn = small[at + 1]
-    grad_gain_latent = small[at + 2, :KVR]
+    output = output.reshape(rows, width)
+    small = small.reshape(down, -1, width)
+    tall = latent_g.shape[0] // down
+    grad_latent = small[:, :tall].reshape(-1, width)[: w_latent.shape[1]].astype(f32).T
+    misc = small[:, tall:].reshape(-1, width).astype(f32)
+    grad_router = misc[:total_experts].T
+    grad_gain_attn = misc[total_experts]
+    grad_gain_ffn = misc[total_experts + 1]
+    grad_gain_latent = misc[total_experts + 2, :KVR]
     shared_g = shared_g.reshape(groups, 3, part + spare, -1)[:, :, :part].transpose(1, 0, 2, 3)
     shared_g = shared_g.reshape(3, groups * part, -1).astype(f32)
     grad_sgate, grad_sup, grad_sdown = shared_g[0].T, shared_g[1].T, shared_g[2]

time: 895 us -> 775 us (0.87); the launches traced: 884 us -> 774 us
  matrix products: 55.6 us -> 2.34 us
  local copies, waits for them, and re-layouts: 81.7 us -> 34.4 us
  Pallas kernels: 692 us -> 715 us
  between operations: 15.8 us -> 1.63 us
  waiting for transfers between devices: 11.4 us -> 0 us
    pallas_call x0 -> x2, Pallas kernels: none -> 58.5 us  [the longest x1 34.2 us: attend_back(): pl.pallas_call(functools.partial(attend_back_kernel, heads), out_shape=ou...]
    pallas_call x1, Pallas kernels: 147 us -> 101 us  [begin(): pl.pallas_call(functools.partial(begin_kernel, far), out_shape=outs, in_s...]
    dot_general x6 -> x0, matrix products: 26 us -> none  [the longest x1 9.34 us: shards(): jnp.einsum('hqk,khd->qhd', dscore, keys, preferred_element_type=f32)]
    pallas_call x1, Pallas kernels: 307 us -> 319 us  [experts_all(): pl.pallas_call(functools.partial(experts_kernel, (far, experts, hidden, s...]
    concatenate x1 -> x0, local copies, waits for them, and re-layouts: 11.8 us -> none  [shards(): jnp.concatenate([grad_latent, grad_router, grad_gain_attn[None], grad_gai...]
    all_gather x2 -> x0, waiting for transfers between devices: 11.4 us -> none  [the longest x1 11.4 us: shards(): output = lax.all_gather(output_own, 'tensor', axis=0, tiled=True)]
    dot_general x5 -> x1, matrix products: 11.5 us -> 0.18 us  [mat_tn(): lax.dot_general(left, right, (((0,), (0,)), ((), ())), preferred_element_...]
    unnamed x140 -> x52, local copies, waits for them, and re-layouts: 25.3 us -> 20.6 us
  transfers between devices with their start and end apart: 3 -> 0, of which waited for: 1 -> 0; matrix products, arithmetic and copies ran while one was open for 15% -> 0% of each run, Pallas kernels for 42% -> 0%
where the time goes in v3:
time: 775 us; the launch traced here: 774 us
  Pallas kernels  715 us (92%)
  local copies, waits for them, and re-layouts  34.4 us (4%)
  other arithmetic  21.4 us (3%)
    pallas_call x1, Pallas kernels, experts_all(): pl.pallas_call(functools.partial(experts_kernel, (far, experts, hidden, s...  319 us
    pallas_call x1, Pallas kernels, finish(): pl.pallas_call(functools.partial(finish_kernel, far), out_shape=outs, in_...  195 us
    pallas_call x1, Pallas kernels, begin(): pl.pallas_call(functools.partial(begin_kernel, far), out_shape=outs, in_s...  101 us
    pallas_call x1, Pallas kernels, attend_back(): pl.pallas_call(functools.partial(attend_back_kernel, heads), out_shape=ou...  34.2 us
    pallas_call x1, Pallas kernels, gather_tensor(): pl.pallas_call(functools.partial(gather_tensor_kernel, groups // 2), out_...  24.9 us
    pallas_call x1, Pallas kernels, attend(): pl.pallas_call(functools.partial(attend_kernel, heads), out_shape=outs, i...  24.3 us
    unnamed x52, local copies, waits for them, and re-layouts  20.6 us
    pallas_call x1, Pallas kernels, sum_tensor(): pl.pallas_call(functools.partial(sum_tensor_kernel, groups // 2), out_sha...  16.4 us

profile of v3, /device:TPU:0, one launch (start us, length us, event | category | flops | bytes accessed | tf_op | source)
XLA Modules:
  0.0 774.4 jit_solution(7830314657029480981)
XLA Ops:
  1.4 0.1 fusion.12
  1.4 2.0 dynamic-slice_multiply_fusion.refs_5_
  3.4 0.7 fusion.2
  4.2 0.6 convert_bitcast_fusion.3.refs_4_
  4.8 1.2 pad_bitcast_fusion
  6.0 1.1 pad_maximum_fusion
  7.2 100.8 %shard_map.297 = (bf16[8,256,768]{2,1,0:T(8,128)(2,1)}, bf16[8,64,1024]{2,1,0:T(8,128)(2,1)}, bf16[8,512,256]{2,1,0:T(8,128)(2,1)}, bf16[8,288,256]{2,1,0:T(8,12...) custom-call(bf16[256,768]{1,0:T(8,128)(2,1)} %refs_0_.1, bf16[64,1024]{1,0:T(8,128)(2,1)} %refs_1_.1, ...), custom_call_target="tpu_custom_call" | custom-call | bytes 300000000 | tf_op jit(solution)/shard_map/pallas_call | solution.py:380
  108.0 1.0 fusion.5
  109.0 1.0 pad_maximum_fusion.1
  110.0 24.3 %shard_map.298 = (bf16[512,2048]{1,0:T(8,128)(2,1)}, bf16[512,2048]{1,0:T(8,128)(2,1)}, bf16[4,512,192]{2,1,0:T(8,128)(2,1)}, bf16[512,1024]{1,0:T(8,128)(2,1)},...) custom-call(bf16[512,2048]{1,0:T(8,128)(2,1)} %tokens.3, ...), custom_call_target="tpu_custom_call" | custom-call | bytes 60000000 | tf_op jit(solution)/shard_map/pallas_call | solution.py:852
  134.3 1.5 fusion.11
  135.7 1.6 copy-done.1
  137.3 16.4 %shard_map.299 = f32[128,2048]{1,0:T(8,128)S(1)} custom-call(bf16[4,128,2048]{2,1,0:T(8,128)(2,1)S(1)} %bitcast.87), custom_call_target="tpu_custom_call" | custom-call | bytes 48000000 | tf_op jit(solution)/shard_map/pallas_call | solution.py:516
  153.7 0.0 copy-start.15
  153.7 2.5 multiply_reduce_fusion.2
  156.3 1.0 copy-done.2
  157.2 0.0 copy-done.15
  157.2 0.9 multiply_convert_fusion.1.refs_0_
  158.3 0.1 convert_element_type.121
  158.4 0.8 convert_bitcast_fusion.2.refs_3_
  159.2 0.7 fusion.7.refs_8_
  159.9 2.1 copy.45
  161.9 1.4 reshape.173.refs_7_
  163.3 1.5 broadcast_multiply_fusion
  164.9 319.1 %shard_map.300 = (bf16[1,128,2048]{2,1,0:T(8,128)(2,1)}, f32[8,8,128]{2,1,0:T(8,128)}, f32[2,352,2048]{2,1,0:T(8,128)}, f32[2,352,2048]{2,1,0:T(8,128)}, f32[2,3...) custom-call(bf16[128,2048]{1,0:T(8,128)(2,1)} %multiply_convert_fusi, ...), custom_call_target="tpu_custom_call" | custom-call | bytes 840000000 | tf_op jit(solution)/shard_map/pallas_call | solution.py:1490
  484.0 0.8 slice.39
  484.8 0.3 fusion.15
  485.2 0.2 convolution_convert_fusion
  485.3 1.9 multiply_reduce_fusion
  487.3 0.0 copy-done.3
  487.3 2.6 multiply_convert_fusion
  489.9 0.2 convert_element_type.126
  490.0 0.1 copy.50
  490.2 24.9 %shard_map.301 = (bf16[4,128,2048]{2,1,0:T(8,128)(2,1)S(1)}, bf16[8,288,256]{2,1,0:T(8,128)(2,1)S(1)}) custom-call(bf16[128,2048]{1,0:T(8,128)(2,1)S(1)} %get-tuple-element.98.own, bf16[8,288,256]{2,1,0:T(8,128)(2,1)S(1)} %bitcast.85), custom_call_target="tpu_custom_call" | custom-call | bytes 75000000 | tf_op jit(solution)/shard_map/pallas_call | solution.py:550
  515.1 0.0 copy-start
  515.1 1.3 copy-done
  516.4 34.2 %shard_map.302 = (bf16[2048,768]{1,0:T(8,128)(2,1)}, bf16[512,1024]{1,0:T(8,128)(2,1)}, bf16[8,512,256]{2,1,0:T(8,128)(2,1)}, bf16[576,2048]{1,0:T(8,128)(2,1)},...) custom-call(bf16[512,2048]{1,0:T(8,128)(2,1)} %bitcast.86, bf16[512,2048]{1,0:T(8,128)(2,1)} %tokens.3, ...), custom_call_target="tpu_custom_call" | custom-call | bytes 120000000 | tf_op jit(solution)/shard_map/pallas_call | solution.py:960
  550.6 0.7 convert.24
  551.3 0.7 convert.26
  552.0 0.7 pad.23.refs_4_
  552.7 0.7 copy.47.refs_12_
  553.5 195.0 %shard_map.303 = (f32[256,768]{1,0:T(8,128)}, f32[64,1024]{1,0:T(8,128)}, f32[512,256]{1,0:T(8,128)}, bf16[640,2048]{1,0:T(8,128)(2,1)}, bf16[4,128,2048]{2,1,0:T(8,128)(2,1)}, /*index=5*/bf16[4,128,2048]{2,1,0:T(8,128)(2,1)}) custom-call(bf16[8,256,768]{2,1,0:T(8,128)(2,1)} %bitcast.107, bf16[8,64,1024]{2,1,0:T(8,128)(2,1)} %bitcast.116, ...), custom_call_target="tpu_custom_call" | custom-call | bytes 330000000 | tf_op jit(solution)/shard_map/pallas_call | solution.py:746
  748.5 1.8 slice.53
  750.3 2.9 convert_bitcast_fusion
  753.3 1.0 slice_convert_fusion
  754.3 0.7 slice_bitcast_fusion
  755.0 0.6 fusion.14
  755.6 0.6 slice.54
  756.2 0.1 convert_bitcast_fusion.1
  756.3 0.0 slice-start.4
  756.3 0.0 slice-start.2
  756.3 1.4 fusion.13
  757.7 0.8 copy-done.8
  758.5 1.3 copy.60
  759.8 1.3 copy.61
  761.2 1.4 copy-done.9
  762.5 0.9 copy.62
  763.4 0.7 copy.63
  764.1 0.1 copy-done.11
  764.2 0.8 copy.64
  765.0 2.9 copy.65
  767.9 2.9 copy.66
  770.8 1.1 slice-done.1
  771.9 2.5 copy.67
  (47 shorter events, 0.3 us)
Async XLA Ops:
  0.6 5.3 copy-start.12
  135.7 1.6 copy-start.1
  153.7 3.5 copy-start.15
  153.7 4.5 copy-start.14
  156.3 1.0 copy-start.2
  156.3 2.9 copy-start.10
  159.9 3.5 copy-start.5
  164.9 319.9 %copy-start.4 = (bf16[128,2048]{1,0:T(8,128)(2,1)S(1)}, bf16[128,2048]{1,0:T(8,128)(2,1)}, u32[]{:S(2)}) copy-start(bf16[128,2048]{1,0:T(8,128)(2,1)} %multiply_convert_fusion.1.refs_0_) | copy-start | bytes 1572868
  483.9 3.3 copy-start.3
  487.3 2.6 copy-start.6
  515.1 1.3 copy-start
  756.1 2.4 copy-start.8
  756.1 3.7 copy-start.7
  756.3 8.7 %slice-start.4 = ((s8[5767168]{0:T(1024)(128)(4,1)}), s8[4194304]{0:T(1024)(128)(4,1)S(1)}, s32[]{:S(2)}) async-start(s8[5767168]{0:T(1024)(128)(4,1)} %bitcast.100), calls=%async_computation.4 | async-start | bytes 8388608
  756.3 11.6 %slice-start.2 = ((s8[5767168]{0:T(1024)(128)(4,1)}), s8[4194304]{0:T(1024)(128)(4,1)S(1)}, s32[]{:S(2)}) async-start(s8[5767168]{0:T(1024)(128)(4,1)} %bitcast.97), calls=%async_computation.2 | async-start | bytes 8388608
  758.5 6.5 slice-start.5
  759.8 2.7 copy-start.9
  759.8 3.6 copy-start.13
  762.5 1.7 copy-start.11
  762.5 5.4 slice-start.3
  765.0 5.8 slice-start
  767.9 4.0 slice-start.1

commit v4 on v3

--- a/solution.py
+++ b/solution.py
@@ -82,6 +82,10 @@
 def places():
     e, t = lax.axis_index("expert"), lax.axis_index("tensor")
     return e // 2, e % 2, t // 2, t % 2
+
+
+def far_first(far):
+    return sorted(range(far), key=lambda r: -min(r, far - r))
 
 
 class Net:
@@ -201,7 +205,7 @@
         self.net, self.part_at, self.acc, self.order = net, part_at, acc, order
         self.bufs = (from_core, from_first, from_second, from_z)
         self.core, self.first, self.second, self.z, self.loads = {}, {}, {}, {}, {}
-        self.turn = list(range(net.far - 1, -1, -1))
+        self.turn = far_first(net.far)
         self.spots = ((1, 1), (0, 1), (1, 0), (0, 0))
         self.links = (net.x, net.y) if order == "xy" else (net.y, net.x)
 
@@ -279,6 +283,69 @@
             pltpu.VMEM((far, rows, width), BF16),
             pltpu.VMEM((far - 1, rows, width), BF16),
         ]
+
+
+class ReduceDirect(ReduceAll):
+    def stage_b(self, i):
+        r = self.turn[i]
+        for v in (1, 0):
+            at = r * 2 + v
+            self.merge(r * 4 + v, self.bufs[1], at, self.first[at])
+            if at:
+                self.z[at] = self.net.push(
+                    self.acc.at[r * 4 + v], self.bufs[2].at[at], self.net.at(r, v)
+                )
+
+    def end(self):
+        for at, k in self.z.items():
+            self.net.arrived(self.bufs[2].at[at], k)
+
+    def total(self, rows):
+        total = self.acc[0, rows, :].astype(F32)
+        for at in range(1, 2 * self.net.far):
+            total = total + self.bufs[2][at, rows, :].astype(F32)
+        return total
+
+    @staticmethod
+    def scratch(far, rows, width):
+        return [
+            pltpu.VMEM((4 * far, rows, width), BF16),
+            pltpu.VMEM((4 * far, rows, width), BF16),
+            pltpu.VMEM((2 * far, rows, width), BF16),
+            pltpu.VMEM((2 * far, rows, width), BF16),
+        ]
+
+
+class GatherDirect:
+    def __init__(self, net, own, out_at):
+        self.net, self.own, self.out_at = net, own, out_at
+        self.spots = [(r, b) for r in range(net.far) for b in range(2)]
+        self.direct, self.x, self.cores = {}, {}, {}
+
+    def place(self, r, b, c=0, d=0):
+        return self.out_at(self.net.slot(-r, b, c, d))
+
+    def start(self):
+        for r, b in self.spots[1:]:
+            self.direct[r, b] = self.net.push(self.own, self.place(0, 0), self.net.at(r, b))
+
+    def stage_a(self, i):
+        r, b = self.spots[i]
+        here = self.place(r, b) if i else self.own
+        if i:
+            self.net.arrived(here, self.direct[r, b])
+        self.x[r, b] = self.net.push(here, self.place(r, b), self.net.x)
+        self.cores[r, b, 0] = self.net.push(here, self.place(r, b), self.net.core)
+
+    def stage_b(self, i):
+        r, b = self.spots[i]
+        here = self.place(r, b, 1)
+        self.net.arrived(here, self.x[r, b])
+        self.cores[r, b, 1] = self.net.push(here, here, self.net.core)
+
+    def end(self):
+        for (r, b, c), k in self.cores.items():
+            self.net.arrived(self.place(r, b, c, 1), k)
 
 
 class Summed:
@@ -392,7 +459,7 @@
     def __init__(self, net, part, out, acc, from_y, from_z):
         self.net, self.part, self.out = net, part, out
         self.acc, self.from_y, self.from_z = acc, from_y, from_z
-        self.turn = list(range(net.far - 1, -1, -1))
+        self.turn = far_first(net.far)
         self.y, self.z = {}, {}
 
     def load(self):
@@ -621,11 +688,11 @@
 
     summed = len(ffn.shape) == 2
     small, sum_own, tokens_own, output_own = scratch[-7:-3]
-    sums = ReduceAll(net, cell(small), *take(5), "xy")
+    sums = ReduceDirect(net, cell(small), *take(4), None, "xy")
     rows_back = ReduceTensor(net, dxn, *take(3))
     ffns = Summed(ffn) if summed else ReduceAll(net, lambda s: ffn.at[s], *take(5), "xy")
     give_output = GatherTensor(net, output_own, ooutput)
-    every = GatherAll(net, sum_own, cell(osmall), "yx")
+    every = GatherDirect(net, sum_own, cell(osmall))
     give_tokens = GatherTensor(net, tokens_own, otokens)
     moved = []
     for k in range(down):
@@ -636,7 +703,7 @@
     for part in (rows_back, *weights, ffns):
         part.load()
     mine = []
-    net.greet(net.near())
+    net.greet(net.line() + [net.x, net.core])
 
     def send_weights(r):
         for part in weights:
@@ -664,7 +731,7 @@
     def sum_rows(rows):
         sum_own[rows, :] = sums.total(rows).astype(BF16)
 
-    turn = list(range(far - 1, -1, -1))
+    turn = far_first(far)
     rows_back.start()
     for copy in moved:
         copy.wait()
@@ -676,41 +743,37 @@
     for i in range(far):
         sums.stage_a(i)
     ffns.stage_a(0)
-    send_weights(turn[1])
     for i in range(far):
         sums.stage_b(i)
+    send_weights(turn[1])
     rows_back.end()
     each(tokens_own.shape[0], tokens_rows)
     give_tokens.start()
     ffns.stage_a(1)
-    for i in range(far):
-        sums.stage_c(i)
-    for k in range(far - 2):
-        step_weights(turn[k])
-        send_weights(turn[k + 2])
-        ffns.stage_b(k)
-        ffns.stage_a(k + 2)
+    step_weights(turn[0])
     sums.end()
     each(sum_own.shape[0], sum_rows)
     mine.append(net.load(sum_own, cell(osmall)(net.slot())))
     every.start()
     every.stage_a(0)
-    step_weights(turn[far - 2])
+    for k in range(far - 2):
+        if k:
+            step_weights(turn[k])
+        send_weights(turn[k + 2])
+        ffns.stage_b(k)
+        ffns.stage_a(k + 2)
+    give_tokens.step()
     for k in range(far - 2):
         ffns.stage_c(k)
-    give_tokens.step()
-    every.stage_b(0)
-    every.stage_c(0)
+    step_weights(turn[far - 2])
+    for i in range(1, 2 * far):
+        every.stage_a(i)
     ffns.stage_b(far - 2)
-    for r in range(1, far):
-        every.stage_a(r)
     step_weights(turn[far - 1])
-    for r in range(1, far):
-        every.stage_b(r)
     ffns.stage_c(far - 2)
     ffns.stage_b(far - 1)
-    for r in range(1, far):
-        every.stage_c(r)
+    for i in range(2 * far):
+        every.stage_b(i)
     ffns.stage_c(far - 1)
     ffns.end()
     each(output_own.shape[0], output_rows)
@@ -737,7 +800,7 @@
     scratch = []
     for w in weights:
         scratch += ReduceGroups.scratch(far, *w.shape[1:])
-    scratch += ReduceAll.scratch(far, *cell)
+    scratch += ReduceDirect.scratch(far, *cell)
     scratch += ReduceTensor.scratch(m, width)
     if len(ffn.shape) == 3:
         scratch += ReduceAll.scratch(far, *ffn.shape[1:])
@@ -1261,6 +1324,8 @@
     begin_all(block_copies(0, dy_near))
     wait_all(weights())
 
+    last = groups - 1
+
     @pl.loop(0, groups)
     def _(s):
         r = s // 2
@@ -1308,6 +1373,7 @@
         pl.when(s > 0)(lambda: h1_post(s - 1))
         pl.when(s > 2)(lambda: h2_post(s - 3))
         pl.when((s > 4) & (s % 2 == 0))(lambda: h3_pre(s - 5))
+        pl.when(s == last)(lambda: h3_pre(last - 4))
         pl.when((s % 2 == 1) & more)(lambda: rows_c(r + 1))
 
         @pl.loop(0, width // 512)
@@ -1317,6 +1383,12 @@
             acc_down[:, at] += dot_nn(hs[:units, :], dy[:, at])
 
         pl.when((s > 4) & (s % 2 == 0))(lambda: h3_post(s - 5))
+
+        @pl.when(s == last)
+        def _():
+            h3_post(last - 4)
+            h2_pre(last - 2)
+
         pl.when((s % 2 == 1) & more)(lambda: rows_d(r + 1))
         pl.when(s + 1 < groups)(lambda: load_block(s + 1))
         hsn[...] = hs[...].T
@@ -1342,6 +1414,7 @@
             ffn_part[:, at] = dot_nn(hsn[:, :units], w_down[:, at]).astype(BF16)
 
         ffn_copy(s).start()
+        pl.when(s == last)(lambda: h2_post(last - 2))
         pl.when((s % 2 == 0) & more)(lambda: rows_b(r + 1))
 
     def stores():
@@ -1365,16 +1438,20 @@
 
     for k in range(3):
         dg_push(k).start()
-    last = groups - 1
+    h2_pre(last - 1)
     h1_pre(last)
-    h2_pre(last - 2)
+    h2_post(last - 1)
     h1_post(last)
     begin_all(stores())
-    h2_post(last - 2)
-    h2_pre(last - 1)
-    h2_post(last - 1)
-    h3_pre(last - 4)
-    h3_post(last - 4)
+    for a in sums:
+        for c in both:
+            wait_for(y1_in.at[a, last // 2, c], y1_r.at[a, last // 2, c])
+    begin_all(h2_more(last))
+    wait_all(h2_more(last))
+    for a in sums:
+        for c in (1, 0):
+            add(a, last, c, half, stage3.at[a, c])
+        x1_push(last, a).start()
     h3_pre(last - 2)
     h3_post(last - 2)
     for k in range(3):
@@ -1390,8 +1467,12 @@
 
     for k in range(len(others)):
         dg_give(k).start()
-    h2_pre(last)
-    h2_post(last)
+    for a in sums:
+        wait_for(x0_in.at[a, last], x0_r.at[a, last])
+    begin_all(h2_loads(last))
+    wait_all(h2_loads(last))
+    for a in sums:
+        add(a, last, 0, 0, stage2.at[a])
     h3_pre(last)
     h3_post(last)
     for r in range(1, far):

time: 775 us -> 762 us (0.983)
  Pallas kernels: 715 us -> 701 us
where the time goes in v4:
time: 762 us; the launch traced here: 761 us
  Pallas kernels  701 us (92%)
  local copies, waits for them, and re-layouts  34.4 us (5%)
  other arithmetic  21.4 us (3%)
    pallas_call x1, Pallas kernels, experts_all(): pl.pallas_call(functools.partial(experts_kernel, (far, experts, hidden, s...  312 us
    pallas_call x1, Pallas kernels, finish(): pl.pallas_call(functools.partial(finish_kernel, far), out_shape=outs, in_...  188 us
    pallas_call x1, Pallas kernels, begin(): pl.pallas_call(functools.partial(begin_kernel, far), out_shape=outs, in_s...  101 us
    pallas_call x1, Pallas kernels, attend_back(): pl.pallas_call(functools.partial(attend_back_kernel, heads), out_shape=ou...  34.2 us
    pallas_call x1, Pallas kernels, gather_tensor(): pl.pallas_call(functools.partial(gather_tensor_kernel, groups // 2), out_...  24.8 us
    pallas_call x1, Pallas kernels, attend(): pl.pallas_call(functools.partial(attend_kernel, heads), out_shape=outs, i...  24.3 us
    unnamed x52, local copies, waits for them, and re-layouts  20.6 us
    pallas_call x1, Pallas kernels, sum_tensor(): pl.pallas_call(functools.partial(sum_tensor_kernel, groups // 2), out_sha...  16.4 us

profile of v4, /device:TPU:0, one launch (start us, length us, event | category | flops | bytes accessed | tf_op | source)
XLA Modules:
  0.0 760.6 jit_solution(7902844758739964880)
XLA Ops:
  1.4 0.1 fusion.12
  1.4 2.0 dynamic-slice_multiply_fusion.refs_5_
  3.4 0.7 fusion.2
  4.2 0.6 convert_bitcast_fusion.3.refs_4_
  4.8 1.2 pad_bitcast_fusion
  6.0 1.1 pad_maximum_fusion
  7.2 100.8 %shard_map.297 = (bf16[8,256,768]{2,1,0:T(8,128)(2,1)}, bf16[8,64,1024]{2,1,0:T(8,128)(2,1)}, bf16[8,512,256]{2,1,0:T(8,128)(2,1)}, bf16[8,288,256]{2,1,0:T(8,12...) custom-call(bf16[256,768]{1,0:T(8,128)(2,1)} %refs_0_.1, bf16[64,1024]{1,0:T(8,128)(2,1)} %refs_1_.1, ...), custom_call_target="tpu_custom_call" | custom-call | bytes 300000000 | tf_op jit(solution)/shard_map/pallas_call | solution.py:447
  108.0 1.0 fusion.5
  109.0 1.0 pad_maximum_fusion.1
  110.0 24.3 %shard_map.298 = (bf16[512,2048]{1,0:T(8,128)(2,1)}, bf16[512,2048]{1,0:T(8,128)(2,1)}, bf16[4,512,192]{2,1,0:T(8,128)(2,1)}, bf16[512,1024]{1,0:T(8,128)(2,1)},...) custom-call(bf16[512,2048]{1,0:T(8,128)(2,1)} %tokens.3, ...), custom_call_target="tpu_custom_call" | custom-call | bytes 60000000 | tf_op jit(solution)/shard_map/pallas_call | solution.py:915
  134.3 1.5 fusion.11
  135.7 1.6 copy-done.1
  137.3 16.4 %shard_map.299 = f32[128,2048]{1,0:T(8,128)S(1)} custom-call(bf16[4,128,2048]{2,1,0:T(8,128)(2,1)S(1)} %bitcast.87), custom_call_target="tpu_custom_call" | custom-call | bytes 48000000 | tf_op jit(solution)/shard_map/pallas_call | solution.py:583
  153.7 0.0 copy-start.15
  153.7 2.5 multiply_reduce_fusion.2
  156.3 1.0 copy-done.2
  157.2 0.9 multiply_convert_fusion.1.refs_0_
  158.2 0.0 copy-done.14
  158.3 0.1 convert_element_type.121
  158.4 0.8 convert_bitcast_fusion.2.refs_3_
  159.2 0.7 fusion.7.refs_8_
  159.9 2.1 copy.45
  161.9 1.4 reshape.173.refs_7_
  163.3 0.0 copy-done.5
  163.3 1.5 broadcast_multiply_fusion
  164.9 311.9 %shard_map.300 = (bf16[1,128,2048]{2,1,0:T(8,128)(2,1)}, f32[8,8,128]{2,1,0:T(8,128)}, f32[2,352,2048]{2,1,0:T(8,128)}, f32[2,352,2048]{2,1,0:T(8,128)}, f32[2,3...) custom-call(bf16[128,2048]{1,0:T(8,128)(2,1)} %multiply_convert_fusi, ...), custom_call_target="tpu_custom_call" | custom-call | bytes 840000000 | tf_op jit(solution)/shard_map/pallas_call | solution.py:1571
  476.8 0.8 slice.39
  477.6 0.3 fusion.15
  478.0 0.2 convolution_convert_fusion
  478.2 1.9 multiply_reduce_fusion
  480.1 2.6 multiply_convert_fusion
  482.7 0.2 convert_element_type.126
  482.9 0.1 copy.50
  483.0 24.8 %shard_map.301 = (bf16[4,128,2048]{2,1,0:T(8,128)(2,1)S(1)}, bf16[8,288,256]{2,1,0:T(8,128)(2,1)S(1)}) custom-call(bf16[128,2048]{1,0:T(8,128)(2,1)S(1)} %get-tuple-element.98.own, bf16[8,288,256]{2,1,0:T(8,128)(2,1)S(1)} %bitcast.85), custom_call_target="tpu_custom_call" | custom-call | bytes 75000000 | tf_op jit(solution)/shard_map/pallas_call | solution.py:617
  507.9 0.0 copy-start
  507.9 1.3 copy-done
  509.2 34.2 %shard_map.302 = (bf16[2048,768]{1,0:T(8,128)(2,1)}, bf16[512,1024]{1,0:T(8,128)(2,1)}, bf16[8,512,256]{2,1,0:T(8,128)(2,1)}, bf16[576,2048]{1,0:T(8,128)(2,1)},...) custom-call(bf16[512,2048]{1,0:T(8,128)(2,1)} %bitcast.86, bf16[512,2048]{1,0:T(8,128)(2,1)} %tokens.3, ...), custom_call_target="tpu_custom_call" | custom-call | bytes 120000000 | tf_op jit(solution)/shard_map/pallas_call | solution.py:1023
  543.4 0.7 convert.24
  544.1 0.7 convert.26
  544.8 0.7 pad.23.refs_4_
  545.6 0.7 copy.47.refs_12_
  546.3 188.3 %shard_map.303 = (f32[256,768]{1,0:T(8,128)}, f32[64,1024]{1,0:T(8,128)}, f32[512,256]{1,0:T(8,128)}, bf16[640,2048]{1,0:T(8,128)(2,1)}, bf16[4,128,2048]{2,1,0:T(8,128)(2,1)}, /*index=5*/bf16[4,128,2048]{2,1,0:T(8,128)(2,1)}) custom-call(bf16[8,256,768]{2,1,0:T(8,128)(2,1)} %bitcast.107, bf16[8,64,1024]{2,1,0:T(8,128)(2,1)} %bitcast.116, ...), custom_call_target="tpu_custom_call" | custom-call | bytes 330000000 | tf_op jit(solution)/shard_map/pallas_call | solution.py:809
  734.6 1.8 slice.53
  736.5 2.9 convert_bitcast_fusion
  739.4 1.0 slice_convert_fusion
  740.4 0.7 slice_bitcast_fusion
  741.1 0.6 fusion.14
  741.7 0.6 slice.54
  742.3 0.1 convert_bitcast_fusion.1
  742.4 0.0 slice-start.4
  742.4 0.0 slice-start.2
  742.4 1.4 fusion.13
  743.8 0.8 copy-done.8
  744.6 1.3 copy.60
  746.0 1.3 copy.61
  747.3 1.4 copy-done.9
  748.6 0.9 copy.62
  749.5 0.7 copy.63
  750.2 0.1 copy-done.11
  750.3 0.8 copy.64
  751.1 2.9 copy.65
  754.1 2.9 copy.66
  757.0 1.1 slice-done.1
  758.0 2.5 copy.67
  (47 shorter events, 0.3 us)
Async XLA Ops:
  0.6 5.3 copy-start.12
  135.7 1.6 copy-start.1
  153.7 3.5 copy-start.15
  153.7 4.5 copy-start.14
  156.3 1.0 copy-start.2
  156.3 2.9 copy-start.10
  159.9 3.5 copy-start.5
  164.9 312.8 %copy-start.4 = (bf16[128,2048]{1,0:T(8,128)(2,1)S(1)}, bf16[128,2048]{1,0:T(8,128)(2,1)}, u32[]{:S(2)}) copy-start(bf16[128,2048]{1,0:T(8,128)(2,1)} %multiply_convert_fusion.1.refs_0_) | copy-start | bytes 1572868
  476.8 3.3 copy-start.3
  480.1 2.6 copy-start.6
  507.9 1.3 copy-start
  742.3 2.4 copy-start.8
  742.3 3.7 copy-start.7
  742.4 8.7 %slice-start.4 = ((s8[5767168]{0:T(1024)(128)(4,1)}), s8[4194304]{0:T(1024)(128)(4,1)S(1)}, s32[]{:S(2)}) async-start(s8[5767168]{0:T(1024)(128)(4,1)} %bitcast.100), calls=%async_computation.4 | async-start | bytes 8388608
  742.4 11.6 %slice-start.2 = ((s8[5767168]{0:T(1024)(128)(4,1)}), s8[4194304]{0:T(1024)(128)(4,1)S(1)}, s32[]{:S(2)}) async-start(s8[5767168]{0:T(1024)(128)(4,1)} %bitcast.97), calls=%async_computation.2 | async-start | bytes 8388608
  744.6 6.5 slice-start.5
  746.0 2.7 copy-start.9
  746.0 3.6 copy-start.13
  748.6 1.7 copy-start.11
  748.6 5.4 slice-start.3
  751.1 5.8 slice-start
  754.0 4.0 slice-start.1

commit v5 on v4

--- a/solution.py
+++ b/solution.py
@@ -403,7 +403,7 @@
     mine.append(net.load(marks, marks_out.at[me]))
     net.greet(net.line() + [net.x, net.core])
     here = [near.at[net.at(0, 0, c, d)[1]] for c in range(2) for d in range(2)]
-    dy_y = net.push(dy, here[0], net.y)
+    dy_y = net.push(dy.at[net.at()[1]], here[0], net.y)
     tokens = {}
     others = [(r, b) for r in range(far) for b in range(2)][1:]
     for a, (w, o) in enumerate(zip(ws, outs)):
@@ -443,7 +443,7 @@
     outs = [jax.ShapeDtypeStruct((groups, *w.shape), w.dtype) for w in ws]
     outs.append(jax.ShapeDtypeStruct(blocks.shape, blocks.dtype))
     outs.append(jax.ShapeDtypeStruct((groups, *marks.shape), marks.dtype))
-    outs.append(jax.ShapeDtypeStruct((tensors, *dy.shape), dy.dtype))
+    outs.append(jax.ShapeDtypeStruct(dy.shape, dy.dtype))
     return pl.pallas_call(
         functools.partial(begin_kernel, far),
         out_shape=outs,
@@ -1300,9 +1300,12 @@
             pairs.append((wg_hbm.at[e], w_in.at[at]))
             pairs.append((wu_hbm.at[e], w_in.at[pl.ds(units + e * hidden, hidden)]))
             pairs.append((wd_hbm.at[e], w_down.at[at]))
-        pairs.append((ws_hbm.at[0], w_in.at[pl.ds(routed, shared)]))
-        pairs.append((ws_hbm.at[1], w_in.at[pl.ds(units + routed, shared)]))
-        pairs.append((ws_hbm.at[2], w_down.at[pl.ds(routed, shared)]))
+        some = ws_hbm.shape[2]
+        for e in range(ws_hbm.shape[0]):
+            across = pl.ds(e * some, some)
+            for j, (ref, at) in enumerate(((w_in, routed), (w_in, units + routed), (w_down, routed))):
+                part_j = ws_hbm.at[e, pl.ds(j * shared, shared)]
+                pairs.append((part_j, ref.at[pl.ds(at, shared), across]))
         pairs.append((wr_hbm, w_in.at[pl.ds(2 * units, total)]))
         return [pltpu.make_async_copy(a, b, wsem.at[i]) for i, (a, b) in enumerate(pairs)]
 
@@ -1514,7 +1517,7 @@
     m, width = x.shape
     far = groups // 2
     experts, hidden, _ = wg.shape
-    shared, total = ws.shape[1], wr.shape[0]
+    shared, total = ws.shape[1] // 3, wr.shape[0]
     units = experts * hidden + shared
     block, half = 4 * m, m // 2
     chunk = min(256, block)
@@ -1526,7 +1529,7 @@
         like(wg.shape, F32),
         like(wu.shape, F32),
         like(wd.shape, F32),
-        like(ws.shape, F32),
+        like((3, shared, width), F32),
         like((groups * tensors, m, width), BF16),
         like((groups * tensors, m, width), BF16),
         like((groups * block, width), BF16),
@@ -1567,7 +1570,7 @@
         (4, 8, far), (1, groups, 2), (1, groups), (1, far, 2), (1, far), (1, far), (1, far), (groups + 2,),
     ):
         scratch += [dma(shape), dma(shape)]
-    scratch += [dma((3 * experts + 4,)), dma((9,)), dma((10,))]
+    scratch += [dma((3 * experts + 3 * ws.shape[0] + 1,)), dma((9,)), dma((10,))]
     got = pl.pallas_call(
         functools.partial(experts_kernel, (far, experts, hidden, shared, total)),
         out_shape=outs,
@@ -1622,7 +1625,6 @@
     live_own = own(live)
     cot_own = own(cotangent).astype(f32)
     dffn_group = (cotangent * live.astype(bf16)).reshape(tensors, quarter, width)
-    dffn_own = own(cotangent) * live_own.astype(bf16)
 
     part = w_shared_down.shape[0] // groups
     spare = -part % TILE
@@ -1640,14 +1642,15 @@
         (w_query, w_kv, w_out),
         shared_w.reshape(groups, -1, shared_w.shape[-1]),
         picks.T.astype(BF16),
-        dffn_own,
+        dffn_group,
         groups,
         tensors,
         0,
     )
     query_w = query_w.reshape(width, -1)
     kv_up = kv_up.reshape(KVR, -1)
-    shared_w = shared_w.transpose(1, 0, 2).reshape(3, part + spare, width)
+    if (width // groups) % 128:
+        shared_w = shared_w.transpose(1, 0, 2).reshape(1, -1, width)
     gate_t, up_t = w_gate.transpose(0, 2, 1), w_up.transpose(0, 2, 1)
     router_t = jnp.roll(w_router.T, -eindex * experts_local, axis=0)
     parts = max(1, every // 4096)

time: 762 us -> 757 us (level)
    unnamed x52 -> x50, local copies, waits for them, and re-layouts: 20.6 us -> 20.6 us
where the time goes in v5:
time: 757 us; the launch traced here: 756 us
  Pallas kernels  701 us (93%)
  local copies, waits for them, and re-layouts  32.3 us (4%)
  other arithmetic  19.3 us (3%)
    pallas_call x1, Pallas kernels, experts_all(): pl.pallas_call(functools.partial(experts_kernel, (far, experts, hidden, s...  312 us
    pallas_call x1, Pallas kernels, finish(): pl.pallas_call(functools.partial(finish_kernel, far), out_shape=outs, in_...  189 us
    pallas_call x1, Pallas kernels, begin(): pl.pallas_call(functools.partial(begin_kernel, far), out_shape=outs, in_s...  101 us
    pallas_call x1, Pallas kernels, attend_back(): pl.pallas_call(functools.partial(attend_back_kernel, heads), out_shape=ou...  34.2 us
    pallas_call x1, Pallas kernels, gather_tensor(): pl.pallas_call(functools.partial(gather_tensor_kernel, groups // 2), out_...  24.8 us
    pallas_call x1, Pallas kernels, attend(): pl.pallas_call(functools.partial(attend_kernel, heads), out_shape=outs, i...  24.3 us
    unnamed x50, local copies, waits for them, and re-layouts  20.6 us
    pallas_call x1, Pallas kernels, sum_tensor(): pl.pallas_call(functools.partial(sum_tensor_kernel, groups // 2), out_sha...  16.4 us

profile of v5, /device:TPU:0, one launch (start us, length us, event | category | flops | bytes accessed | tf_op | source)
XLA Modules:
  0.0 756.4 jit_solution(16927706569070392711)
XLA Ops:
  1.3 0.7 fusion.2
  2.1 0.6 convert_bitcast_fusion.3.refs_4_
  2.7 1.3 pad_bitcast_fusion
  4.0 1.0 pad_bitcast_fusion.2
  5.0 1.1 pad_maximum_fusion
  6.2 1.5 broadcast_multiply_fusion
  7.7 100.8 %shard_map.297 = (bf16[8,256,768]{2,1,0:T(8,128)(2,1)}, bf16[8,64,1024]{2,1,0:T(8,128)(2,1)}, bf16[8,512,256]{2,1,0:T(8,128)(2,1)}, bf16[8,288,256]{2,1,0:T(8,12...) custom-call(bf16[256,768]{1,0:T(8,128)(2,1)} %refs_0_.1, bf16[64,1024]{1,0:T(8,128)(2,1)} %refs_1_.1, ...), custom_call_target="tpu_custom_call" | custom-call | bytes 300000000 | tf_op jit(solution)/shard_map/pallas_call | solution.py:447
  108.5 1.0 fusion.5
  109.5 1.0 pad_maximum_fusion.1
  110.5 24.3 %shard_map.298 = (bf16[512,2048]{1,0:T(8,128)(2,1)}, bf16[512,2048]{1,0:T(8,128)(2,1)}, bf16[4,512,192]{2,1,0:T(8,128)(2,1)}, bf16[512,1024]{1,0:T(8,128)(2,1)},...) custom-call(bf16[512,2048]{1,0:T(8,128)(2,1)} %tokens.3, ...), custom_call_target="tpu_custom_call" | custom-call | bytes 60000000 | tf_op jit(solution)/shard_map/pallas_call | solution.py:915
  134.8 1.5 fusion.11
  136.3 1.6 copy-done.1
  137.9 16.4 %shard_map.299 = f32[128,2048]{1,0:T(8,128)S(1)} custom-call(bf16[4,128,2048]{2,1,0:T(8,128)(2,1)S(1)} %bitcast.87), custom_call_target="tpu_custom_call" | custom-call | bytes 48000000 | tf_op jit(solution)/shard_map/pallas_call | solution.py:583
  154.3 0.0 copy-start.14
  154.3 0.1 dynamic-slice.3
  154.4 2.4 multiply_reduce_fusion.2
  156.8 1.0 copy-done.2
  157.8 0.9 multiply_convert_fusion.1.refs_0_
  158.9 0.1 convert_element_type.116
  158.9 0.8 convert_bitcast_fusion.2.refs_3_
  159.7 0.7 fusion.7.refs_8_
  160.4 311.9 %shard_map.300 = (bf16[1,128,2048]{2,1,0:T(8,128)(2,1)}, f32[8,8,128]{2,1,0:T(8,128)}, f32[2,352,2048]{2,1,0:T(8,128)}, f32[2,352,2048]{2,1,0:T(8,128)}, f32[2,3...) custom-call(bf16[128,2048]{1,0:T(8,128)(2,1)} %multiply_convert_fusi, ...), custom_call_target="tpu_custom_call" | custom-call | bytes 840000000 | tf_op jit(solution)/shard_map/pallas_call | solution.py:1574
  472.3 0.8 slice.39
  473.2 0.3 fusion.14
  473.5 0.2 convolution_convert_fusion
  473.7 1.9 multiply_reduce_fusion
  475.6 0.0 copy-done.3
  475.6 0.0 copy-start.6
  475.6 2.6 multiply_convert_fusion
  478.2 0.0 copy-done.6
  478.2 0.2 convert_element_type.121
  478.4 0.1 copy.47
  478.5 24.8 %shard_map.301 = (bf16[4,128,2048]{2,1,0:T(8,128)(2,1)S(1)}, bf16[8,288,256]{2,1,0:T(8,128)(2,1)S(1)}) custom-call(bf16[128,2048]{1,0:T(8,128)(2,1)S(1)} %get-tuple-element.98.own, bf16[8,288,256]{2,1,0:T(8,128)(2,1)S(1)} %bitcast.85), custom_call_target="tpu_custom_call" | custom-call | bytes 75000000 | tf_op jit(solution)/shard_map/pallas_call | solution.py:617
  503.4 0.0 copy-start
  503.4 1.3 copy-done
  504.7 34.2 %shard_map.302 = (bf16[2048,768]{1,0:T(8,128)(2,1)}, bf16[512,1024]{1,0:T(8,128)(2,1)}, bf16[8,512,256]{2,1,0:T(8,128)(2,1)}, bf16[576,2048]{1,0:T(8,128)(2,1)},...) custom-call(bf16[512,2048]{1,0:T(8,128)(2,1)} %bitcast.86, bf16[512,2048]{1,0:T(8,128)(2,1)} %tokens.3, ...), custom_call_target="tpu_custom_call" | custom-call | bytes 120000000 | tf_op jit(solution)/shard_map/pallas_call | solution.py:1023
  538.9 0.7 convert.24
  539.6 0.7 convert.26
  540.4 0.7 pad.23.refs_4_
  541.1 0.1 dynamic-slice_bitcast_fusion
  541.1 0.7 copy.44.refs_12_
  541.9 188.6 %shard_map.303 = (f32[256,768]{1,0:T(8,128)}, f32[64,1024]{1,0:T(8,128)}, f32[512,256]{1,0:T(8,128)}, bf16[640,2048]{1,0:T(8,128)(2,1)}, bf16[4,128,2048]{2,1,0:T(8,128)(2,1)}, /*index=5*/bf16[4,128,2048]{2,1,0:T(8,128)(2,1)}) custom-call(bf16[8,256,768]{2,1,0:T(8,128)(2,1)} %bitcast.108, bf16[8,64,1024]{2,1,0:T(8,128)(2,1)} %bitcast.116, ...), custom_call_target="tpu_custom_call" | custom-call | bytes 330000000 | tf_op jit(solution)/shard_map/pallas_call | solution.py:809
  730.5 1.8 slice.53
  732.3 2.9 convert_bitcast_fusion
  735.3 1.0 slice_convert_fusion
  736.3 0.7 slice_bitcast_fusion
  736.9 0.6 fusion.13
  737.5 0.6 slice.54
  738.1 0.1 convert_bitcast_fusion.1
  738.3 0.0 slice-start.4
  738.3 0.0 slice-start.2
  738.3 1.4 fusion.12
  739.7 0.8 copy-done.8
  740.5 1.3 copy.57
  741.8 1.3 copy.58
  743.1 1.4 copy-done.9
  744.5 0.9 copy.59
  745.4 0.7 copy.60
  746.1 0.1 copy-done.11
  746.2 0.8 copy.61
  747.0 2.9 copy.62
  749.9 2.9 copy.63
  752.8 1.1 slice-done.1
  753.9 2.5 copy.64
  (43 shorter events, 0.3 us)
Async XLA Ops:
  2.7 3.5 copy-start.5
  136.3 1.6 copy-start.1
  154.3 3.5 copy-start.14
  154.4 4.4 copy-start.13
  156.8 1.0 copy-start.2
  156.8 2.9 copy-start.10
  160.4 312.7 %copy-start.4 = (bf16[128,2048]{1,0:T(8,128)(2,1)S(1)}, bf16[128,2048]{1,0:T(8,128)(2,1)}, u32[]{:S(2)}) copy-start(bf16[128,2048]{1,0:T(8,128)(2,1)} %multiply_convert_fusion.1.refs_0_) | copy-start | bytes 1572868
  472.3 3.3 copy-start.3
  475.6 2.6 copy-start.6
  503.4 1.3 copy-start
  738.1 2.4 copy-start.8
  738.1 3.7 copy-start.7
  738.3 8.7 %slice-start.4 = ((s8[5767168]{0:T(1024)(128)(4,1)}), s8[4194304]{0:T(1024)(128)(4,1)S(1)}, s32[]{:S(2)}) async-start(s8[5767168]{0:T(1024)(128)(4,1)} %bitcast.101), calls=%async_computation.4 | async-start | bytes 8388608
  738.3 11.6 %slice-start.2 = ((s8[5767168]{0:T(1024)(128)(4,1)}), s8[4194304]{0:T(1024)(128)(4,1)S(1)}, s32[]{:S(2)}) async-start(s8[5767168]{0:T(1024)(128)(4,1)} %bitcast.98), calls=%async_computation.2 | async-start | bytes 8388608
  740.5 6.5 slice-start.5
  741.8 2.7 copy-start.9
  741.8 3.6 copy-start.12
  744.5 1.7 copy-start.11
  744.5 5.4 slice-start.3
  747.0 5.8 slice-start
  749.9 4.0 slice-start.1
